TPU v7x, 128 devices: a whole 4x4x4 slice. The times are simulated.
128 devices in a mesh: section: 8 (over x, y_lo), expert: 16 (over y_hi, z, core).
Axes of the slice: x: 4, y: 4 (y_hi: 2, y_lo: 2; y = y_hi * 2 + y_lo), z: 4, core: 2. Of those that a mesh axis runs over, the one named last changes fastest.
Arguments:
- up_acts: bfloat16 [8, 1024, 3584], P('section', 'expert'), may hold values from -6 to 6
- down_acts: bfloat16 [8, 1024, 3584], P('section', 'expert'), may hold values from -6 to 6
- norm_gain: float32 [8, 3584], P('section'), may hold values from 0.1 to 1.9
- up_routes: int32 [8, 1024, 2], P('section', 'expert'), may hold values from 0 to 3, all different within a row; in each aligned block of 64 rows (0 to 63, 64 to 127, ..., all dimensions but the last counted through in order) at most 64 rows name the same one
- down_routes: int32 [8, 1024, 2], P('section', 'expert'), may hold values from 0 to 3, all different within a row; in each aligned block of 64 rows (0 to 63, 64 to 127, ..., all dimensions but the last counted through in order) at most 64 rows name the same one
- up_gates: float32 [8, 1024, 2], P('section', 'expert'), may hold values from 0.2 to 1
- down_gates: float32 [8, 1024, 2], P('section', 'expert'), may hold values from 0.2 to 1
- gate_weight: bfloat16 [8, 3584, 8192], P('section', None, 'expert'), may hold values from -0.09375 to 0.09375
- up_weight: bfloat16 [8, 3584, 8192], P('section', None, 'expert'), may hold values from -0.09375 to 0.09375
- down_weight: bfloat16 [8, 8192, 3584], P('section', 'expert'), may hold values from -0.125 to 0.125
Outputs:
- next_up: bfloat16 [8, 1024, 3584], P('section', 'expert')
- next_down: bfloat16 [8, 1024, 3584], P('section', 'expert')
Inputs may be any that keep to these rules, and one draw needn't show every extreme that they name: `up_routes`: each row names 2 different experts. `down_routes`: each row names 2 different experts.
All inputs are finite; a program needn't handle non-finite values.
Results may differ from a plain program's by a relative error of at most 0.0052.
Values may be sent and summed in bfloat16 or wider, within the bound.
No kernel may reach another device: no remote copies, remote signals or barrier semaphores. Data moves between devices by JAX's collectives and lax.ppermute only.
A program may use at most 128 MiB of HBM per device.

v0:
```python
import jax
import jax.numpy as jnp
from jax import lax
from jax.sharding import PartitionSpec as P

SPLIT = 4


def shifted(block, axis, distance):
    devices = range(lax.axis_size(axis))
    route = [((i - distance) % len(devices), i) for i in devices]
    return lax.ppermute(block, axis, route)


def expert_rows(rows, gate_block, up_block, down_block):
    gate_value = jnp.dot(rows, gate_block, preferred_element_type=jnp.float32)
    up_value = jnp.dot(rows, up_block, preferred_element_type=jnp.float32)
    hidden = (jax.nn.silu(gate_value) * up_value).astype(jnp.bfloat16)
    return jnp.dot(hidden, down_block, preferred_element_type=jnp.float32).astype(jnp.bfloat16)


def prepare(activations, scaling, routes, gate_weights, experts):
    row_count = activations.shape[0]
    widened = activations.astype(jnp.float32)
    mean_square = jnp.mean(widened * widened, axis=-1, keepdims=True)
    normed = (widened * lax.rsqrt(mean_square + 1e-06) * scaling[None, :]).astype(jnp.bfloat16)
    labels = jnp.arange(experts, dtype=jnp.int32)
    chosen = (routes[:, :, None] == labels[None, None, :]).astype(jnp.float32)
    mixing = jnp.sum(gate_weights[:, :, None] * chosen, axis=1)
    member = jnp.sum(chosen, axis=1)
    position = jnp.cumsum(member, axis=0) - 1.0
    slot_index = jnp.arange(row_count, dtype=jnp.float32)
    placing = member.T[:, None, :] * (position.T[:, None, :] == slot_index[None, :, None]).astype(
        jnp.float32
    )
    placing = placing.astype(jnp.bfloat16)
    buffer = jnp.einsum("ect,td->ecd", placing, normed, preferred_element_type=jnp.float32).astype(
        jnp.bfloat16
    )
    return (widened, mixing, placing, buffer)


def finish(widened, mixing, placing, outputs):
    gathered = jnp.einsum("ect,ecd->ted", placing, outputs, preferred_element_type=jnp.float32)
    return (widened + jnp.sum(mixing[:, :, None] * gathered, axis=1)).astype(jnp.bfloat16)


def body(
    up_acts,
    down_acts,
    norm_gain,
    up_routes,
    down_routes,
    up_gates,
    down_gates,
    gate_weight,
    up_weight,
    down_weight,
):
    row_count = up_acts.shape[1]
    model_width = up_acts.shape[2]
    groups = lax.axis_size("expert")
    experts = groups // SPLIT
    gate_block = gate_weight[0]
    up_block = up_weight[0]
    down_block = down_weight[0]
    scaling = norm_gain[0]
    up_wide, up_mixing, up_placing, up_buffer = prepare(
        up_acts[0], scaling, up_routes[0], up_gates[0], experts
    )
    down_wide, down_mixing, down_placing, down_buffer = prepare(
        down_acts[0], scaling, down_routes[0], down_gates[0], experts
    )
    outgoing = jnp.stack([up_buffer, down_buffer], axis=1)
    copies = jnp.broadcast_to(outgoing[:, None], (experts, SPLIT, 2, row_count, model_width))
    copies = copies.reshape(groups, 2 * row_count, model_width)
    arrived = lax.all_to_all(copies, "expert", split_axis=0, concat_axis=0, tiled=True)
    item_count = arrived.shape[1]
    partial_value = expert_rows(arrived.reshape(-1, model_width), gate_block, up_block, down_block)
    partial_value = partial_value.reshape(groups, item_count, model_width)
    returned = lax.all_to_all(partial_value, "expert", split_axis=0, concat_axis=0, tiled=True)
    returned = returned.reshape(experts, SPLIT, 2, row_count, model_width).astype(jnp.float32)
    outputs = jnp.sum(returned, axis=1).astype(jnp.bfloat16)
    up_layer = finish(up_wide, up_mixing, up_placing, outputs[:, 0])
    down_layer = finish(down_wide, down_mixing, down_placing, outputs[:, 1])
    next_up = shifted(up_layer, "section", 1)
    next_down = shifted(down_layer, "section", -1)
    return (next_up[None], next_down[None])


def solution(mesh):
    return jax.shard_map(
        body,
        mesh=mesh,
        in_specs=(
            P("section", "expert", None),
            P("section", "expert", None),
            P("section", None),
            P("section", "expert", None),
            P("section", "expert", None),
            P("section", "expert", None),
            P("section", "expert", None),
            P("section", None, "expert"),
            P("section", None, "expert"),
            P("section", "expert", None),
        ),
        out_specs=(P("section", "expert", None), P("section", "expert", None)),
        check_vma=False,
    )
```

profile of v0, /device:TPU:1, one launch (start us, length us, event | category | flops | bytes accessed | tf_op | source)
XLA Modules:
  0.0 430.3 jit_solution(9249576636267951420)
XLA Ops:
  0.6 1.3 fusion.15
  1.9 1.2 fusion.19
  3.2 0.7 select_reduce_fusion
  3.9 0.1 copy.39
  4.0 0.1 reduce_window_sum.18
  4.1 0.1 copy.40
  4.1 0.7 select_reduce_fusion.1
  4.9 0.1 copy.36
  5.0 0.1 reduce_window_sum.17
  5.1 0.8 reduce.1
  5.9 1.8 fusion.2
  7.7 0.8 fusion.3
  8.5 0.3 pad_maximum_fusion
  8.9 0.2 copy.42
  9.1 1.7 broadcast_in_dim.6
  10.9 172.5 %all_to_all.10 = bf16[16,128,3584]{2,1,0:T(8,128)(2,1)S(1)} all-to-all(bf16[16,128,3584]{2,1,0:T(8,128)(2,1)S(1)} %bitcast.84), channel_id=1, replica_groups=mesh['section'=8,'expert'=16] {'expert'}, dimensions={0} | all-to-all | bytes 29360128 | tf_op jit(solution)/shard_map/all_to_all | solution.py:77
  183.4 5.2 %copy-done = bf16[16,128,3584]{2,1,0:T(8,128)(2,1)} copy-done((bf16[16,128,3584]{2,1,0:T(8,128)(2,1)}, bf16[16,128,3584]{2,1,0:T(8,128)(2,1)S(1)}, u32[]{:S(2)}) %copy-start) | copy-done | bytes 14680088
  188.5 9.2 %fusion.5 = f32[2048,512]{1,0:T(8,128)} fusion(bf16[2048,3584]{1,0:T(8,128)(2,1)S(1)} %bitcast.85, bf16[1,3584,512]{2,1,0:T(8,128)(2,1)S(1)} %copy-done.4), kind=kOutput, calls=%fused_computation.12 | convolution fusion | flops 7516192768 | bytes 22544384 | tf_op jit(solution)/shard_map/dot_general | solution.py:17
  197.7 24.6 %convolution_convert_fusion = bf16[2048,3584]{1,0:T(8,128)(2,1)} fusion(bf16[1,512,3584]{2,1,0:T(8,128)(2,1)} %param.19, f32[2048,512]{1,0:T(8,128)} %fusion.5, bf16[2048,3584]{1,0:T(8,128)(2,1)} %bitcast.86, bf16[1,3584,512]{2,1,0:T(8,128)(2,1)} %param.17), kind=kOutput, calls=%fused_computation | convolution fusion | flops 15046017024 | bytes 40894464 | tf_op jit(solution)/shard_map/dot_general | solution.py:19
  222.4 169.9 %all_to_all.11 = bf16[16,128,3584]{2,1,0:T(8,128)(2,1)} all-to-all(bf16[16,128,3584]{2,1,0:T(8,128)(2,1)} %bitcast.87), channel_id=1, replica_groups=mesh['section'=8,'expert'=16] {'expert'}, dimensions={0} | all-to-all | bytes 29360128 | tf_op jit(solution)/shard_map/all_to_all | solution.py:81
  392.2 10.8 %reduce_sum.89 = bf16[4,2,64,3584]{3,2,1,0:T(8,128)(2,1)} reduce(bf16[4,4,2,64,3584]{4,3,2,1,0:T(8,128)(2,1)} %bitcast.83, bf16[]{:T(256)} %constant.24.clone.1), dimensions={1}, to_apply=%region_7.8 | reduce | flops 5505024 | bytes 18350082 | tf_op jit(solution)/shard_map/reduce_sum | solution.py:83
  403.0 2.4 fusion.11
  405.4 0.2 copy-done.3
  405.6 0.7 fusion.12
  406.3 0.1 fusion.18
  406.4 0.5 collective-permute-start
  406.9 0.1 fusion.22
  406.9 3.2 collective-permute-start.1
  410.2 15.2 %collective-permute-done = bf16[64,3584]{1,0:T(8,128)(2,1)S(1)} collective-permute-done((bf16[64,3584]{1,0:T(8,128)(2,1)S(1)}, bf16[64,3584]{1,0:T(8,128)(2,1)S(1)}, u32[]{:S(2)}, u32[]{:S(2)}) %collective-permute-start) | collective-permute-done | bytes 458784 | tf_op jit(solution)/shard_map/ppermute | solution.py:12
  425.3 3.4 collective-permute-done.1
  428.7 0.8 copy.51
  429.5 0.8 copy.52
  (13 shorter events, 0.1 us)
Async XLA Ops:
  0.6 7.1 %copy-start.2 = (bf16[1,64,3584]{2,1,0:T(8,128)(2,1)S(1)}, bf16[1,64,3584]{2,1,0:T(8,128)(2,1)}, u32[]{:S(2)}) copy-start(bf16[1,64,3584]{2,1,0:T(8,128)(2,1)} %param.11) | copy-start | bytes 1376260
  10.9 177.7 %copy-start.4 = (bf16[1,3584,512]{2,1,0:T(8,128)(2,1)S(1)}, bf16[1,3584,512]{2,1,0:T(8,128)(2,1)}, u32[]{:S(2)}) copy-start(bf16[1,3584,512]{2,1,0:T(8,128)(2,1)} %param.18) | copy-start | bytes 11010052
  183.3 5.2 %copy-start = (bf16[16,128,3584]{2,1,0:T(8,128)(2,1)}, bf16[16,128,3584]{2,1,0:T(8,128)(2,1)S(1)}, u32[]{:S(2)}) copy-start(bf16[16,128,3584]{2,1,0:T(8,128)(2,1)S(1)} %all_to_all.10) | copy-start | bytes 44040196
  403.0 2.6 copy-start.3
  403.0 3.3 copy-start.1
  406.4 19.0 %collective-permute-start = (bf16[64,3584]{1,0:T(8,128)(2,1)S(1)}, bf16[64,3584]{1,0:T(8,128)(2,1)S(1)}, u32[]{:S(2)}, u32[]{:S(2)}) collective-permute-start(bf16[64,3584]{1,0:T(8,128)(2,1)S(1)} %fusion.18), channel_id=1, source_target_pairs={{112,0},{0,16},{16,32},{32,48},{48,64},{64,80},{80,96},{96,112},{1... | collective-permute-start | bytes 1376264 | tf_op jit(solution)/shard_map/ppermute | solution.py:12
  406.9 21.8 %collective-permute-start.1 = (bf16[64,3584]{1,0:T(8,128)(2,1)S(1)}, bf16[64,3584]{1,0:T(8,128)(2,1)S(1)}, u32[]{:S(2)}, u32[]{:S(2)}) collective-permute-start(bf16[64,3584]{1,0:T(8,128)(2,1)S(1)} %fusion.22), channel_id=1, source_target_pairs={{16,0},{32,16},{48,32},{64,48},{80,64},{96,80},{112,96},{0,112},{1... | collective-permute-start | bytes 1376264 | tf_op jit(solution)/shard_map/ppermute | solution.py:12
where the time goes:
time: 431 us; the launch traced here: 430 us
  blocking collectives  342 us (79%)
  matrix products  39.5 us (9%)
  waiting for transfers between devices  18.6 us (4%)
  other arithmetic  16.1 us (4%)
  local copies, waits for them, and re-layouts  9.24 us (2%)
    all_to_all x1, blocking collectives, body(): lax.all_to_all(copies, 'expert', split_axis=0, concat_axis=0, tiled=True)  172 us
    all_to_all x1, blocking collectives, body(): lax.all_to_all(partial_value, 'expert', split_axis=0, concat_axis=0, tile...  170 us
    dot_general x1, matrix products, expert_rows(): jnp.dot(hidden, down_block, preferred_element_type=jnp.float32)  24.6 us
    ppermute x2, waiting for transfers between devices, shifted(): return lax.ppermute(block, axis, route)  18.6 us
    reduce_sum x1, other arithmetic, body(): outputs = jnp.sum(returned, axis=1).astype(jnp.bfloat16)  10.8 us
    dot_general x1, matrix products, expert_rows(): up_value = jnp.dot(rows, up_block, preferred_element_type=jnp.float32)  9.2 us
  transfers between devices with their start and end apart: 2, of which 2 were waited for; matrix products, arithmetic and copies ran while one was open for 0% of the time, Pallas kernels for 0%

commit v1 on v0

v1 whole, which is shorter than its diff:
```python
import functools

import jax
import jax.numpy as jnp
from jax import lax
from jax.experimental import pallas as pl
from jax.experimental.pallas import tpu as pltpu
from jax.sharding import PartitionSpec as P

EXTRA = 128
TILE = 256


def place(y, z, c):
    return (y * 4 + z) * 2 + c


DEVICES = [(y, z, c) for y in range(2) for z in range(4) for c in range(2)]
CORE = [(place(y, z, c), place(y, z, 1 - c)) for y, z, c in DEVICES]
ACROSS = [(place(y, z, c), place(1 - y, z, c)) for y, z, c in DEVICES]
OUTWARD = [(place(y, z, c), place(y, (z + 1 - 2 * c) % 4, c)) for y, z, c in DEVICES]
HOMEWARD = [(place(y, z, c), place(y, (z - 1 + 2 * c) % 4, c)) for y, z, c in DEVICES]


def core(block):
    return lax.ppermute(block, "expert", CORE)


def across(block):
    return lax.ppermute(block, "expert", ACROSS)


def outward(block):
    return lax.ppermute(block, "expert", OUTWARD)


def homeward(block):
    return lax.ppermute(block, "expert", HOMEWARD)


def shifted(block, distance):
    devices = range(lax.axis_size("section"))
    route = [((i - distance) % len(devices), i) for i in devices]
    return lax.ppermute(block, "section", route)


def ffn_kernel(parts, width, *refs):
    x_refs = refs[:parts]
    mine = refs[parts : parts + 3]
    other = refs[parts + 3 : parts + 6]
    out_refs = refs[parts + 6 : 2 * parts + 6]
    x_all, mix_all, total = refs[2 * parts + 6 :]
    step = pl.program_id(0)
    half = pl.num_programs(0) // 2

    @pl.when(step == 0)
    def _():
        expert = lax.axis_index("expert") // 4
        row = 0
        for x_ref in x_refs:
            rows = x_ref.shape[0]
            x_all[row : row + rows, :] = x_ref[:, :width]
            tail = x_ref[:, width:].astype(jnp.float32)
            column = lax.broadcasted_iota(jnp.int32, tail.shape, 1)
            kept = jnp.where((column == expert) | (column == expert + 4), tail, 0.0)
            mix_all[row : row + rows, :] = jnp.sum(kept, axis=1, keepdims=True)
            row += rows

    def work(weights):
        gate_ref, up_ref, down_ref = weights
        x = x_all[...]
        gate_value = jnp.dot(x, gate_ref[...], preferred_element_type=jnp.float32)
        up_value = jnp.dot(x, up_ref[...], preferred_element_type=jnp.float32)
        hidden = gate_value * (1.0 / (1.0 + jnp.exp(-gate_value))) * up_value * mix_all[...]
        return jnp.dot(hidden.astype(jnp.bfloat16), down_ref[...], preferred_element_type=jnp.float32)

    @pl.when(step == 0)
    def _():
        total[...] = work(mine)

    @pl.when((step > 0) & (step < half))
    def _():
        total[...] += work(mine)

    @pl.when(step >= half)
    def _():
        total[...] += work(other)

    @pl.when(step == pl.num_programs(0) - 1)
    def _():
        row = 0
        for out_ref in out_refs:
            rows = out_ref.shape[0]
            out_ref[...] = total[row : row + rows, :].astype(out_ref.dtype)
            row += rows


def ffn(blocks, mine, other):
    width = mine[2].shape[1]
    units = mine[2].shape[0]
    rows = [block.shape[0] for block in blocks]
    total_rows = sum(rows)
    half = units // TILE

    def whole(count, columns):
        return pl.BlockSpec((count, columns), lambda j: (0, 0))

    def first(j):
        return jnp.minimum(j, half - 1)

    def second(j):
        return jnp.maximum(j - half, 0)

    def weight_specs(turn):
        return [
            pl.BlockSpec((width, TILE), lambda j: (0, turn(j))),
            pl.BlockSpec((width, TILE), lambda j: (0, turn(j))),
            pl.BlockSpec((TILE, width), lambda j: (turn(j), 0)),
        ]

    return pl.pallas_call(
        functools.partial(ffn_kernel, len(blocks), width),
        grid=(2 * half,),
        in_specs=[whole(r, width + EXTRA) for r in rows] + weight_specs(first) + weight_specs(second),
        out_specs=[whole(r, width) for r in rows],
        out_shape=[jax.ShapeDtypeStruct((r, width), jnp.bfloat16) for r in rows],
        scratch_shapes=[
            pltpu.VMEM((total_rows, width), jnp.bfloat16),
            pltpu.VMEM((total_rows, 1), jnp.float32),
            pltpu.VMEM((total_rows, width), jnp.float32),
        ],
        cost_estimate=pl.CostEstimate(
            flops=2 * total_rows * width * 2 * units * 3,
            bytes_accessed=2 * 3 * 2 * units * width + 4 * total_rows * width,
            transcendentals=total_rows * 2 * units,
        ),
        compiler_params=pltpu.CompilerParams(vmem_limit_bytes=58 * 1024 * 1024),
    )(*blocks, *mine, *other)


def prepare(activations, scaling, routes, gate_weights):
    widened = activations.astype(jnp.float32)
    mean_square = jnp.mean(widened * widened, axis=-1, keepdims=True)
    normed = (widened * lax.rsqrt(mean_square + 1e-06) * scaling[None, :]).astype(jnp.bfloat16)
    column = jnp.arange(EXTRA, dtype=jnp.int32)
    label = jnp.where(column < 8, column % 4, -1)
    mixing = jnp.zeros((activations.shape[0], EXTRA), jnp.float32)
    for k in range(routes.shape[1]):
        mixing += jnp.where(routes[:, k : k + 1] == label[None, :], gate_weights[:, k : k + 1], 0.0)
    coarse = lax.reduce_precision(mixing, 8, 7)
    tail = jnp.where(column[None, :] < 4, coarse, mixing - coarse).astype(jnp.bfloat16)
    return jnp.concatenate([normed, tail], axis=1)


def gather(own):
    rows = own.shape[0]
    beside = core(own)
    near = outward(jnp.concatenate([own, beside]))
    facing = across(own)
    facing_beside = core(facing)
    second = outward(jnp.concatenate([near[:rows], facing, facing_beside]))
    far, facing_near = second[:rows], second[rows:]
    facing_far = across(far)
    return (own, near, facing, far, facing_near, facing_far)


def add(*terms):
    total = terms[0].astype(jnp.float32)
    for term in terms[1:]:
        total = total + term.astype(jnp.float32)
    return total


def combine(activations, partials):
    own, near, facing, far, facing_near, facing_far = partials
    rows = own.shape[0]
    far = add(far, across(facing_far)).astype(jnp.bfloat16)
    back = homeward(jnp.concatenate([far, facing_near]))
    near = jnp.concatenate([add(near[:rows], back[:rows]).astype(jnp.bfloat16), near[rows:]])
    facing = add(facing, back[rows : 2 * rows], core(back[2 * rows :])).astype(jnp.bfloat16)
    last = homeward(near)
    crossed = across(facing)
    return add(activations, own, last[:rows], core(last[rows:]), crossed).astype(jnp.bfloat16)


def body(
    up_acts,
    down_acts,
    norm_gain,
    up_routes,
    down_routes,
    up_gates,
    down_gates,
    gate_weight,
    up_weight,
    down_weight,
):
    mine = (gate_weight[0], up_weight[0], down_weight[0])
    other = tuple(core(w) for w in mine)
    up_own = prepare(up_acts[0], norm_gain[0], up_routes[0], up_gates[0])
    down_own = prepare(down_acts[0], norm_gain[0], down_routes[0], down_gates[0])
    up_blocks = gather(up_own)
    down_blocks = gather(down_own)
    up_partials = ffn(up_blocks, mine, other)
    up_layer = combine(up_acts[0], up_partials)
    next_up = shifted(up_layer, 1)
    down_partials = ffn(down_blocks, mine, other)
    down_layer = combine(down_acts[0], down_partials)
    next_down = shifted(down_layer, -1)
    return (next_up[None], next_down[None])


def solution(mesh):
    return jax.shard_map(
        body,
        mesh=mesh,
        in_specs=(
            P("section", "expert", None),
            P("section", "expert", None),
            P("section", None),
            P("section", "expert", None),
            P("section", "expert", None),
            P("section", "expert", None),
            P("section", "expert", None),
            P("section", None, "expert"),
            P("section", None, "expert"),
            P("section", "expert", None),
        ),
        out_specs=(P("section", "expert", None), P("section", "expert", None)),
        check_vma=False,
    )
```

time: 431 us -> 222 us (0.52)
  blocking collectives: 342 us -> 0 us
  waiting for transfers between devices: 18.6 us -> 123 us
  Pallas kernels: 0 us -> 41 us
  matrix products: 39.5 us -> 0 us
  starting transfers between devices: 3.71 us -> 39.2 us
  other arithmetic: 16.1 us -> 6.83 us
    all_to_all x2 -> x0, blocking collectives: 342 us -> none  [the longest x1 172 us: body(): lax.all_to_all(copies, 'expert', split_axis=0, concat_axis=0, tiled=True)]
    ppermute x2 -> x29, waiting for transfers between devices: 18.6 us -> 123 us  [the longest x4 43.2 us: homeward(): return lax.ppermute(block, 'expert', HOMEWARD)]
    pallas_call x0 -> x2, Pallas kernels: none -> 41 us  [ffn(): pl.pallas_call(functools.partial(ffn_kernel, len(blocks), width), grid=(2...]
    dot_general x6 -> x0, matrix products: 39.5 us -> none  [the longest x1 24.6 us: expert_rows(): jnp.dot(hidden, down_block, preferred_element_type=jnp.float32)]
    ppermute x2 -> x29, starting transfers between devices: 3.71 us -> 39.2 us  [the longest x8 14.8 us: across(): return lax.ppermute(block, 'expert', ACROSS)]
    reduce_sum x3 -> x0, other arithmetic: 12.2 us -> none  [the longest x1 10.8 us: body(): outputs = jnp.sum(returned, axis=1).astype(jnp.bfloat16)]
  transfers between devices with their start and end apart: 2 -> 29, of which waited for: 2 -> 13; matrix products, arithmetic and copies ran while one was open for 0% -> 2% of each run, Pallas kernels for 0% -> 19%
where the time goes in v1:
time: 222 us; the launch traced here: 221 us
  waiting for transfers between devices  123 us (55%)
  Pallas kernels  41 us (18%)
  starting transfers between devices  39.2 us (18%)
  local copies, waits for them, and re-layouts  10.1 us (5%)
  other arithmetic  6.83 us (3%)
    ppermute x4, waiting for transfers between devices, homeward(): return lax.ppermute(block, 'expert', HOMEWARD)  43.2 us
    pallas_call x2, Pallas kernels, ffn(): pl.pallas_call(functools.partial(ffn_kernel, len(blocks), width), grid=(2...  41 us
    ppermute x4, waiting for transfers between devices, outward(): return lax.ppermute(block, 'expert', OUTWARD)  38.2 us
    ppermute x8, waiting for transfers between devices, across(): return lax.ppermute(block, 'expert', ACROSS)  22.5 us
    ppermute x2, waiting for transfers between devices, shifted(): return lax.ppermute(block, 'section', route)  17.8 us
    ppermute x8, starting transfers between devices, across(): return lax.ppermute(block, 'expert', ACROSS)  14.8 us
    ppermute x4, starting transfers between devices, outward(): return lax.ppermute(block, 'expert', OUTWARD)  10.9 us
    ppermute x11, starting transfers between devices, core(): return lax.ppermute(block, 'expert', CORE)  10.2 us
  transfers between devices with their start and end apart: 29, of which 13 were waited for; matrix products, arithmetic and copies ran while one was open for 2% of the time, Pallas kernels for 19%

profile of v1, /device:TPU:1, one launch (start us, length us, event | category | flops | bytes accessed | tf_op | source)
XLA Modules:
  0.0 220.9 jit_solution(13446030634784772061)
XLA Ops:
  0.7 1.2 fusion
  1.9 1.2 fusion.7
  5.4 1.4 fusion.9
  7.0 1.5 collective-permute-start.16
  8.5 3.0 %collective-permute-start.18 = (bf16[64,3712]{1,0:T(8,128)(2,1)S(1)}, bf16[64,3712]{1,0:T(8,128)(2,1)S(1)}, u32[]{:S(2)}, u32[]{:S(2)}) collective-permute-start(bf16[64,3712]{1,0:T(8,128)(2,1)S(1)} %pad_maximum_fusion.9.refs_0_), channel_id=1, source_target_pairs={{0,8},{1,9},{2,10},{3,11},{4,12},{5,13},{6,14},{7,15},{8,0},{9,1},... | collective-permute-start | bytes 1425416 | tf_op jit(solution)/shard_map/ppermute | solution.py:30
  12.1 3.8 %collective-permute-start.17 = (bf16[128,3712]{1,0:T(8,128)(2,1)S(1)}, bf16[128,3712]{1,0:T(8,128)(2,1)S(1)}, u32[]{:S(2)}, u32[]{:S(2)}) collective-permute-start(bf16[128,3712]{1,0:T(8,128)(2,1)S(1)} %pad_maximum_fusion.5), channel_id=1, source_target_pairs={{0,2},{1,7},{2,4},{3,1},{4,6},{5,3},{6,0},{7,5},{8,10},{9,15},{10,... | collective-permute-start | bytes 2850824 | tf_op jit(solution)/shard_map/ppermute | solution.py:34
  16.9 5.6 %collective-permute-done.18.refs_2_ = bf16[64,3712]{1,0:T(8,128)(2,1)S(1)} collective-permute-done((bf16[64,3712]{1,0:T(8,128)(2,1)S(1)}, bf16[64,3712]{1,0:T(8,128)(2,1)S(1)}, u32[]{:S(2)}, u32[]{:S(2)}) %collective-permute-start.18) | collective-permute-done | bytes 475168 | tf_op jit(solution)/shard_map/ppermute | solution.py:30
  22.5 1.3 collective-permute-start.7
  23.9 8.8 %collective-permute-done.2.refs_2_ = bf16[64,3712]{1,0:T(8,128)(2,1)S(1)} collective-permute-done((bf16[64,3712]{1,0:T(8,128)(2,1)S(1)}, bf16[64,3712]{1,0:T(8,128)(2,1)S(1)}, u32[]{:S(2)}, u32[]{:S(2)}) %collective-permute-start.2) | collective-permute-done | bytes 475168 | tf_op jit(solution)/shard_map/ppermute | solution.py:30
  33.6 3.9 %collective-permute-start.1 = (bf16[128,3712]{1,0:T(8,128)(2,1)S(1)}, bf16[128,3712]{1,0:T(8,128)(2,1)S(1)}, u32[]{:S(2)}, u32[]{:S(2)}) collective-permute-start(bf16[128,3712]{1,0:T(8,128)(2,1)S(1)} %pad_maximum_fusion.4), channel_id=1, source_target_pairs={{0,2},{1,7},{2,4},{3,1},{4,6},{5,3},{6,0},{7,5},{8,10},{9,15},{10,... | collective-permute-start | bytes 2850824 | tf_op jit(solution)/shard_map/ppermute | solution.py:34
  37.8 10.4 %collective-permute-done.1.refs_1_ = bf16[128,3712]{1,0:T(8,128)(2,1)S(1)} collective-permute-done((bf16[128,3712]{1,0:T(8,128)(2,1)S(1)}, bf16[128,3712]{1,0:T(8,128)(2,1)S(1)}, u32[]{:S(2)}, u32[]{:S(2)}) %collective-permute-start.1) | collective-permute-done | bytes 950304 | tf_op jit(solution)/shard_map/ppermute | solution.py:34
  48.2 3.1 %collective-permute-start.20 = (bf16[192,3712]{1,0:T(8,128)(2,1)S(1)}, bf16[192,3712]{1,0:T(8,128)(2,1)S(1)}, u32[]{:S(2)}, u32[]{:S(2)}) collective-permute-start(bf16[192,3712]{1,0:T(8,128)(2,1)S(1)} %pad_maximum_fusion.1), channel_id=1, source_target_pairs={{0,2},{1,7},{2,4},{3,1},{4,6},{5,3},{6,0},{7,5},{8,10},{9,15},{10,... | collective-permute-start | bytes 4276232 | tf_op jit(solution)/shard_map/ppermute | solution.py:34
  51.6 15.5 %collective-permute-done.20 = bf16[192,3712]{1,0:T(8,128)(2,1)S(1)} collective-permute-done((bf16[192,3712]{1,0:T(8,128)(2,1)S(1)}, bf16[192,3712]{1,0:T(8,128)(2,1)S(1)}, u32[]{:S(2)}, u32[]{:S(2)}) %collective-permute-start.20) | collective-permute-done | bytes 1425440 | tf_op jit(solution)/shard_map/ppermute | solution.py:34
  67.2 3.0 %collective-permute-start.21 = (bf16[64,3712]{1,0:T(8,128)(2,1)S(1)}, bf16[64,3712]{1,0:T(8,128)(2,1)S(1)}, u32[]{:S(2)}, u32[]{:S(2)}) collective-permute-start(bf16[64,3712]{1,0:T(8,128)(2,1)S(1)} %slice.121.refs_3_), channel_id=1, source_target_pairs={{0,8},{1,9},{2,10},{3,11},{4,12},{5,13},{6,14},{7,15},{8,0},{9,1},... | collective-permute-start | bytes 1425416 | tf_op jit(solution)/shard_map/ppermute | solution.py:30
  70.2 12.2 %collective-permute-done.4 = bf16[192,3712]{1,0:T(8,128)(2,1)S(1)} collective-permute-done((bf16[192,3712]{1,0:T(8,128)(2,1)S(1)}, bf16[192,3712]{1,0:T(8,128)(2,1)S(1)}, u32[]{:S(2)}, u32[]{:S(2)}) %collective-permute-start.4) | collective-permute-done | bytes 1425440 | tf_op jit(solution)/shard_map/ppermute | solution.py:34
  82.5 3.2 %collective-permute-start.5 = (bf16[64,3712]{1,0:T(8,128)(2,1)S(1)}, bf16[64,3712]{1,0:T(8,128)(2,1)S(1)}, u32[]{:S(2)}, u32[]{:S(2)}) collective-permute-start(bf16[64,3712]{1,0:T(8,128)(2,1)S(1)} %slice.113.refs_3_), channel_id=1, source_target_pairs={{0,8},{1,9},{2,10},{3,11},{4,12},{5,13},{6,14},{7,15},{8,0},{9,1},... | collective-permute-start | bytes 1425416 | tf_op jit(solution)/shard_map/ppermute | solution.py:30
  85.6 1.0 slice.122.refs_4_
  86.6 1.1 slice.114.refs_4_
  87.8 1.8 copy-done.21
  89.6 1.9 copy-done.22
  91.5 20.5 %shard_map.114 = (bf16[64,3584]{1,0:T(8,128)(2,1)}, bf16[128,3584]{1,0:T(8,128)(2,1)}, bf16[64,3584]{1,0:T(8,128)(2,1)}, bf16[64,3584]{1,0:T(8,128)(2,1)}, bf16[...) custom-call(bf16[64,3712]{1,0:T(8,128)(2,1)} %copy-done.7, bf16[128,3712]{1,0:T(8,128)(2,1)} %copy-done.18, ...), custom_call_target="tpu_custom_call" | custom-call | flops 11274289152 | bytes 29360128 | tf_op jit(solution)/shard_map/pallas_call | solution.py:121
  113.1 20.5 %shard_map.113 = (bf16[64,3584]{1,0:T(8,128)(2,1)}, bf16[128,3584]{1,0:T(8,128)(2,1)}, bf16[64,3584]{1,0:T(8,128)(2,1)}, bf16[64,3584]{1,0:T(8,128)(2,1)}, bf16[...) custom-call(bf16[64,3712]{1,0:T(8,128)(2,1)} %copy-done.6, bf16[128,3712]{1,0:T(8,128)(2,1)} %copy-done.19, ...), custom_call_target="tpu_custom_call" | custom-call | flops 11274289152 | bytes 29360128 | tf_op jit(solution)/shard_map/pallas_call | solution.py:121
  133.6 3.0 %collective-permute-start.9 = (bf16[64,3584]{1,0:T(8,128)(2,1)}, bf16[64,3584]{1,0:T(8,128)(2,1)S(1)}, u32[]{:S(2)}, u32[]{:S(2)}) collective-permute-start(bf16[64,3584]{1,0:T(8,128)(2,1)} %get-tuple-element.17), channel_id=1, source_target_pairs={{0,8},{1,9},{2,10},{3,11},{4,12},{5,13},{6,14},{7,15},{8,0},{9,1},... | collective-permute-start | bytes 1376264 | tf_op jit(solution)/shard_map/ppermute | solution.py:30
  136.9 7.5 %collective-permute-done.9 = bf16[64,3584]{1,0:T(8,128)(2,1)S(1)} collective-permute-done((bf16[64,3584]{1,0:T(8,128)(2,1)}, bf16[64,3584]{1,0:T(8,128)(2,1)S(1)}, u32[]{:S(2)}, u32[]{:S(2)}) %collective-permute-start.9) | collective-permute-done | bytes 458784 | tf_op jit(solution)/shard_map/ppermute | solution.py:30
  144.9 10.8 %collective-permute-done.23 = bf16[192,3584]{1,0:T(8,128)(2,1)S(1)} collective-permute-done((bf16[192,3584]{1,0:T(8,128)(2,1)S(1)}, bf16[192,3584]{1,0:T(8,128)(2,1)S(1)}, u32[]{:S(2)}, u32[]{:S(2)}) %collective-permute-start.23) | collective-permute-done | bytes 1376288 | tf_op jit(solution)/shard_map/ppermute | solution.py:38
  155.8 2.9 %collective-permute-start.26 = (bf16[64,3584]{1,0:T(8,128)(2,1)S(1)}, bf16[64,3584]{1,0:T(8,128)(2,1)S(1)}, u32[]{:S(2)}, u32[]{:S(2)}) collective-permute-start(bf16[64,3584]{1,0:T(8,128)(2,1)S(1)} %slice.127), channel_id=1, source_target_pairs={{0,1},{1,0},{2,3},{3,2},{4,5},{5,4},{6,7},{7,6},{8,9},{9,8},{10,11... | collective-permute-start | bytes 1376264 | tf_op jit(solution)/shard_map/ppermute | solution.py:26
  158.7 11.7 %collective-permute-done.10 = bf16[192,3584]{1,0:T(8,128)(2,1)S(1)} collective-permute-done((bf16[192,3584]{1,0:T(8,128)(2,1)S(1)}, bf16[192,3584]{1,0:T(8,128)(2,1)S(1)}, u32[]{:S(2)}, u32[]{:S(2)}) %collective-permute-start.10) | collective-permute-done | bytes 1376288 | tf_op jit(solution)/shard_map/ppermute | solution.py:38
  170.5 2.9 %collective-permute-start.13 = (bf16[64,3584]{1,0:T(8,128)(2,1)S(1)}, bf16[64,3584]{1,0:T(8,128)(2,1)S(1)}, u32[]{:S(2)}, u32[]{:S(2)}) collective-permute-start(bf16[64,3584]{1,0:T(8,128)(2,1)S(1)} %slice.119), channel_id=1, source_target_pairs={{0,1},{1,0},{2,3},{3,2},{4,5},{5,4},{6,7},{7,6},{8,9},{9,8},{10,11... | collective-permute-start | bytes 1376264 | tf_op jit(solution)/shard_map/ppermute | solution.py:26
  176.0 11.5 %collective-permute-done.24 = bf16[128,3584]{1,0:T(8,128)(2,1)S(1)} collective-permute-done((bf16[128,3584]{1,0:T(8,128)(2,1)S(1)}, bf16[128,3584]{1,0:T(8,128)(2,1)S(1)}, u32[]{:S(2)}, u32[]{:S(2)}) %collective-permute-start.24) | collective-permute-done | bytes 917536 | tf_op jit(solution)/shard_map/ppermute | solution.py:38
  188.3 9.1 %collective-permute-done.11 = bf16[128,3584]{1,0:T(8,128)(2,1)S(1)} collective-permute-done((bf16[128,3584]{1,0:T(8,128)(2,1)S(1)}, bf16[128,3584]{1,0:T(8,128)(2,1)S(1)}, u32[]{:S(2)}, u32[]{:S(2)}) %collective-permute-start.11) | collective-permute-done | bytes 917536 | tf_op jit(solution)/shard_map/ppermute | solution.py:38
  197.8 2.5 %collective-permute-start.28 = (bf16[64,3584]{1,0:T(8,128)(2,1)S(1)}, bf16[64,3584]{1,0:T(8,128)(2,1)S(1)}, u32[]{:S(2)}, u32[]{:S(2)}) collective-permute-start(bf16[64,3584]{1,0:T(8,128)(2,1)S(1)} %fusion.13), channel_id=1, source_target_pairs={{16,0},{32,16},{48,32},{64,48},{80,64},{96,80},{112,96},{0,112},{1... | collective-permute-start | bytes 1376264 | tf_op jit(solution)/shard_map/ppermute | solution.py:44
  201.6 17.8 %collective-permute-done.28 = bf16[64,3584]{1,0:T(8,128)(2,1)S(1)} collective-permute-done((bf16[64,3584]{1,0:T(8,128)(2,1)S(1)}, bf16[64,3584]{1,0:T(8,128)(2,1)S(1)}, u32[]{:S(2)}, u32[]{:S(2)}) %collective-permute-start.28) | collective-permute-done | bytes 458784 | tf_op jit(solution)/shard_map/ppermute | solution.py:44
  (118 shorter events, 14.0 us)
Async XLA Ops:
  7.0 26.6 %copy-start.7 = (bf16[64,3712]{1,0:T(8,128)(2,1)}, bf16[64,3712]{1,0:T(8,128)(2,1)S(1)}, u32[]{:S(2)}) copy-start(bf16[64,3712]{1,0:T(8,128)(2,1)S(1)} %pad_maximum_fusion.9.refs_0_) | copy-start | bytes 1425412
  7.0 5.0 %collective-permute-start.16 = (bf16[64,3712]{1,0:T(8,128)(2,1)S(1)}, bf16[64,3712]{1,0:T(8,128)(2,1)S(1)}, u32[]{:S(2)}, u32[]{:S(2)}) collective-permute-start(bf16[64,3712]{1,0:T(8,128)(2,1)S(1)} %pad_maximum_fusion.9.refs_0_), channel_id=1, source_target_pairs={{0,1},{1,0},{2,3},{3,2},{4,5},{5,4},{6,7},{7,6},{8,9},{9,8},{10,11... | collective-permute-start | bytes 1425416 | tf_op jit(solution)/shard_map/ppermute | solution.py:26
  8.5 14.0 %collective-permute-start.18 = (bf16[64,3712]{1,0:T(8,128)(2,1)S(1)}, bf16[64,3712]{1,0:T(8,128)(2,1)S(1)}, u32[]{:S(2)}, u32[]{:S(2)}) collective-permute-start(bf16[64,3712]{1,0:T(8,128)(2,1)S(1)} %pad_maximum_fusion.9.refs_0_), channel_id=1, source_target_pairs={{0,8},{1,9},{2,10},{3,11},{4,12},{5,13},{6,14},{7,15},{8,0},{9,1},... | collective-permute-start | bytes 1425416 | tf_op jit(solution)/shard_map/ppermute | solution.py:30
  11.6 12.2 %collective-permute-start = (bf16[64,3712]{1,0:T(8,128)(2,1)S(1)}, bf16[64,3712]{1,0:T(8,128)(2,1)S(1)}, u32[]{:S(2)}, u32[]{:S(2)}) collective-permute-start(bf16[64,3712]{1,0:T(8,128)(2,1)S(1)} %pad_maximum_fusion.8.refs_0_), channel_id=1, source_target_pairs={{0,1},{1,0},{2,3},{3,2},{4,5},{5,4},{6,7},{7,6},{8,9},{9,8},{10,11... | collective-permute-start | bytes 1425416 | tf_op jit(solution)/shard_map/ppermute | solution.py:26
  12.1 21.5 %collective-permute-start.17 = (bf16[128,3712]{1,0:T(8,128)(2,1)S(1)}, bf16[128,3712]{1,0:T(8,128)(2,1)S(1)}, u32[]{:S(2)}, u32[]{:S(2)}) collective-permute-start(bf16[128,3712]{1,0:T(8,128)(2,1)S(1)} %pad_maximum_fusion.5), channel_id=1, source_target_pairs={{0,2},{1,7},{2,4},{3,1},{4,6},{5,3},{6,0},{7,5},{8,10},{9,15},{10,... | collective-permute-start | bytes 2850824 | tf_op jit(solution)/shard_map/ppermute | solution.py:34
  15.9 16.8 %collective-permute-start.2 = (bf16[64,3712]{1,0:T(8,128)(2,1)S(1)}, bf16[64,3712]{1,0:T(8,128)(2,1)S(1)}, u32[]{:S(2)}, u32[]{:S(2)}) collective-permute-start(bf16[64,3712]{1,0:T(8,128)(2,1)S(1)} %pad_maximum_fusion.8.refs_0_), channel_id=1, source_target_pairs={{0,8},{1,9},{2,10},{3,11},{4,12},{5,13},{6,14},{7,15},{8,0},{9,1},... | collective-permute-start | bytes 1425416 | tf_op jit(solution)/shard_map/ppermute | solution.py:30
  16.9 70.9 %collective-permute-start.6 = (bf16[3584,512]{1,0:T(8,128)(2,1)S(1)}, bf16[3584,512]{1,0:T(8,128)(2,1)S(1)}, u32[]{:S(2)}, u32[]{:S(2)}) collective-permute-start(bf16[3584,512]{1,0:T(8,128)(2,1)S(1)} %bitcast.43), channel_id=1, source_target_pairs={{0,1},{1,0},{2,3},{3,2},{4,5},{5,4},{6,7},{7,6},{8,9},{9,8},{10,11... | collective-permute-start | bytes 11010056 | tf_op jit(solution)/shard_map/ppermute | solution.py:26
  22.5 67.1 %collective-permute-start.7 = (bf16[3584,512]{1,0:T(8,128)(2,1)}, bf16[3584,512]{1,0:T(8,128)(2,1)S(1)}, u32[]{:S(2)}, u32[]{:S(2)}) collective-permute-start(bf16[3584,512]{1,0:T(8,128)(2,1)} %bitcast.44), channel_id=1, source_target_pairs={{0,1},{1,0},{2,3},{3,2},{4,5},{5,4},{6,7},{7,6},{8,9},{9,8},{10,11... | collective-permute-start | bytes 11010056 | tf_op jit(solution)/shard_map/ppermute | solution.py:26
  23.8 67.7 %collective-permute-start.8 = (bf16[512,3584]{1,0:T(8,128)(2,1)}, bf16[512,3584]{1,0:T(8,128)(2,1)}, u32[]{:S(2)}, u32[]{:S(2)}) collective-permute-start(bf16[512,3584]{1,0:T(8,128)(2,1)} %bitcast.47), channel_id=1, source_target_pairs={{0,1},{1,0},{2,3},{3,2},{4,5},{5,4},{6,7},{7,6},{8,9},{9,8},{10,11... | collective-permute-start | bytes 11010056 | tf_op jit(solution)/shard_map/ppermute | solution.py:26
  32.7 4.9 %collective-permute-start.19 = (bf16[64,3712]{1,0:T(8,128)(2,1)S(1)}, bf16[64,3712]{1,0:T(8,128)(2,1)S(1)}, u32[]{:S(2)}, u32[]{:S(2)}) collective-permute-start(bf16[64,3712]{1,0:T(8,128)(2,1)S(1)} %collective-permute-done.18.refs_2_), channel_id=1, source_target_pairs={{0,1},{1,0},{2,3},{3,2},{4,5},{5,4},{6,7},{7,6},{8,9},{9,8},{10,11... | collective-permute-start | bytes 1425416 | tf_op jit(solution)/shard_map/ppermute | solution.py:26
  33.6 14.6 %collective-permute-start.1 = (bf16[128,3712]{1,0:T(8,128)(2,1)S(1)}, bf16[128,3712]{1,0:T(8,128)(2,1)S(1)}, u32[]{:S(2)}, u32[]{:S(2)}) collective-permute-start(bf16[128,3712]{1,0:T(8,128)(2,1)S(1)} %pad_maximum_fusion.4), channel_id=1, source_target_pairs={{0,2},{1,7},{2,4},{3,1},{4,6},{5,3},{6,0},{7,5},{8,10},{9,15},{10,... | collective-permute-start | bytes 2850824 | tf_op jit(solution)/shard_map/ppermute | solution.py:34
  37.6 13.8 %collective-permute-start.3 = (bf16[64,3712]{1,0:T(8,128)(2,1)S(1)}, bf16[64,3712]{1,0:T(8,128)(2,1)S(1)}, u32[]{:S(2)}, u32[]{:S(2)}) collective-permute-start(bf16[64,3712]{1,0:T(8,128)(2,1)S(1)} %collective-permute-done.2.refs_2_), channel_id=1, source_target_pairs={{0,1},{1,0},{2,3},{3,2},{4,5},{5,4},{6,7},{7,6},{8,9},{9,8},{10,11... | collective-permute-start | bytes 1425416 | tf_op jit(solution)/shard_map/ppermute | solution.py:26
  48.2 18.9 %collective-permute-start.20 = (bf16[192,3712]{1,0:T(8,128)(2,1)S(1)}, bf16[192,3712]{1,0:T(8,128)(2,1)S(1)}, u32[]{:S(2)}, u32[]{:S(2)}) collective-permute-start(bf16[192,3712]{1,0:T(8,128)(2,1)S(1)} %pad_maximum_fusion.1), channel_id=1, source_target_pairs={{0,2},{1,7},{2,4},{3,1},{4,6},{5,3},{6,0},{7,5},{8,10},{9,15},{10,... | collective-permute-start | bytes 4276232 | tf_op jit(solution)/shard_map/ppermute | solution.py:34
  51.5 30.9 %collective-permute-start.4 = (bf16[192,3712]{1,0:T(8,128)(2,1)S(1)}, bf16[192,3712]{1,0:T(8,128)(2,1)S(1)}, u32[]{:S(2)}, u32[]{:S(2)}) collective-permute-start(bf16[192,3712]{1,0:T(8,128)(2,1)S(1)} %pad_maximum_fusion), channel_id=1, source_target_pairs={{0,2},{1,7},{2,4},{3,1},{4,6},{5,3},{6,0},{7,5},{8,10},{9,15},{10,... | collective-permute-start | bytes 4276232 | tf_op jit(solution)/shard_map/ppermute | solution.py:34
  67.2 20.6 %collective-permute-start.21 = (bf16[64,3712]{1,0:T(8,128)(2,1)S(1)}, bf16[64,3712]{1,0:T(8,128)(2,1)S(1)}, u32[]{:S(2)}, u32[]{:S(2)}) collective-permute-start(bf16[64,3712]{1,0:T(8,128)(2,1)S(1)} %slice.121.refs_3_), channel_id=1, source_target_pairs={{0,8},{1,9},{2,10},{3,11},{4,12},{5,13},{6,14},{7,15},{8,0},{9,1},... | collective-permute-start | bytes 1425416 | tf_op jit(solution)/shard_map/ppermute | solution.py:30
  82.5 29.9 %collective-permute-start.5 = (bf16[64,3712]{1,0:T(8,128)(2,1)S(1)}, bf16[64,3712]{1,0:T(8,128)(2,1)S(1)}, u32[]{:S(2)}, u32[]{:S(2)}) collective-permute-start(bf16[64,3712]{1,0:T(8,128)(2,1)S(1)} %slice.113.refs_3_), channel_id=1, source_target_pairs={{0,8},{1,9},{2,10},{3,11},{4,12},{5,13},{6,14},{7,15},{8,0},{9,1},... | collective-permute-start | bytes 1425416 | tf_op jit(solution)/shard_map/ppermute | solution.py:30
  112.0 24.6 %copy-start.16 = (bf16[64,3584]{1,0:T(8,128)(2,1)S(1)}, bf16[64,3584]{1,0:T(8,128)(2,1)}, u32[]{:S(2)}) copy-start(bf16[64,3584]{1,0:T(8,128)(2,1)} %get-tuple-element.22) | copy-start | bytes 1376260
  112.0 24.6 %collective-permute-start.22 = (bf16[64,3584]{1,0:T(8,128)(2,1)}, bf16[64,3584]{1,0:T(8,128)(2,1)S(1)}, u32[]{:S(2)}, u32[]{:S(2)}) collective-permute-start(bf16[64,3584]{1,0:T(8,128)(2,1)} %get-tuple-element.23), channel_id=1, source_target_pairs={{0,8},{1,9},{2,10},{3,11},{4,12},{5,13},{6,14},{7,15},{8,0},{9,1},... | collective-permute-start | bytes 1376264 | tf_op jit(solution)/shard_map/ppermute | solution.py:30
  133.6 10.8 %collective-permute-start.9 = (bf16[64,3584]{1,0:T(8,128)(2,1)}, bf16[64,3584]{1,0:T(8,128)(2,1)S(1)}, u32[]{:S(2)}, u32[]{:S(2)}) collective-permute-start(bf16[64,3584]{1,0:T(8,128)(2,1)} %get-tuple-element.17), channel_id=1, source_target_pairs={{0,8},{1,9},{2,10},{3,11},{4,12},{5,13},{6,14},{7,15},{8,0},{9,1},... | collective-permute-start | bytes 1376264 | tf_op jit(solution)/shard_map/ppermute | solution.py:30
  136.8 18.9 %collective-permute-start.23 = (bf16[192,3584]{1,0:T(8,128)(2,1)S(1)}, bf16[192,3584]{1,0:T(8,128)(2,1)S(1)}, u32[]{:S(2)}, u32[]{:S(2)}) collective-permute-start(bf16[192,3584]{1,0:T(8,128)(2,1)S(1)} %pad_maximum_fusion.3), channel_id=1, source_target_pairs={{0,6},{1,3},{2,0},{3,5},{4,2},{5,7},{6,4},{7,1},{8,14},{9,11},{10,... | collective-permute-start | bytes 4128776 | tf_op jit(solution)/shard_map/ppermute | solution.py:38
  144.6 28.8 %copy-start.12 = (bf16[64,3584]{1,0:T(8,128)(2,1)S(1)}, bf16[64,3584]{1,0:T(8,128)(2,1)}, u32[]{:S(2)}) copy-start(bf16[64,3584]{1,0:T(8,128)(2,1)} %get-tuple-element.25) | copy-start | bytes 1376260
  144.6 25.8 %collective-permute-start.10 = (bf16[192,3584]{1,0:T(8,128)(2,1)S(1)}, bf16[192,3584]{1,0:T(8,128)(2,1)S(1)}, u32[]{:S(2)}, u32[]{:S(2)}) collective-permute-start(bf16[192,3584]{1,0:T(8,128)(2,1)S(1)} %pad_maximum_fusion.2), channel_id=1, source_target_pairs={{0,6},{1,3},{2,0},{3,5},{4,2},{5,7},{6,4},{7,1},{8,14},{9,11},{10,... | collective-permute-start | bytes 4128776 | tf_op jit(solution)/shard_map/ppermute | solution.py:38
  155.8 17.6 %collective-permute-start.26 = (bf16[64,3584]{1,0:T(8,128)(2,1)S(1)}, bf16[64,3584]{1,0:T(8,128)(2,1)S(1)}, u32[]{:S(2)}, u32[]{:S(2)}) collective-permute-start(bf16[64,3584]{1,0:T(8,128)(2,1)S(1)} %slice.127), channel_id=1, source_target_pairs={{0,1},{1,0},{2,3},{3,2},{4,5},{5,4},{6,7},{7,6},{8,9},{9,8},{10,11... | collective-permute-start | bytes 1376264 | tf_op jit(solution)/shard_map/ppermute | solution.py:26
  170.5 4.3 %collective-permute-start.13 = (bf16[64,3584]{1,0:T(8,128)(2,1)S(1)}, bf16[64,3584]{1,0:T(8,128)(2,1)S(1)}, u32[]{:S(2)}, u32[]{:S(2)}) collective-permute-start(bf16[64,3584]{1,0:T(8,128)(2,1)S(1)} %slice.119), channel_id=1, source_target_pairs={{0,1},{1,0},{2,3},{3,2},{4,5},{5,4},{6,7},{7,6},{8,9},{9,8},{10,11... | collective-permute-start | bytes 1376264 | tf_op jit(solution)/shard_map/ppermute | solution.py:26
  173.7 13.8 %collective-permute-start.24 = (bf16[128,3584]{1,0:T(8,128)(2,1)S(1)}, bf16[128,3584]{1,0:T(8,128)(2,1)S(1)}, u32[]{:S(2)}, u32[]{:S(2)}) collective-permute-start(bf16[128,3584]{1,0:T(8,128)(2,1)S(1)} %pad_maximum_fusion.7), channel_id=1, source_target_pairs={{0,6},{1,3},{2,0},{3,5},{4,2},{5,7},{6,4},{7,1},{8,14},{9,11},{10,... | collective-permute-start | bytes 2752520 | tf_op jit(solution)/shard_map/ppermute | solution.py:38
  175.2 22.2 %collective-permute-start.11 = (bf16[128,3584]{1,0:T(8,128)(2,1)S(1)}, bf16[128,3584]{1,0:T(8,128)(2,1)S(1)}, u32[]{:S(2)}, u32[]{:S(2)}) collective-permute-start(bf16[128,3584]{1,0:T(8,128)(2,1)S(1)} %pad_maximum_fusion.6), channel_id=1, source_target_pairs={{0,6},{1,3},{2,0},{3,5},{4,2},{5,7},{6,4},{7,1},{8,14},{9,11},{10,... | collective-permute-start | bytes 2752520 | tf_op jit(solution)/shard_map/ppermute | solution.py:38
  175.3 22.2 %collective-permute-start.27 = (bf16[64,3584]{1,0:T(8,128)(2,1)S(1)}, bf16[64,3584]{1,0:T(8,128)(2,1)S(1)}, u32[]{:S(2)}, u32[]{:S(2)}) collective-permute-start(bf16[64,3584]{1,0:T(8,128)(2,1)S(1)} %get-tuple-element.27), channel_id=1, source_target_pairs={{0,8},{1,9},{2,10},{3,11},{4,12},{5,13},{6,14},{7,15},{8,0},{9,1},... | collective-permute-start | bytes 1376264 | tf_op jit(solution)/shard_map/ppermute | solution.py:30
  187.6 9.9 %collective-permute-start.25 = (bf16[64,3584]{1,0:T(8,128)(2,1)S(1)}, bf16[64,3584]{1,0:T(8,128)(2,1)S(1)}, u32[]{:S(2)}, u32[]{:S(2)}) collective-permute-start(bf16[64,3584]{1,0:T(8,128)(2,1)S(1)} %slice.125), channel_id=1, source_target_pairs={{0,1},{1,0},{2,3},{3,2},{4,5},{5,4},{6,7},{7,6},{8,9},{9,8},{10,11... | collective-permute-start | bytes 1376264 | tf_op jit(solution)/shard_map/ppermute | solution.py:26
  187.7 13.3 %collective-permute-start.14 = (bf16[64,3584]{1,0:T(8,128)(2,1)S(1)}, bf16[64,3584]{1,0:T(8,128)(2,1)S(1)}, u32[]{:S(2)}, u32[]{:S(2)}) collective-permute-start(bf16[64,3584]{1,0:T(8,128)(2,1)S(1)} %get-tuple-element.29), channel_id=1, source_target_pairs={{0,8},{1,9},{2,10},{3,11},{4,12},{5,13},{6,14},{7,15},{8,0},{9,1},... | collective-permute-start | bytes 1376264 | tf_op jit(solution)/shard_map/ppermute | solution.py:30
  197.4 3.6 %collective-permute-start.12 = (bf16[64,3584]{1,0:T(8,128)(2,1)S(1)}, bf16[64,3584]{1,0:T(8,128)(2,1)S(1)}, u32[]{:S(2)}, u32[]{:S(2)}) collective-permute-start(bf16[64,3584]{1,0:T(8,128)(2,1)S(1)} %slice.117), channel_id=1, source_target_pairs={{0,1},{1,0},{2,3},{3,2},{4,5},{5,4},{6,7},{7,6},{8,9},{9,8},{10,11... | collective-permute-start | bytes 1376264 | tf_op jit(solution)/shard_map/ppermute | solution.py:26
  197.8 21.5 %collective-permute-start.28 = (bf16[64,3584]{1,0:T(8,128)(2,1)S(1)}, bf16[64,3584]{1,0:T(8,128)(2,1)S(1)}, u32[]{:S(2)}, u32[]{:S(2)}) collective-permute-start(bf16[64,3584]{1,0:T(8,128)(2,1)S(1)} %fusion.13), channel_id=1, source_target_pairs={{16,0},{32,16},{48,32},{64,48},{80,64},{96,80},{112,96},{0,112},{1... | collective-permute-start | bytes 1376264 | tf_op jit(solution)/shard_map/ppermute | solution.py:44
  201.3 18.1 %collective-permute-start.15 = (bf16[64,3584]{1,0:T(8,128)(2,1)S(1)}, bf16[64,3584]{1,0:T(8,128)(2,1)S(1)}, u32[]{:S(2)}, u32[]{:S(2)}) collective-permute-start(bf16[64,3584]{1,0:T(8,128)(2,1)S(1)} %fusion.6), channel_id=1, source_target_pairs={{112,0},{0,16},{16,32},{32,48},{48,64},{64,80},{80,96},{96,112},{1... | collective-permute-start | bytes 1376264 | tf_op jit(solution)/shard_map/ppermute | solution.py:44
  (22 other events, 243.3 us)

commit v2 on v1

v2 whole, which is shorter than its diff:
```python
import functools

import jax
import jax.numpy as jnp
from jax import lax
from jax.experimental import pallas as pl
from jax.experimental.pallas import tpu as pltpu
from jax.sharding import PartitionSpec as P

EXTRA = 128
TILE = 256
WIDE = 1792


def place(y, z, c):
    return (y * 4 + z) * 2 + c


DEVICES = [(y, z, c) for y in range(2) for z in range(4) for c in range(2)]
CORE = [(place(y, z, c), place(y, z, 1 - c)) for y, z, c in DEVICES]
ACROSS = [(place(y, z, c), place(1 - y, z, c)) for y, z, c in DEVICES]
OUTWARD = [(place(y, z, c), place(y, (z + 1 - 2 * c) % 4, c)) for y, z, c in DEVICES]
OPPOSITE = [(place(y, z, c), place(y, (z + 2) % 4, c)) for y, z, c in DEVICES]
CROSSING = [(place(y, z, c), place(y, (z - 1 + 2 * c) % 4, 1 - c)) for y, z, c in DEVICES]


def core(block):
    return lax.ppermute(block, "expert", CORE)


def across(block):
    return lax.ppermute(block, "expert", ACROSS)


def outward(block):
    return lax.ppermute(block, "expert", OUTWARD)


def crossing(block):
    return lax.ppermute(block, "expert", CROSSING)


def homeward(block):
    return lax.ppermute(block, "expert", [(target, source) for source, target in OUTWARD])


def recrossing(block):
    return lax.ppermute(block, "expert", [(target, source) for source, target in CROSSING])


def opposite(block):
    return lax.ppermute(block, "expert", OPPOSITE)


def shifted(block, distance):
    sections = lax.axis_size("section")
    route = [(i, (i + distance) % sections) for i in range(sections)]
    return lax.ppermute(block, "section", route)


def shifted_across(block, distance):
    sections, group = lax.axis_size("section"), len(DEVICES)
    route = [
        (i * group + source, (i + distance) % sections * group + target)
        for i in range(sections)
        for source, target in ACROSS
    ]
    return lax.ppermute(block, ("section", "expert"), route)


def ffn_kernel(parts, width, *refs):
    x_refs = refs[:parts]
    mine = refs[parts : parts + 3]
    other = refs[parts + 3 : parts + 6]
    out_refs = refs[parts + 6 : 2 * parts + 6]
    x_all, hidden_all = refs[2 * parts + 6 :]
    units = mine[2].shape[0]
    expert = lax.axis_index("expert") // 4
    shares = []
    row = 0
    for x_ref in x_refs:
        rows = x_ref.shape[0]
        x_all[row : row + rows, :] = x_ref[:, :width]
        tail = x_ref[:, width:].astype(jnp.float32)
        column = lax.broadcasted_iota(jnp.int32, tail.shape, 1)
        kept = jnp.where((column == expert) | (column == expert + 4), tail, 0.0)
        shares.append(jnp.sum(kept, axis=1, keepdims=True))
        row += rows
    share = jnp.concatenate(shares)
    for side, (gate_ref, up_ref, _) in enumerate((mine, other)):
        for start in range(0, units, TILE):
            x = x_all[...]
            columns = pl.ds(start, TILE)
            gate_value = jnp.dot(x, gate_ref[:, columns], preferred_element_type=jnp.float32)
            up_value = jnp.dot(x, up_ref[:, columns], preferred_element_type=jnp.float32)
            hidden = gate_value * (1.0 / (1.0 + jnp.exp(-gate_value))) * up_value * share
            hidden_all[:, pl.ds(side * units + start, TILE)] = hidden.astype(jnp.bfloat16)

    @pl.loop(0, width // WIDE)
    def _(n):
        columns = pl.ds(pl.multiple_of(n * WIDE, WIDE), WIDE)
        partial = jnp.dot(hidden_all[:, :units], mine[2][:, columns], preferred_element_type=jnp.float32)
        partial += jnp.dot(hidden_all[:, units:], other[2][:, columns], preferred_element_type=jnp.float32)
        row = 0
        for out_ref in out_refs:
            rows = out_ref.shape[0]
            out_ref[:, columns] = partial[row : row + rows].astype(out_ref.dtype)
            row += rows


def ffn(blocks, mine, other):
    units, width = mine[2].shape
    rows = [block.shape[0] for block in blocks]
    total_rows = sum(rows)
    vmem = pl.BlockSpec(memory_space=pltpu.VMEM)
    return pl.pallas_call(
        functools.partial(ffn_kernel, len(blocks), width),
        in_specs=[vmem] * (len(blocks) + 6),
        out_specs=[vmem] * len(blocks),
        out_shape=[jax.ShapeDtypeStruct((r, width), jnp.bfloat16) for r in rows],
        scratch_shapes=[
            pltpu.VMEM((total_rows, width), jnp.bfloat16),
            pltpu.VMEM((total_rows, 2 * units), jnp.bfloat16),
        ],
        cost_estimate=pl.CostEstimate(
            flops=2 * total_rows * width * 2 * units * 3,
            bytes_accessed=2 * 3 * 2 * units * width,
            transcendentals=total_rows * 2 * units,
        ),
        compiler_params=pltpu.CompilerParams(vmem_limit_bytes=14 * 1024 * 1024),
    )(*blocks, *mine, *other)


def prepare_kernel(acts_hbm, gain_hbm, routes_hbm, gates_hbm, out_ref, acts_ref, gain_ref, routes_ref, gates_ref, sems):
    pairs = ((routes_hbm, routes_ref), (gates_hbm, gates_ref), (gain_hbm, gain_ref), (acts_hbm, acts_ref))
    copies = [pltpu.make_async_copy(source, target, sems.at[i]) for i, (source, target) in enumerate(pairs)]
    for copy in copies:
        copy.start()
    for copy in copies:
        copy.wait()
    width = acts_ref.shape[1]
    widened = acts_ref[...].astype(jnp.float32)
    mean_square = jnp.mean(widened * widened, axis=-1, keepdims=True)
    normed = widened * lax.rsqrt(mean_square + 1e-06) * gain_ref[...]
    out_ref[:, :width] = normed.astype(jnp.bfloat16)
    rows = acts_ref.shape[0]
    label = lax.broadcasted_iota(jnp.int32, (EXTRA, rows), 0)
    expert = jnp.where(label < 8, label % 4, -1)
    mixing = jnp.zeros(label.shape, jnp.float32)
    for k in range(routes_ref.shape[0]):
        mixing += jnp.where(routes_ref[k : k + 1, :] == expert, gates_ref[k : k + 1, :], 0.0)
    coarse = mixing.astype(jnp.bfloat16).astype(jnp.float32)
    tail = jnp.where(label < 4, coarse, mixing - coarse)
    out_ref[:, width:] = tail.T.astype(jnp.bfloat16)


def prepare(activations, gain, routes, gate_weights):
    rows, width = activations.shape
    arrays = (activations, gain, routes.T, gate_weights.T)
    return pl.pallas_call(
        prepare_kernel,
        in_specs=[pl.BlockSpec(memory_space=pltpu.HBM)] * 4,
        out_specs=pl.BlockSpec(memory_space=pltpu.VMEM),
        out_shape=jax.ShapeDtypeStruct((rows, width + EXTRA), jnp.bfloat16),
        scratch_shapes=[pltpu.VMEM(array.shape, array.dtype) for array in arrays] + [pltpu.SemaphoreType.DMA((4,))],
        cost_estimate=pl.CostEstimate(flops=6 * rows * width, bytes_accessed=4 * rows * width, transcendentals=rows),
        compiler_params=pltpu.CompilerParams(vmem_limit_bytes=8 * 1024 * 1024),
    )(*arrays)


def after(block, *earlier):
    return lax.optimization_barrier((block, *earlier))[0]


def add(*terms):
    total = terms[0].astype(jnp.float32)
    for term in terms[1:]:
        total = total + term.astype(jnp.float32)
    return total.astype(jnp.bfloat16)


def first_step(own):
    return across(own), outward(own), crossing(own)


def second_step(facing, near, beside):
    facing, near, beside = lax.optimization_barrier((facing, near, beside))
    rows = facing.shape[0]
    ahead = outward(jnp.concatenate([near, facing]))
    facing_beside = crossing(facing)
    return ahead[:rows], ahead[rows:], facing_beside


def combine(activations, close, distant, last, distance):
    own, near, beside, facing = close
    far, facing_near, facing_beside = distant
    rows = own.shape[0]
    far = add(far, across(last))
    ahead = homeward(jnp.concatenate([far, facing_near]))
    near = add(near, ahead[:rows])
    facing = add(facing, ahead[rows:], recrossing(facing_beside))
    near, facing, beside = lax.optimization_barrier((near, facing, beside))
    crossed = shifted_across(facing, distance)
    layer = add(activations, own, homeward(near), recrossing(beside))
    return add(shifted(layer, distance), crossed)


def body(
    up_acts,
    down_acts,
    norm_gain,
    up_routes,
    down_routes,
    up_gates,
    down_gates,
    gate_weight,
    up_weight,
    down_weight,
):
    mine = (gate_weight[0], up_weight[0], down_weight[0])
    other = tuple(core(w) for w in mine)
    up_own = prepare(up_acts[0], norm_gain, up_routes[0], up_gates[0])
    down_own = prepare(down_acts[0], norm_gain, down_routes[0], down_gates[0])
    run = functools.partial(ffn, mine=mine, other=other)
    up_facing, up_near, up_beside = first_step(up_own)
    down_facing, down_near, down_beside = first_step(down_own)
    up_distant = second_step(up_facing, up_near, up_beside)
    up_close = run((up_own, up_near, up_beside, up_facing))
    down_distant = second_step(after(down_facing, up_close[0]), down_near, down_beside)
    down_close = run((down_own, down_near, down_beside, down_facing))
    up_last = across(after(up_distant[0], down_close[0]))
    up_distant = run(up_distant)
    down_last = across(after(down_distant[0], up_distant[0]))
    down_distant = run(down_distant)
    (up_last,) = run((after(up_last, down_distant[0]),))
    (down_last,) = run((after(down_last, up_last),))
    next_up = combine(up_acts[0], up_close, up_distant, up_last, 1)
    next_down = combine(down_acts[0], down_close, down_distant, down_last, -1)
    return (next_up[None], next_down[None])


def solution(mesh):
    return jax.shard_map(
        body,
        mesh=mesh,
        in_specs=(
            P("section", "expert", None),
            P("section", "expert", None),
            P("section", None),
            P("section", "expert", None),
            P("section", "expert", None),
            P("section", "expert", None),
            P("section", "expert", None),
            P("section", None, "expert"),
            P("section", None, "expert"),
            P("section", "expert", None),
        ),
        out_specs=(P("section", "expert", None), P("section", "expert", None)),
        check_vma=False,
    )
```

time: 222 us -> 174 us (0.78)
  waiting for transfers between devices: 123 us -> 70.2 us
  starting transfers between devices: 39.2 us -> 56.2 us
  Pallas kernels: 41 us -> 31.7 us
  other arithmetic: 6.83 us -> 3.21 us
    ppermute x4, waiting for transfers between devices: 38.2 us -> 10.1 us  [outward(): return lax.ppermute(block, 'expert', OUTWARD)]
    ppermute x4 -> x14, starting transfers between devices: 0.47 us -> 21.8 us  [the longest x4 6.84 us: homeward(): lax.ppermute(block, 'expert', [(target, source) for source, target in OUT...]
    ppermute x4 -> x14, waiting for transfers between devices: 43.2 us -> 25 us  [the longest x4 22.2 us: homeward(): lax.ppermute(block, 'expert', [(target, source) for source, target in OUT...]
    pallas_call x2 -> x8, Pallas kernels: 41 us -> 31.7 us  [the longest x6 30.6 us: ffn(): pl.pallas_call(functools.partial(ffn_kernel, len(blocks), width), in_spec...]
    ppermute x11 -> x3, starting transfers between devices: 10.2 us -> 2.01 us  [core(): return lax.ppermute(block, 'expert', CORE)]
    ppermute x2, waiting for transfers between devices: 17.8 us -> 10 us  [shifted(): return lax.ppermute(block, 'section', route)]
    unnamed x52 -> x28, local copies, waits for them, and re-layouts: 6.12 us -> 10.3 us
    ppermute x8 -> x6, waiting for transfers between devices: 22.5 us -> 25.1 us  [across(): return lax.ppermute(block, 'expert', ACROSS)]
  transfers between devices with their start and end apart: 29 -> 29, of which waited for: 13 -> 13; matrix products, arithmetic and copies ran while one was open for 2% -> 1% of each run, Pallas kernels for 19% -> 18%
where the time goes in v2:
time: 174 us; the launch traced here: 173 us
  waiting for transfers between devices  70.2 us (40%)
  starting transfers between devices  56.2 us (32%)
  Pallas kernels  31.7 us (18%)
  local copies, waits for them, and re-layouts  10.4 us (6%)
  other arithmetic  3.21 us (2%)
    pallas_call x6, Pallas kernels, ffn(): pl.pallas_call(functools.partial(ffn_kernel, len(blocks), width), in_spec...  30.6 us
    ppermute x6, waiting for transfers between devices, across(): return lax.ppermute(block, 'expert', ACROSS)  25.1 us
    ppermute x4, waiting for transfers between devices, homeward(): lax.ppermute(block, 'expert', [(target, source) for source, target in OUT...  22.2 us
    ppermute x6, starting transfers between devices, across(): return lax.ppermute(block, 'expert', ACROSS)  15.3 us
    ppermute x4, starting transfers between devices, outward(): return lax.ppermute(block, 'expert', OUTWARD)  12.4 us
    unnamed x28, local copies, waits for them, and re-layouts  10.3 us
    ppermute x4, waiting for transfers between devices, outward(): return lax.ppermute(block, 'expert', OUTWARD)  10.1 us
    ppermute x2, waiting for transfers between devices, shifted(): return lax.ppermute(block, 'section', route)  10 us
  transfers between devices with their start and end apart: 29, of which 13 were waited for; matrix products, arithmetic and copies ran while one was open for 1% of the time, Pallas kernels for 18%

profile of v2, /device:TPU:1, one launch (start us, length us, event | category | flops | bytes accessed | tf_op | source)
XLA Modules:
  0.0 172.6 jit_solution(16389829762308470545)
XLA Ops:
  6.3 3.1 %collective-permute-start.2 = (bf16[64,3712]{1,0:T(8,128)(2,1)S(1)}, bf16[64,3712]{1,0:T(8,128)(2,1)S(1)}, u32[]{:S(2)}, u32[]{:S(2)}) collective-permute-start(bf16[64,3712]{1,0:T(8,128)(2,1)S(1)} %shard_map.113.refs_0_), channel_id=1, source_target_pairs={{0,8},{1,9},{2,10},{3,11},{4,12},{5,13},{6,14},{7,15},{8,0},{9,1},... | collective-permute-start | bytes 1425416 | tf_op jit(solution)/shard_map/ppermute | solution.py:32
  9.4 3.8 %collective-permute-start = (bf16[64,3712]{1,0:T(8,128)(2,1)S(1)}, bf16[64,3712]{1,0:T(8,128)(2,1)S(1)}, u32[]{:S(2)}, u32[]{:S(2)}) collective-permute-start(bf16[64,3712]{1,0:T(8,128)(2,1)S(1)} %shard_map.113.refs_0_), channel_id=1, source_target_pairs={{0,2},{1,7},{2,4},{3,1},{4,6},{5,3},{6,0},{7,5},{8,10},{9,15},{10,... | collective-permute-start | bytes 1425416 | tf_op jit(solution)/shard_map/ppermute | solution.py:36
  13.1 7.2 %collective-permute-done.2.refs_3_ = bf16[64,3712]{1,0:T(8,128)(2,1)S(1)} collective-permute-done((bf16[64,3712]{1,0:T(8,128)(2,1)S(1)}, bf16[64,3712]{1,0:T(8,128)(2,1)S(1)}, u32[]{:S(2)}, u32[]{:S(2)}) %collective-permute-start.2) | collective-permute-done | bytes 475168 | tf_op jit(solution)/shard_map/ppermute | solution.py:32
  20.3 2.4 %collective-permute-start.1 = (bf16[64,3712]{1,0:T(8,128)(2,1)S(1)}, bf16[64,3712]{1,0:T(8,128)(2,1)S(1)}, u32[]{:S(2)}, u32[]{:S(2)}) collective-permute-start(bf16[64,3712]{1,0:T(8,128)(2,1)S(1)} %shard_map.113.refs_0_), channel_id=1, source_target_pairs={{0,7},{1,2},{2,1},{3,4},{4,3},{5,6},{6,5},{7,0},{8,15},{9,10},{10,... | collective-permute-start | bytes 1425416 | tf_op jit(solution)/shard_map/ppermute | solution.py:40
  30.9 3.0 %collective-permute-start.10 = (bf16[64,3712]{1,0:T(8,128)(2,1)S(1)}, bf16[64,3712]{1,0:T(8,128)(2,1)S(1)}, u32[]{:S(2)}, u32[]{:S(2)}) collective-permute-start(bf16[64,3712]{1,0:T(8,128)(2,1)S(1)} %shard_map.116.refs_0_), channel_id=1, source_target_pairs={{0,8},{1,9},{2,10},{3,11},{4,12},{5,13},{6,14},{7,15},{8,0},{9,1},... | collective-permute-start | bytes 1425416 | tf_op jit(solution)/shard_map/ppermute | solution.py:32
  34.5 7.1 %collective-permute-start.6 = (bf16[128,3712]{1,0:T(8,128)(2,1)S(1)}, bf16[128,3712]{1,0:T(8,128)(2,1)S(1)}, u32[]{:S(2)}, u32[]{:S(2)}) collective-permute-start(bf16[128,3712]{1,0:T(8,128)(2,1)S(1)} %pad_maximum_fusion), channel_id=1, source_target_pairs={{0,2},{1,7},{2,4},{3,1},{4,6},{5,3},{6,0},{7,5},{8,10},{9,15},{10,... | collective-permute-start | bytes 2850824 | tf_op jit(solution)/shard_map/ppermute | solution.py:36
  41.6 2.0 %copy-done.1 = bf16[1,3584,512]{2,1,0:T(8,128)(2,1)S(1)} copy-done((bf16[1,3584,512]{2,1,0:T(8,128)(2,1)S(1)}, bf16[1,3584,512]{2,1,0:T(8,128)(2,1)}, u32[]{:S(2)}) %copy-start.1) | copy-done | bytes 3670040
  43.7 2.0 %copy-done.3 = bf16[1,512,3584]{2,1,0:T(8,128)(2,1)S(1)} copy-done((bf16[1,512,3584]{2,1,0:T(8,128)(2,1)S(1)}, bf16[1,512,3584]{2,1,0:T(8,128)(2,1)}, u32[]{:S(2)}) %copy-start.3) | copy-done | bytes 3670040
  45.7 6.3 %shard_map.114 = (bf16[64,3584]{1,0:T(8,128)(2,1)S(1)}, bf16[64,3584]{1,0:T(8,128)(2,1)S(1)}, bf16[64,3584]{1,0:T(8,128)(2,1)S(1)}, bf16[64,3584]{1,0:T(8,128)(2,1)S(1)}) custom-call(bf16[64,3712]{1,0:T(8,128)(2,1)S(1)} %shard_map.113.refs_0_, bf16[64,3712]{1,0:T(8,128)(2,1)S(1)} %collective-permute-done.refs_1_, ...), custom_call_target="tpu_custom_call" | custom-call | flops 5637144576 | bytes 22020096 | tf_op jit(solution)/shard_map/pallas_call | solution.py:116
  52.2 4.5 %collective-permute-done.6 = bf16[128,3712]{1,0:T(8,128)(2,1)S(1)} collective-permute-done((bf16[128,3712]{1,0:T(8,128)(2,1)S(1)}, bf16[128,3712]{1,0:T(8,128)(2,1)S(1)}, u32[]{:S(2)}, u32[]{:S(2)}) %collective-permute-start.6) | collective-permute-done | bytes 950304 | tf_op jit(solution)/shard_map/ppermute | solution.py:36
  57.2 6.3 %shard_map.117 = (bf16[64,3584]{1,0:T(8,128)(2,1)S(1)}, bf16[64,3584]{1,0:T(8,128)(2,1)S(1)}, bf16[64,3584]{1,0:T(8,128)(2,1)S(1)}, bf16[64,3584]{1,0:T(8,128)(2,1)S(1)}) custom-call(bf16[64,3712]{1,0:T(8,128)(2,1)S(1)} %shard_map.116.refs_0_, bf16[64,3712]{1,0:T(8,128)(2,1)S(1)} %collective-permute-done.8.refs_1_, ...), custom_call_target="tpu_custom_call" | custom-call | flops 5637144576 | bytes 22020096 | tf_op jit(solution)/shard_map/pallas_call | solution.py:116
  63.5 3.0 %collective-permute-start.11 = (bf16[64,3712]{1,0:T(8,128)(2,1)S(1)}, bf16[64,3712]{1,0:T(8,128)(2,1)S(1)}, u32[]{:S(2)}, u32[]{:S(2)}) collective-permute-start(bf16[64,3712]{1,0:T(8,128)(2,1)S(1)} %get-tuple-element.37.refs_0_), channel_id=1, source_target_pairs={{0,8},{1,9},{2,10},{3,11},{4,12},{5,13},{6,14},{7,15},{8,0},{9,1},... | collective-permute-start | bytes 1425416 | tf_op jit(solution)/shard_map/ppermute | solution.py:32
  66.5 5.5 %collective-permute-done.12 = bf16[128,3712]{1,0:T(8,128)(2,1)S(1)} collective-permute-done((bf16[128,3712]{1,0:T(8,128)(2,1)S(1)}, bf16[128,3712]{1,0:T(8,128)(2,1)S(1)}, u32[]{:S(2)}, u32[]{:S(2)}) %collective-permute-start.12) | collective-permute-done | bytes 950304 | tf_op jit(solution)/shard_map/ppermute | solution.py:36
  72.1 4.9 %shard_map.118 = (bf16[64,3584]{1,0:T(8,128)(2,1)S(1)}, bf16[64,3584]{1,0:T(8,128)(2,1)S(1)}, bf16[64,3584]{1,0:T(8,128)(2,1)S(1)}) custom-call(bf16[64,3712]{1,0:T(8,128)(2,1)S(1)} %get-tuple-element.51.refs_0_, bf16[64,3712]{1,0:T(8,128)(2,1)S(1)} %get-tuple-element.60.refs_1_, bf16[64,3712]{1,0:T(8,128)(2,1)S(1)} %collective-permute-done.13.refs_2_, ...), custom_call_target="tpu_custom_call" | custom-call | flops 4227858432 | bytes 22020096 | tf_op jit(solution)/shard_map/pallas_call | solution.py:116
  77.0 4.2 %shard_map.119 = bf16[64,3584]{1,0:T(8,128)(2,1)S(1)} custom-call(bf16[64,3712]{1,0:T(8,128)(2,1)S(1)} %collective-permute-done.11.refs_0_, bf16[3584,512]{1,0:T(8,128)(2,1)S(1)} %bitcast.27, bf16[3584,512]{1,0:T(8,128)(2,1)S(1)} %bitcast.34, bf16[512,3584]{1,0:T(8,128)(2,1)S(1)} %bitcast.41, ...), custom_call_target="tpu_custom_call" | custom-call | flops 1409286144 | bytes 22020096 | tf_op jit(solution)/shard_map/pallas_call | solution.py:116
  81.2 3.2 %collective-permute-start.14 = (bf16[64,3584]{1,0:T(8,128)(2,1)S(1)}, bf16[64,3584]{1,0:T(8,128)(2,1)S(1)}, u32[]{:S(2)}, u32[]{:S(2)}) collective-permute-start(bf16[64,3584]{1,0:T(8,128)(2,1)S(1)} %shard_map.119), channel_id=1, source_target_pairs={{0,8},{1,9},{2,10},{3,11},{4,12},{5,13},{6,14},{7,15},{8,0},{9,1},... | collective-permute-start | bytes 1376264 | tf_op jit(solution)/shard_map/ppermute | solution.py:32
  84.4 4.9 %shard_map.115 = (bf16[64,3584]{1,0:T(8,128)(2,1)S(1)}, bf16[64,3584]{1,0:T(8,128)(2,1)S(1)}, bf16[64,3584]{1,0:T(8,128)(2,1)S(1)}) custom-call(bf16[64,3712]{1,0:T(8,128)(2,1)S(1)} %get-tuple-element.37.refs_0_, bf16[64,3712]{1,0:T(8,128)(2,1)S(1)} %get-tuple-element.62.refs_1_, bf16[64,3712]{1,0:T(8,128)(2,1)S(1)} %collective-permute-done.7.refs_2_, ...), custom_call_target="tpu_custom_call" | custom-call | flops 4227858432 | bytes 22020096 | tf_op jit(solution)/shard_map/pallas_call | solution.py:116
  89.2 2.7 %collective-permute-start.16 = (bf16[64,3584]{1,0:T(8,128)(2,1)S(1)}, bf16[64,3584]{1,0:T(8,128)(2,1)S(1)}, u32[]{:S(2)}, u32[]{:S(2)}) collective-permute-start(bf16[64,3584]{1,0:T(8,128)(2,1)S(1)} %get-tuple-element.45), channel_id=1, source_target_pairs={{7,0},{2,1},{1,2},{4,3},{3,4},{6,5},{5,6},{0,7},{15,8},{10,9},{9,1... | collective-permute-start | bytes 1376264 | tf_op jit(solution)/shard_map/ppermute | solution.py:48
  93.3 10.3 %collective-permute-done.21.refs_0_ = bf16[64,3712]{1,0:T(8,128)(2,1)S(1)} collective-permute-done((bf16[64,3712]{1,0:T(8,128)(2,1)S(1)}, bf16[64,3712]{1,0:T(8,128)(2,1)S(1)}, u32[]{:S(2)}, u32[]{:S(2)}) %collective-permute-start.21) | collective-permute-done | bytes 475168 | tf_op jit(solution)/shard_map/ppermute | solution.py:32
  103.7 4.2 %shard_map.120 = bf16[64,3584]{1,0:T(8,128)(2,1)S(1)} custom-call(bf16[64,3712]{1,0:T(8,128)(2,1)S(1)} %collective-permute-done.21.refs_0_, bf16[3584,512]{1,0:T(8,128)(2,1)S(1)} %bitcast.29, bf16[3584,512]{1,0:T(8,128)(2,1)S(1)} %bitcast.36, bf16[512,3584]{1,0:T(8,128)(2,1)S(1)} %bitcast.43, ...), custom_call_target="tpu_custom_call" | custom-call | flops 1409286144 | bytes 22020096 | tf_op jit(solution)/shard_map/pallas_call | solution.py:116
  107.8 3.0 %collective-permute-start.22 = (bf16[64,3584]{1,0:T(8,128)(2,1)S(1)}, bf16[64,3584]{1,0:T(8,128)(2,1)S(1)}, u32[]{:S(2)}, u32[]{:S(2)}) collective-permute-start(bf16[64,3584]{1,0:T(8,128)(2,1)S(1)} %shard_map.120), channel_id=1, source_target_pairs={{0,8},{1,9},{2,10},{3,11},{4,12},{5,13},{6,14},{7,15},{8,0},{9,1},... | collective-permute-start | bytes 1376264 | tf_op jit(solution)/shard_map/ppermute | solution.py:32
  111.8 6.5 %collective-permute-done.22 = bf16[64,3584]{1,0:T(8,128)(2,1)S(1)} collective-permute-done((bf16[64,3584]{1,0:T(8,128)(2,1)S(1)}, bf16[64,3584]{1,0:T(8,128)(2,1)S(1)}, u32[]{:S(2)}, u32[]{:S(2)}) %collective-permute-start.22) | collective-permute-done | bytes 458784 | tf_op jit(solution)/shard_map/ppermute | solution.py:32
  118.5 2.4 %collective-permute-start.23 = (bf16[128,3584]{1,0:T(8,128)(2,1)S(1)}, bf16[128,3584]{1,0:T(8,128)(2,1)S(1)}, u32[]{:S(2)}, u32[]{:S(2)}) collective-permute-start(bf16[128,3584]{1,0:T(8,128)(2,1)S(1)} %pad_maximum_fusion.3), channel_id=1, source_target_pairs={{2,0},{7,1},{4,2},{1,3},{6,4},{3,5},{0,6},{5,7},{10,8},{15,9},{12,... | collective-permute-start | bytes 2752520 | tf_op jit(solution)/shard_map/ppermute | solution.py:44
  120.9 5.1 %collective-permute-done.15 = bf16[128,3584]{1,0:T(8,128)(2,1)S(1)} collective-permute-done((bf16[128,3584]{1,0:T(8,128)(2,1)S(1)}, bf16[128,3584]{1,0:T(8,128)(2,1)S(1)}, u32[]{:S(2)}, u32[]{:S(2)}) %collective-permute-start.15) | collective-permute-done | bytes 917536 | tf_op jit(solution)/shard_map/ppermute | solution.py:44
  127.1 2.2 %collective-permute-start.18 = (bf16[64,3584]{1,0:T(8,128)(2,1)S(1)}, bf16[64,3584]{1,0:T(8,128)(2,1)S(1)}, u32[]{:S(2)}, u32[]{:S(2)}) collective-permute-start(bf16[64,3584]{1,0:T(8,128)(2,1)S(1)} %get-tuple-element.48), channel_id=1, source_target_pairs={{7,0},{2,1},{1,2},{4,3},{3,4},{6,5},{5,6},{0,7},{15,8},{10,9},{9,1... | collective-permute-start | bytes 1376264 | tf_op jit(solution)/shard_map/ppermute | solution.py:48
  131.0 6.6 %collective-permute-done.23 = bf16[128,3584]{1,0:T(8,128)(2,1)S(1)} collective-permute-done((bf16[128,3584]{1,0:T(8,128)(2,1)S(1)}, bf16[128,3584]{1,0:T(8,128)(2,1)S(1)}, u32[]{:S(2)}, u32[]{:S(2)}) %collective-permute-start.23) | collective-permute-done | bytes 917536 | tf_op jit(solution)/shard_map/ppermute | solution.py:44
  138.4 1.7 %collective-permute-start.25 = (bf16[64,3584]{1,0:T(8,128)(2,1)S(1)}, bf16[64,3584]{1,0:T(8,128)(2,1)S(1)}, u32[]{:S(2)}, u32[]{:S(2)}) collective-permute-start(bf16[64,3584]{1,0:T(8,128)(2,1)S(1)} %get-tuple-element.57), channel_id=1, source_target_pairs={{2,0},{7,1},{4,2},{1,3},{6,4},{3,5},{0,6},{5,7},{10,8},{15,9},{12,... | collective-permute-start | bytes 1376264 | tf_op jit(solution)/shard_map/ppermute | solution.py:44
  141.4 5.7 %collective-permute-done.17 = bf16[64,3584]{1,0:T(8,128)(2,1)S(1)} collective-permute-done((bf16[64,3584]{1,0:T(8,128)(2,1)S(1)}, bf16[64,3584]{1,0:T(8,128)(2,1)S(1)}, u32[]{:S(2)}, u32[]{:S(2)}) %collective-permute-start.17) | collective-permute-done | bytes 458784 | tf_op jit(solution)/shard_map/ppermute | solution.py:44
  148.6 3.7 %collective-permute-start.28 = (bf16[64,3584]{1,0:T(8,128)(2,1)S(1)}, bf16[64,3584]{1,0:T(8,128)(2,1)S(1)}, u32[]{:S(2)}, u32[]{:S(2)}) collective-permute-start(bf16[64,3584]{1,0:T(8,128)(2,1)S(1)} %get-tuple-element.59), channel_id=1, source_target_pairs={{0,120},{1,121},{2,122},{3,123},{4,124},{5,125},{6,126},{7,127},{8... | collective-permute-start | bytes 1376264 | tf_op jit(solution)/shard_map/ppermute | solution.py:68
  152.3 4.9 %collective-permute-done.25 = bf16[64,3584]{1,0:T(8,128)(2,1)S(1)} collective-permute-done((bf16[64,3584]{1,0:T(8,128)(2,1)S(1)}, bf16[64,3584]{1,0:T(8,128)(2,1)S(1)}, u32[]{:S(2)}, u32[]{:S(2)}) %collective-permute-start.25) | collective-permute-done | bytes 458784 | tf_op jit(solution)/shard_map/ppermute | solution.py:44
  157.4 3.4 %collective-permute-start.27 = (bf16[64,3584]{1,0:T(8,128)(2,1)S(1)}, bf16[64,3584]{1,0:T(8,128)(2,1)S(1)}, u32[]{:S(2)}, u32[]{:S(2)}) collective-permute-start(bf16[64,3584]{1,0:T(8,128)(2,1)S(1)} %add_convert_fusion.1), channel_id=1, source_target_pairs={{0,112},{16,0},{32,16},{48,32},{64,48},{80,64},{96,80},{112,96},{1... | collective-permute-start | bytes 1376264 | tf_op jit(solution)/shard_map/ppermute | solution.py:58
  161.8 10.0 %collective-permute-done.27 = bf16[64,3584]{1,0:T(8,128)(2,1)S(1)} collective-permute-done((bf16[64,3584]{1,0:T(8,128)(2,1)S(1)}, bf16[64,3584]{1,0:T(8,128)(2,1)S(1)}, u32[]{:S(2)}, u32[]{:S(2)}) %collective-permute-start.27) | collective-permute-done | bytes 458784 | tf_op jit(solution)/shard_map/ppermute | solution.py:58
  (76 shorter events, 26.0 us)
Async XLA Ops:
  0.6 30.3 %collective-permute-start.3 = (bf16[3584,512]{1,0:T(8,128)(2,1)}, bf16[3584,512]{1,0:T(8,128)(2,1)S(1)}, u32[]{:S(2)}, u32[]{:S(2)}) collective-permute-start(bf16[3584,512]{1,0:T(8,128)(2,1)} %bitcast.23), channel_id=1, source_target_pairs={{0,1},{1,0},{2,3},{3,2},{4,5},{5,4},{6,7},{7,6},{8,9},{9,8},{10,11... | collective-permute-start | bytes 11010056 | tf_op jit(solution)/shard_map/ppermute | solution.py:28
  2.1 31.8 %collective-permute-start.4 = (bf16[3584,512]{1,0:T(8,128)(2,1)}, bf16[3584,512]{1,0:T(8,128)(2,1)S(1)}, u32[]{:S(2)}, u32[]{:S(2)}) collective-permute-start(bf16[3584,512]{1,0:T(8,128)(2,1)} %bitcast.30), channel_id=1, source_target_pairs={{0,1},{1,0},{2,3},{3,2},{4,5},{5,4},{6,7},{7,6},{8,9},{9,8},{10,11... | collective-permute-start | bytes 11010056 | tf_op jit(solution)/shard_map/ppermute | solution.py:28
  2.2 32.3 %collective-permute-start.5 = (bf16[512,3584]{1,0:T(8,128)(2,1)}, bf16[512,3584]{1,0:T(8,128)(2,1)S(1)}, u32[]{:S(2)}, u32[]{:S(2)}) collective-permute-start(bf16[512,3584]{1,0:T(8,128)(2,1)} %bitcast.37), channel_id=1, source_target_pairs={{0,1},{1,0},{2,3},{3,2},{4,5},{5,4},{6,7},{7,6},{8,9},{9,8},{10,11... | collective-permute-start | bytes 11010056 | tf_op jit(solution)/shard_map/ppermute | solution.py:28
  5.7 35.9 %copy-start = (bf16[1,3584,512]{2,1,0:T(8,128)(2,1)S(1)}, bf16[1,3584,512]{2,1,0:T(8,128)(2,1)}, u32[]{:S(2)}) copy-start(bf16[1,3584,512]{2,1,0:T(8,128)(2,1)} %param.17) | copy-start | bytes 11010052
  6.3 14.1 %collective-permute-start.2 = (bf16[64,3712]{1,0:T(8,128)(2,1)S(1)}, bf16[64,3712]{1,0:T(8,128)(2,1)S(1)}, u32[]{:S(2)}, u32[]{:S(2)}) collective-permute-start(bf16[64,3712]{1,0:T(8,128)(2,1)S(1)} %shard_map.113.refs_0_), channel_id=1, source_target_pairs={{0,8},{1,9},{2,10},{3,11},{4,12},{5,13},{6,14},{7,15},{8,0},{9,1},... | collective-permute-start | bytes 1425416 | tf_op jit(solution)/shard_map/ppermute | solution.py:32
  9.4 17.0 %collective-permute-start = (bf16[64,3712]{1,0:T(8,128)(2,1)S(1)}, bf16[64,3712]{1,0:T(8,128)(2,1)S(1)}, u32[]{:S(2)}, u32[]{:S(2)}) collective-permute-start(bf16[64,3712]{1,0:T(8,128)(2,1)S(1)} %shard_map.113.refs_0_), channel_id=1, source_target_pairs={{0,2},{1,7},{2,4},{3,1},{4,6},{5,3},{6,0},{7,5},{8,10},{9,15},{10,... | collective-permute-start | bytes 1425416 | tf_op jit(solution)/shard_map/ppermute | solution.py:36
  20.3 9.1 %collective-permute-start.1 = (bf16[64,3712]{1,0:T(8,128)(2,1)S(1)}, bf16[64,3712]{1,0:T(8,128)(2,1)S(1)}, u32[]{:S(2)}, u32[]{:S(2)}) collective-permute-start(bf16[64,3712]{1,0:T(8,128)(2,1)S(1)} %shard_map.113.refs_0_), channel_id=1, source_target_pairs={{0,7},{1,2},{2,1},{3,4},{4,3},{5,6},{6,5},{7,0},{8,15},{9,10},{10,... | collective-permute-start | bytes 1425416 | tf_op jit(solution)/shard_map/ppermute | solution.py:40
  26.4 25.6 %collective-permute-start.8 = (bf16[64,3712]{1,0:T(8,128)(2,1)S(1)}, bf16[64,3712]{1,0:T(8,128)(2,1)S(1)}, u32[]{:S(2)}, u32[]{:S(2)}) collective-permute-start(bf16[64,3712]{1,0:T(8,128)(2,1)S(1)} %shard_map.116.refs_0_), channel_id=1, source_target_pairs={{0,2},{1,7},{2,4},{3,1},{4,6},{5,3},{6,0},{7,5},{8,10},{9,15},{10,... | collective-permute-start | bytes 1425416 | tf_op jit(solution)/shard_map/ppermute | solution.py:36
  29.4 22.6 %collective-permute-start.9 = (bf16[64,3712]{1,0:T(8,128)(2,1)S(1)}, bf16[64,3712]{1,0:T(8,128)(2,1)S(1)}, u32[]{:S(2)}, u32[]{:S(2)}) collective-permute-start(bf16[64,3712]{1,0:T(8,128)(2,1)S(1)} %shard_map.116.refs_0_), channel_id=1, source_target_pairs={{0,7},{1,2},{2,1},{3,4},{4,3},{5,6},{6,5},{7,0},{8,15},{9,10},{10,... | collective-permute-start | bytes 1425416 | tf_op jit(solution)/shard_map/ppermute | solution.py:40
  30.9 21.1 %collective-permute-start.10 = (bf16[64,3712]{1,0:T(8,128)(2,1)S(1)}, bf16[64,3712]{1,0:T(8,128)(2,1)S(1)}, u32[]{:S(2)}, u32[]{:S(2)}) collective-permute-start(bf16[64,3712]{1,0:T(8,128)(2,1)S(1)} %shard_map.116.refs_0_), channel_id=1, source_target_pairs={{0,8},{1,9},{2,10},{3,11},{4,12},{5,13},{6,14},{7,15},{8,0},{9,1},... | collective-permute-start | bytes 1425416 | tf_op jit(solution)/shard_map/ppermute | solution.py:32
  33.9 50.5 %collective-permute-start.7 = (bf16[64,3712]{1,0:T(8,128)(2,1)S(1)}, bf16[64,3712]{1,0:T(8,128)(2,1)S(1)}, u32[]{:S(2)}, u32[]{:S(2)}) collective-permute-start(bf16[64,3712]{1,0:T(8,128)(2,1)S(1)} %collective-permute-done.2.refs_3_), channel_id=1, source_target_pairs={{0,7},{1,2},{2,1},{3,4},{4,3},{5,6},{6,5},{7,0},{8,15},{9,10},{10,... | collective-permute-start | bytes 1425416 | tf_op jit(solution)/shard_map/ppermute | solution.py:40
  34.5 22.2 %collective-permute-start.6 = (bf16[128,3712]{1,0:T(8,128)(2,1)S(1)}, bf16[128,3712]{1,0:T(8,128)(2,1)S(1)}, u32[]{:S(2)}, u32[]{:S(2)}) collective-permute-start(bf16[128,3712]{1,0:T(8,128)(2,1)S(1)} %pad_maximum_fusion), channel_id=1, source_target_pairs={{0,2},{1,7},{2,4},{3,1},{4,6},{5,3},{6,0},{7,5},{8,10},{9,15},{10,... | collective-permute-start | bytes 2850824 | tf_op jit(solution)/shard_map/ppermute | solution.py:36
  52.1 19.9 %collective-permute-start.12 = (bf16[128,3712]{1,0:T(8,128)(2,1)S(1)}, bf16[128,3712]{1,0:T(8,128)(2,1)S(1)}, u32[]{:S(2)}, u32[]{:S(2)}) collective-permute-start(bf16[128,3712]{1,0:T(8,128)(2,1)S(1)} %pad_maximum_fusion.1), channel_id=1, source_target_pairs={{0,2},{1,7},{2,4},{3,1},{4,6},{5,3},{6,0},{7,5},{8,10},{9,15},{10,... | collective-permute-start | bytes 2850824 | tf_op jit(solution)/shard_map/ppermute | solution.py:36
  56.8 15.3 %collective-permute-start.13 = (bf16[64,3712]{1,0:T(8,128)(2,1)S(1)}, bf16[64,3712]{1,0:T(8,128)(2,1)S(1)}, u32[]{:S(2)}, u32[]{:S(2)}) collective-permute-start(bf16[64,3712]{1,0:T(8,128)(2,1)S(1)} %collective-permute-done.10.refs_3_), channel_id=1, source_target_pairs={{0,7},{1,2},{2,1},{3,4},{4,3},{5,6},{6,5},{7,0},{8,15},{9,10},{10,... | collective-permute-start | bytes 1425416 | tf_op jit(solution)/shard_map/ppermute | solution.py:40
  63.5 13.5 %collective-permute-start.11 = (bf16[64,3712]{1,0:T(8,128)(2,1)S(1)}, bf16[64,3712]{1,0:T(8,128)(2,1)S(1)}, u32[]{:S(2)}, u32[]{:S(2)}) collective-permute-start(bf16[64,3712]{1,0:T(8,128)(2,1)S(1)} %get-tuple-element.37.refs_0_), channel_id=1, source_target_pairs={{0,8},{1,9},{2,10},{3,11},{4,12},{5,13},{6,14},{7,15},{8,0},{9,1},... | collective-permute-start | bytes 1425416 | tf_op jit(solution)/shard_map/ppermute | solution.py:32
  81.2 12.0 %collective-permute-start.14 = (bf16[64,3584]{1,0:T(8,128)(2,1)S(1)}, bf16[64,3584]{1,0:T(8,128)(2,1)S(1)}, u32[]{:S(2)}, u32[]{:S(2)}) collective-permute-start(bf16[64,3584]{1,0:T(8,128)(2,1)S(1)} %shard_map.119), channel_id=1, source_target_pairs={{0,8},{1,9},{2,10},{3,11},{4,12},{5,13},{6,14},{7,15},{8,0},{9,1},... | collective-permute-start | bytes 1376264 | tf_op jit(solution)/shard_map/ppermute | solution.py:32
  89.2 31.7 %collective-permute-start.16 = (bf16[64,3584]{1,0:T(8,128)(2,1)S(1)}, bf16[64,3584]{1,0:T(8,128)(2,1)S(1)}, u32[]{:S(2)}, u32[]{:S(2)}) collective-permute-start(bf16[64,3584]{1,0:T(8,128)(2,1)S(1)} %get-tuple-element.45), channel_id=1, source_target_pairs={{7,0},{2,1},{1,2},{4,3},{3,4},{6,5},{5,6},{0,7},{15,8},{10,9},{9,1... | collective-permute-start | bytes 1376264 | tf_op jit(solution)/shard_map/ppermute | solution.py:48
  91.9 39.0 %collective-permute-start.24 = (bf16[64,3584]{1,0:T(8,128)(2,1)S(1)}, bf16[64,3584]{1,0:T(8,128)(2,1)S(1)}, u32[]{:S(2)}, u32[]{:S(2)}) collective-permute-start(bf16[64,3584]{1,0:T(8,128)(2,1)S(1)} %get-tuple-element.55), channel_id=1, source_target_pairs={{7,0},{2,1},{1,2},{4,3},{3,4},{6,5},{5,6},{0,7},{15,8},{10,9},{9,1... | collective-permute-start | bytes 1376264 | tf_op jit(solution)/shard_map/ppermute | solution.py:48
  92.0 11.6 %collective-permute-start.21 = (bf16[64,3712]{1,0:T(8,128)(2,1)S(1)}, bf16[64,3712]{1,0:T(8,128)(2,1)S(1)}, u32[]{:S(2)}, u32[]{:S(2)}) collective-permute-start(bf16[64,3712]{1,0:T(8,128)(2,1)S(1)} %get-tuple-element.51.refs_0_), channel_id=1, source_target_pairs={{0,8},{1,9},{2,10},{3,11},{4,12},{5,13},{6,14},{7,15},{8,0},{9,1},... | collective-permute-start | bytes 1425416 | tf_op jit(solution)/shard_map/ppermute | solution.py:32
  107.8 10.4 %collective-permute-start.22 = (bf16[64,3584]{1,0:T(8,128)(2,1)S(1)}, bf16[64,3584]{1,0:T(8,128)(2,1)S(1)}, u32[]{:S(2)}, u32[]{:S(2)}) collective-permute-start(bf16[64,3584]{1,0:T(8,128)(2,1)S(1)} %shard_map.120), channel_id=1, source_target_pairs={{0,8},{1,9},{2,10},{3,11},{4,12},{5,13},{6,14},{7,15},{8,0},{9,1},... | collective-permute-start | bytes 1376264 | tf_op jit(solution)/shard_map/ppermute | solution.py:32
  110.9 15.1 %collective-permute-start.15 = (bf16[128,3584]{1,0:T(8,128)(2,1)S(1)}, bf16[128,3584]{1,0:T(8,128)(2,1)S(1)}, u32[]{:S(2)}, u32[]{:S(2)}) collective-permute-start(bf16[128,3584]{1,0:T(8,128)(2,1)S(1)} %pad_maximum_fusion.2), channel_id=1, source_target_pairs={{2,0},{7,1},{4,2},{1,3},{6,4},{3,5},{0,6},{5,7},{10,8},{15,9},{12,... | collective-permute-start | bytes 2752520 | tf_op jit(solution)/shard_map/ppermute | solution.py:44
  118.5 19.1 %collective-permute-start.23 = (bf16[128,3584]{1,0:T(8,128)(2,1)S(1)}, bf16[128,3584]{1,0:T(8,128)(2,1)S(1)}, u32[]{:S(2)}, u32[]{:S(2)}) collective-permute-start(bf16[128,3584]{1,0:T(8,128)(2,1)S(1)} %pad_maximum_fusion.3), channel_id=1, source_target_pairs={{2,0},{7,1},{4,2},{1,3},{6,4},{3,5},{0,6},{5,7},{10,8},{15,9},{12,... | collective-permute-start | bytes 2752520 | tf_op jit(solution)/shard_map/ppermute | solution.py:44
  126.2 20.9 %copy-start.5 = (bf16[1,64,3584]{2,1,0:T(8,128)(2,1)S(1)}, bf16[1,64,3584]{2,1,0:T(8,128)(2,1)}, u32[]{:S(2)}) copy-start(bf16[1,64,3584]{2,1,0:T(8,128)(2,1)} %param.10) | copy-start | bytes 1376260
  126.2 34.7 %collective-permute-start.20 = (bf16[64,3584]{1,0:T(8,128)(2,1)S(1)}, bf16[64,3584]{1,0:T(8,128)(2,1)S(1)}, u32[]{:S(2)}, u32[]{:S(2)}) collective-permute-start(bf16[64,3584]{1,0:T(8,128)(2,1)S(1)} %get-tuple-element.49), channel_id=1, source_target_pairs={{0,24},{1,25},{2,26},{3,27},{4,28},{5,29},{6,30},{7,31},{8,16},{9,... | collective-permute-start | bytes 1376264 | tf_op jit(solution)/shard_map/ppermute | solution.py:68
  127.1 14.3 %collective-permute-start.18 = (bf16[64,3584]{1,0:T(8,128)(2,1)S(1)}, bf16[64,3584]{1,0:T(8,128)(2,1)S(1)}, u32[]{:S(2)}, u32[]{:S(2)}) collective-permute-start(bf16[64,3584]{1,0:T(8,128)(2,1)S(1)} %get-tuple-element.48), channel_id=1, source_target_pairs={{7,0},{2,1},{1,2},{4,3},{3,4},{6,5},{5,6},{0,7},{15,8},{10,9},{9,1... | collective-permute-start | bytes 1376264 | tf_op jit(solution)/shard_map/ppermute | solution.py:48
  129.2 17.8 %collective-permute-start.17 = (bf16[64,3584]{1,0:T(8,128)(2,1)S(1)}, bf16[64,3584]{1,0:T(8,128)(2,1)S(1)}, u32[]{:S(2)}, u32[]{:S(2)}) collective-permute-start(bf16[64,3584]{1,0:T(8,128)(2,1)S(1)} %get-tuple-element.47), channel_id=1, source_target_pairs={{2,0},{7,1},{4,2},{1,3},{6,4},{3,5},{0,6},{5,7},{10,8},{15,9},{12,... | collective-permute-start | bytes 1376264 | tf_op jit(solution)/shard_map/ppermute | solution.py:44
  137.8 19.4 %copy-start.7 = (bf16[1,64,3584]{2,1,0:T(8,128)(2,1)S(1)}, bf16[1,64,3584]{2,1,0:T(8,128)(2,1)}, u32[]{:S(2)}) copy-start(bf16[1,64,3584]{2,1,0:T(8,128)(2,1)} %param.11) | copy-start | bytes 1376260
  137.8 14.5 %collective-permute-start.26 = (bf16[64,3584]{1,0:T(8,128)(2,1)S(1)}, bf16[64,3584]{1,0:T(8,128)(2,1)S(1)}, u32[]{:S(2)}, u32[]{:S(2)}) collective-permute-start(bf16[64,3584]{1,0:T(8,128)(2,1)S(1)} %get-tuple-element.58), channel_id=1, source_target_pairs={{7,0},{2,1},{1,2},{4,3},{3,4},{6,5},{5,6},{0,7},{15,8},{10,9},{9,1... | collective-permute-start | bytes 1376264 | tf_op jit(solution)/shard_map/ppermute | solution.py:48
  138.4 18.8 %collective-permute-start.25 = (bf16[64,3584]{1,0:T(8,128)(2,1)S(1)}, bf16[64,3584]{1,0:T(8,128)(2,1)S(1)}, u32[]{:S(2)}, u32[]{:S(2)}) collective-permute-start(bf16[64,3584]{1,0:T(8,128)(2,1)S(1)} %get-tuple-element.57), channel_id=1, source_target_pairs={{2,0},{7,1},{4,2},{1,3},{6,4},{3,5},{0,6},{5,7},{10,8},{15,9},{12,... | collective-permute-start | bytes 1376264 | tf_op jit(solution)/shard_map/ppermute | solution.py:44
  147.3 13.6 %collective-permute-start.19 = (bf16[64,3584]{1,0:T(8,128)(2,1)S(1)}, bf16[64,3584]{1,0:T(8,128)(2,1)S(1)}, u32[]{:S(2)}, u32[]{:S(2)}) collective-permute-start(bf16[64,3584]{1,0:T(8,128)(2,1)S(1)} %add_convert_fusion.6), channel_id=1, source_target_pairs={{0,16},{16,32},{32,48},{48,64},{64,80},{80,96},{96,112},{112,0},{1... | collective-permute-start | bytes 1376264 | tf_op jit(solution)/shard_map/ppermute | solution.py:58
  148.6 13.2 %collective-permute-start.28 = (bf16[64,3584]{1,0:T(8,128)(2,1)S(1)}, bf16[64,3584]{1,0:T(8,128)(2,1)S(1)}, u32[]{:S(2)}, u32[]{:S(2)}) collective-permute-start(bf16[64,3584]{1,0:T(8,128)(2,1)S(1)} %get-tuple-element.59), channel_id=1, source_target_pairs={{0,120},{1,121},{2,122},{3,123},{4,124},{5,125},{6,126},{7,127},{8... | collective-permute-start | bytes 1376264 | tf_op jit(solution)/shard_map/ppermute | solution.py:68
  157.4 14.3 %collective-permute-start.27 = (bf16[64,3584]{1,0:T(8,128)(2,1)S(1)}, bf16[64,3584]{1,0:T(8,128)(2,1)S(1)}, u32[]{:S(2)}, u32[]{:S(2)}) collective-permute-start(bf16[64,3584]{1,0:T(8,128)(2,1)S(1)} %add_convert_fusion.1), channel_id=1, source_target_pairs={{0,112},{16,0},{32,16},{48,32},{64,48},{80,64},{96,80},{112,96},{1... | collective-permute-start | bytes 1376264 | tf_op jit(solution)/shard_map/ppermute | solution.py:58
  (11 other events, 15.4 us)

commit v3 on v2

v3 whole, which is shorter than its diff:
```python
import functools

import jax
import jax.numpy as jnp
from jax import lax
from jax.experimental import pallas as pl
from jax.experimental.pallas import tpu as pltpu
from jax.sharding import PartitionSpec as P

EXTRA = 128
TILE = 256
WIDE = 1792


def place(y, z, c):
    return (y * 4 + z) * 2 + c


DEVICES = [(y, z, c) for y in range(2) for z in range(4) for c in range(2)]
CORE = [(place(y, z, c), place(y, z, 1 - c)) for y, z, c in DEVICES]
ACROSS = [(place(y, z, c), place(1 - y, z, c)) for y, z, c in DEVICES]
OUTWARD = [(place(y, z, c), place(y, (z + 1 - 2 * c) % 4, c)) for y, z, c in DEVICES]
CROSSING = [(place(y, z, c), place(y, (z - 1 + 2 * c) % 4, 1 - c)) for y, z, c in DEVICES]
OPPOSITE = [(place(y, z, c), place(y, (z + 2) % 4, c)) for y, z, c in DEVICES]


def sent(route):
    return lambda block: lax.ppermute(block, "expert", route)


def inverse(route):
    return [(target, source) for source, target in route]


core, across, opposite = sent(CORE), sent(ACROSS), sent(OPPOSITE)
outward, crossing = sent(OUTWARD), sent(CROSSING)
homeward, recrossing = sent(inverse(OUTWARD)), sent(inverse(CROSSING))


def shifted(block, distance):
    sections = lax.axis_size("section")
    route = [(i, (i + distance) % sections) for i in range(sections)]
    return lax.ppermute(block, "section", route)


def shifted_across(block, distance):
    sections, group = lax.axis_size("section"), len(DEVICES)
    route = [
        (i * group + source, (i + distance) % sections * group + target)
        for i in range(sections)
        for source, target in ACROSS
    ]
    return lax.ppermute(block, ("section", "expert"), route)


def ffn_kernel(parts, width, *refs):
    x_refs = refs[:parts]
    mine = refs[parts : parts + 3]
    other = refs[parts + 3 : parts + 6]
    out_refs = refs[parts + 6 : -2]
    x_all, hidden_all = refs[-2:]
    units = mine[2].shape[0]
    expert = lax.axis_index("expert") // 4
    shares = []
    row = 0
    for x_ref in x_refs:
        rows = x_ref.shape[0]
        x_all[row : row + rows, :] = x_ref[:, :width]
        tail = x_ref[:, width:].astype(jnp.float32)
        column = lax.broadcasted_iota(jnp.int32, tail.shape, 1)
        kept = jnp.where((column == expert) | (column == expert + 4), tail, 0.0)
        shares.append(jnp.sum(kept, axis=1, keepdims=True))
        row += rows
    share = jnp.concatenate(shares)
    for side, (gate_ref, up_ref, _) in enumerate((mine, other)):
        for start in range(0, units, TILE):
            x = x_all[...]
            columns = pl.ds(start, TILE)
            gate_value = jnp.dot(x, gate_ref[:, columns], preferred_element_type=jnp.float32)
            up_value = jnp.dot(x, up_ref[:, columns], preferred_element_type=jnp.float32)
            hidden = gate_value * (1.0 / (1.0 + jnp.exp(-gate_value))) * up_value * share
            hidden_all[:, pl.ds(side * units + start, TILE)] = hidden.astype(jnp.bfloat16)

    @pl.loop(0, width // WIDE)
    def _(n):
        columns = pl.ds(pl.multiple_of(n * WIDE, WIDE), WIDE)
        partial = jnp.dot(hidden_all[:, :units], mine[2][:, columns], preferred_element_type=jnp.float32)
        partial += jnp.dot(hidden_all[:, units:], other[2][:, columns], preferred_element_type=jnp.float32)
        row = 0
        for out_ref in out_refs:
            rows = out_ref.shape[0]
            out_ref[:, columns] = partial[row : row + rows].astype(out_ref.dtype)
            row += rows


def ffn(*blocks, weights):
    mine, other = weights[:3], weights[3:]
    units, width = mine[2].shape
    results = [block.shape[0] for block in blocks]
    total_rows = sum(block.shape[0] for block in blocks)
    vmem = pl.BlockSpec(memory_space=pltpu.VMEM)
    return pl.pallas_call(
        functools.partial(ffn_kernel, len(blocks), width),
        in_specs=[vmem] * (len(blocks) + 6),
        out_specs=[vmem] * len(results),
        out_shape=[jax.ShapeDtypeStruct((r, width), jnp.bfloat16) for r in results],
        scratch_shapes=[
            pltpu.VMEM((total_rows, width), jnp.bfloat16),
            pltpu.VMEM((total_rows, 2 * units), jnp.bfloat16),
        ],
        cost_estimate=pl.CostEstimate(
            flops=2 * total_rows * width * 2 * units * 3,
            bytes_accessed=2 * 3 * 2 * units * width,
            transcendentals=total_rows * 2 * units,
        ),
        compiler_params=pltpu.CompilerParams(vmem_limit_bytes=14 * 1024 * 1024),
    )(*blocks, *mine, *other)


def prepare_kernel(*refs):
    count = len(refs) // 2 - 1
    sources, out_ref, targets, sems = refs[:count], refs[count], refs[count + 1 : -1], refs[-1]
    copies = [pltpu.make_async_copy(sources[i], targets[i], sems.at[i]) for i in range(count)]
    for copy in copies:
        copy.start()
    for copy in copies:
        copy.wait()
    acts_ref, gain_ref, routes_ref, gates_ref = targets
    rows, width = acts_ref.shape
    widened = acts_ref[...].astype(jnp.float32)
    mean_square = jnp.mean(widened * widened, axis=-1, keepdims=True)
    normed = widened * lax.rsqrt(mean_square + 1e-06) * gain_ref[...]
    out_ref[:, :width] = normed.astype(jnp.bfloat16)
    label = lax.broadcasted_iota(jnp.int32, (EXTRA, rows), 0)
    expert = jnp.where(label < 8, label % 4, -1)
    mixing = jnp.zeros(label.shape, jnp.float32)
    for k in range(routes_ref.shape[0]):
        mixing += jnp.where(routes_ref[k : k + 1, :] == expert, gates_ref[k : k + 1, :], 0.0)
    coarse = mixing.astype(jnp.bfloat16).astype(jnp.float32)
    tail = jnp.where(label < 4, coarse, mixing - coarse)
    out_ref[:, width:] = tail.T.astype(jnp.bfloat16)


def prepare(activations, gain, routes, gate_weights):
    rows, width = activations.shape
    arrays = (activations, gain, routes.T, gate_weights.T)
    return pl.pallas_call(
        prepare_kernel,
        in_specs=[pl.BlockSpec(memory_space=pltpu.HBM)] * len(arrays),
        out_specs=pl.BlockSpec(memory_space=pltpu.VMEM),
        out_shape=jax.ShapeDtypeStruct((rows, width + EXTRA), jnp.bfloat16),
        scratch_shapes=[pltpu.VMEM(array.shape, array.dtype) for array in arrays]
        + [pltpu.SemaphoreType.DMA((len(arrays),))],
        cost_estimate=pl.CostEstimate(flops=6 * rows * width, bytes_accessed=4 * rows * width, transcendentals=rows),
        compiler_params=pltpu.CompilerParams(vmem_limit_bytes=60 * 1024 * 1024),
    )(*arrays)


def after(block, *earlier):
    return lax.optimization_barrier((block, *[e[0] if isinstance(e, (tuple, list)) else e for e in earlier]))[0]


def add(*terms):
    total = terms[0].astype(jnp.float32)
    for term in terms[1:]:
        total = total + term.astype(jnp.float32)
    return total.astype(jnp.bfloat16)


def body(
    up_acts,
    down_acts,
    norm_gain,
    up_routes,
    down_routes,
    up_gates,
    down_gates,
    gate_weight,
    up_weight,
    down_weight,
):
    up_acts, up_routes, up_gates = up_acts[0], up_routes[0], up_gates[0]
    down_acts, down_routes, down_gates = down_acts[0], down_routes[0], down_gates[0]
    gate_weight, up_weight, down_weight = gate_weight[0], up_weight[0], down_weight[0]
    down_rows = prepare(down_acts, norm_gain, down_routes, down_gates)
    up_rows = prepare(after(up_acts, down_rows), norm_gain, up_routes, up_gates)
    other_gate = core(after(gate_weight, up_rows))
    other_down = core(after(down_weight, up_rows))
    up_near = outward(up_rows)
    up_far = outward(up_near)
    down_near = outward(down_rows)
    other_up = core(after(up_weight, other_gate, other_down, down_near))
    up_facing = across(after(up_rows, other_down, down_near))
    down_facing = across(after(down_rows, up_rows, down_near))
    down_facing_beside = crossing(after(down_facing, other_up))
    down_far = outward(down_near)
    up_facing_beside = crossing(after(up_facing, other_up, down_far, down_facing))
    up_facing_far = across(after(up_far, other_up, down_far, down_facing))
    down_facing_near = outward(after(down_facing, other_gate, up_near, other_down, down_near))
    up_facing_near = outward(after(up_facing, down_facing_near, up_far, other_up, down_far))
    down_beside = crossing(after(down_rows, up_facing_far, up_facing_near))
    down_facing_far = across(after(down_far, down_facing, other_gate, other_down, other_up))
    run = functools.partial(ffn, weights=(gate_weight, up_weight, down_weight, other_gate, other_up, other_down))
    down_distant = run(down_far, down_facing_near, down_facing_beside)
    up_beside = crossing(after(up_rows, up_facing_beside, down_distant, down_facing_far))
    down_last = run(after(down_facing_far, up_facing_beside, down_distant))
    up_distant = run(after(up_far, down_last, up_facing_far), up_facing_near, up_facing_beside)
    up_last = run(after(up_facing_far, up_beside, up_distant))
    up_last_back = across(after(up_last, down_beside)[0])
    down_last_back = across(after(down_last, up_facing_far, up_facing_near)[0])
    down_facing_beside_back = recrossing(after(down_distant, down_facing_far)[2])
    up_facing_beside_back = recrossing(after(up_distant, down_facing_beside_back)[2])
    up_facing_near_back = homeward(after(up_distant, up_beside, down_facing_beside_back)[1])
    down_close = run(after(down_rows, up_facing_beside_back, down_last_back, up_last), down_near, down_beside, down_facing)
    up_close = run(after(up_rows, down_close), up_near, up_beside, up_facing)
    down_far_back = opposite(add(after(down_distant, up_last, down_beside)[0], down_last_back))
    up_facing_out = shifted_across(add(after(up_close, down_far_back, up_last_back)[3], up_facing_near_back, up_facing_beside_back), 1)
    up_far_back = homeward(add(after(up_distant, up_close, down_far_back)[0], up_last_back))
    down_near_back = homeward(after(down_close, up_facing_near_back)[1])
    down_beside_back = recrossing(down_close[2])
    up_beside_back = recrossing(after(up_close, down_beside_back, down_far_back, up_last_back)[2])
    up_near_back = homeward(add(after(up_close, down_near_back, down_beside_back)[1], up_far_back))
    down_facing_near_back = homeward(after(down_distant, down_beside_back, up_close, down_far_back, up_last_back)[1])
    down_facing_out = shifted_across(add(after(down_close, up_facing_out, up_beside_back, down_near_back)[3], down_facing_near_back, down_facing_beside_back), -1)
    down_layer = shifted(add(after(down_acts, up_close, up_last_back), down_close[0], down_near_back, down_beside_back, down_far_back), -1)
    up_layer = shifted(add(after(up_acts, down_layer, down_facing_near_back, up_facing_out), up_close[0], up_near_back, up_beside_back), 1)
    down_next = add(down_layer, down_facing_out)
    up_next = add(after(up_layer, down_next), up_facing_out)
    return (up_next[None], down_next[None])


def solution(mesh):
    return jax.shard_map(
        body,
        mesh=mesh,
        in_specs=(
            P("section", "expert", None),
            P("section", "expert", None),
            P("section", None),
            P("section", "expert", None),
            P("section", "expert", None),
            P("section", "expert", None),
            P("section", "expert", None),
            P("section", None, "expert"),
            P("section", None, "expert"),
            P("section", "expert", None),
        ),
        out_specs=(P("section", "expert", None), P("section", "expert", None)),
        check_vma=False,
    )
```

time: 174 us -> 148 us (0.85)
  waiting for transfers between devices: 70.2 us -> 51.5 us
  starting transfers between devices: 56.2 us -> 51.3 us
  local copies, waits for them, and re-layouts: 10.4 us -> 6.14 us
  Pallas kernels: 31.7 us -> 34.7 us
    ppermute x25 -> x29, waiting for transfers between devices: 60.2 us -> 39.1 us  [sent(): return lambda block: lax.ppermute(block, 'expert', route)]
    ppermute x2, waiting for transfers between devices: 0.01 us -> 7.1 us  [shifted_across(): return lax.ppermute(block, ('section', 'expert'), route)]
    ppermute x2, waiting for transfers between devices: 10 us -> 5.3 us  [shifted(): return lax.ppermute(block, 'section', route)]
    unnamed x28 -> x16, local copies, waits for them, and re-layouts: 10.3 us -> 6.14 us
    pallas_call x2, Pallas kernels: 1.06 us -> 4.11 us  [prepare(): pl.pallas_call(prepare_kernel, in_specs=[pl.BlockSpec(memory_space=pltpu....]
    ppermute x25 -> x29, starting transfers between devices: 46.9 us -> 44.5 us  [sent(): return lambda block: lax.ppermute(block, 'expert', route)]
  transfers between devices with their start and end apart: 29 -> 33, of which waited for: 13 -> 15; matrix products, arithmetic and copies ran while one was open for 1% -> 1% of each run, Pallas kernels for 18% -> 21%
where the time goes in v3:
time: 148 us; the launch traced here: 147 us
  waiting for transfers between devices  51.5 us (35%)
  starting transfers between devices  51.3 us (35%)
  Pallas kernels  34.7 us (23%)
  local copies, waits for them, and re-layouts  6.14 us (4%)
  other arithmetic  2.91 us (2%)
    ppermute x29, starting transfers between devices, sent(): return lambda block: lax.ppermute(block, 'expert', route)  44.5 us
    ppermute x29, waiting for transfers between devices, sent(): return lambda block: lax.ppermute(block, 'expert', route)  39.1 us
    pallas_call x6, Pallas kernels, ffn(): pl.pallas_call(functools.partial(ffn_kernel, len(blocks), width), in_spec...  30.6 us
    ppermute x2, waiting for transfers between devices, shifted_across(): return lax.ppermute(block, ('section', 'expert'), route)  7.1 us
    unnamed x16, local copies, waits for them, and re-layouts  6.14 us
    ppermute x2, waiting for transfers between devices, shifted(): return lax.ppermute(block, 'section', route)  5.3 us
    pallas_call x2, Pallas kernels, prepare(): pl.pallas_call(prepare_kernel, in_specs=[pl.BlockSpec(memory_space=pltpu....  4.11 us
    ppermute x2, starting transfers between devices, shifted_across(): return lax.ppermute(block, ('section', 'expert'), route)  3.88 us
  transfers between devices with their start and end apart: 33, of which 15 were waited for; matrix products, arithmetic and copies ran while one was open for 1% of the time, Pallas kernels for 21%

profile of v3, /device:TPU:1, one launch (start us, length us, event | category | flops | bytes accessed | tf_op | source)
XLA Modules:
  0.0 147.5 jit_solution(17090571853315785714)
XLA Ops:
  0.6 2.0 %shard_map.113.refs_0_ = bf16[64,3712]{1,0:T(8,128)(2,1)} custom-call(bf16[64,3584]{1,0:T(8,128)(2,1)} %bitcast.41, f32[1,3584]{1,0:T(1,128)} %refs_1_.3, s32[2,64]{1,0:T(2,128)} %bitcast.46, f32[2,64]{1,0:T(2,128)} %bitcast.47), custom_call_target="tpu_custom_call" | custom-call | flops 1376256 | bytes 917504 | tf_op jit(solution)/shard_map/pallas_call | solution.py:147
  2.7 2.1 %shard_map.114.refs_0_ = bf16[64,3712]{1,0:T(8,128)(2,1)} custom-call(bf16[64,3584]{1,0:T(8,128)(2,1)} %bitcast.43, f32[1,3584]{1,0:T(1,128)} %refs_1_.3, s32[2,64]{1,0:T(2,128)} %bitcast.48, f32[2,64]{1,0:T(2,128)} %bitcast.49), custom_call_target="tpu_custom_call" | custom-call | flops 1376256 | bytes 917504 | tf_op jit(solution)/shard_map/pallas_call | solution.py:147
  6.3 3.8 %collective-permute-start.2 = (bf16[64,3712]{1,0:T(8,128)(2,1)}, bf16[64,3712]{1,0:T(8,128)(2,1)S(1)}, u32[]{:S(2)}, u32[]{:S(2)}) collective-permute-start(bf16[64,3712]{1,0:T(8,128)(2,1)} %shard_map.113.refs_0_), channel_id=1, source_target_pairs={{0,2},{1,7},{2,4},{3,1},{4,6},{5,3},{6,0},{7,5},{8,10},{9,15},{10,... | collective-permute-start | bytes 1425416 | tf_op jit(solution)/shard_map/ppermute | solution.py:28
  10.2 5.9 %collective-permute-done.2.refs_1_ = bf16[64,3712]{1,0:T(8,128)(2,1)S(1)} collective-permute-done((bf16[64,3712]{1,0:T(8,128)(2,1)}, bf16[64,3712]{1,0:T(8,128)(2,1)S(1)}, u32[]{:S(2)}, u32[]{:S(2)}) %collective-permute-start.2) | collective-permute-done | bytes 475168 | tf_op jit(solution)/shard_map/ppermute | solution.py:28
  18.1 3.8 %collective-permute-start = (bf16[64,3712]{1,0:T(8,128)(2,1)}, bf16[64,3712]{1,0:T(8,128)(2,1)S(1)}, u32[]{:S(2)}, u32[]{:S(2)}) collective-permute-start(bf16[64,3712]{1,0:T(8,128)(2,1)} %shard_map.114.refs_0_), channel_id=1, source_target_pairs={{0,2},{1,7},{2,4},{3,1},{4,6},{5,3},{6,0},{7,5},{8,10},{9,15},{10,... | collective-permute-start | bytes 1425416 | tf_op jit(solution)/shard_map/ppermute | solution.py:28
  22.0 2.9 %collective-permute-start.4 = (bf16[64,3712]{1,0:T(8,128)(2,1)}, bf16[64,3712]{1,0:T(8,128)(2,1)S(1)}, u32[]{:S(2)}, u32[]{:S(2)}) collective-permute-start(bf16[64,3712]{1,0:T(8,128)(2,1)} %shard_map.113.refs_0_), channel_id=1, source_target_pairs={{0,8},{1,9},{2,10},{3,11},{4,12},{5,13},{6,14},{7,15},{8,0},{9,1},... | collective-permute-start | bytes 1425416 | tf_op jit(solution)/shard_map/ppermute | solution.py:28
  25.1 2.8 %collective-permute-done.refs_1_ = bf16[64,3712]{1,0:T(8,128)(2,1)S(1)} collective-permute-done((bf16[64,3712]{1,0:T(8,128)(2,1)}, bf16[64,3712]{1,0:T(8,128)(2,1)S(1)}, u32[]{:S(2)}, u32[]{:S(2)}) %collective-permute-start) | collective-permute-done | bytes 475168 | tf_op jit(solution)/shard_map/ppermute | solution.py:28
  27.9 3.3 %collective-permute-start.1 = (bf16[64,3712]{1,0:T(8,128)(2,1)S(1)}, bf16[64,3712]{1,0:T(8,128)(2,1)S(1)}, u32[]{:S(2)}, u32[]{:S(2)}) collective-permute-start(bf16[64,3712]{1,0:T(8,128)(2,1)S(1)} %collective-permute-done.refs_1_), channel_id=1, source_target_pairs={{0,2},{1,7},{2,4},{3,1},{4,6},{5,3},{6,0},{7,5},{8,10},{9,15},{10,... | collective-permute-start | bytes 1425416 | tf_op jit(solution)/shard_map/ppermute | solution.py:28
  31.2 5.4 %collective-permute-done.4.refs_3_ = bf16[64,3712]{1,0:T(8,128)(2,1)S(1)} collective-permute-done((bf16[64,3712]{1,0:T(8,128)(2,1)}, bf16[64,3712]{1,0:T(8,128)(2,1)S(1)}, u32[]{:S(2)}, u32[]{:S(2)}) %collective-permute-start.4) | collective-permute-done | bytes 475168 | tf_op jit(solution)/shard_map/ppermute | solution.py:28
  36.6 2.3 %collective-permute-start.12 = (bf16[64,3712]{1,0:T(8,128)(2,1)S(1)}, bf16[64,3712]{1,0:T(8,128)(2,1)S(1)}, u32[]{:S(2)}, u32[]{:S(2)}) collective-permute-start(bf16[64,3712]{1,0:T(8,128)(2,1)S(1)} %collective-permute-done.4.refs_3_), channel_id=1, source_target_pairs={{0,7},{1,2},{2,1},{3,4},{4,3},{5,6},{6,5},{7,0},{8,15},{9,10},{10,... | collective-permute-start | bytes 1425416 | tf_op jit(solution)/shard_map/ppermute | solution.py:28
  38.9 2.9 %collective-permute-start.8 = (bf16[64,3712]{1,0:T(8,128)(2,1)S(1)}, bf16[64,3712]{1,0:T(8,128)(2,1)S(1)}, u32[]{:S(2)}, u32[]{:S(2)}) collective-permute-start(bf16[64,3712]{1,0:T(8,128)(2,1)S(1)} %collective-permute-done.3.refs_0_), channel_id=1, source_target_pairs={{0,8},{1,9},{2,10},{3,11},{4,12},{5,13},{6,14},{7,15},{8,0},{9,1},... | collective-permute-start | bytes 1425416 | tf_op jit(solution)/shard_map/ppermute | solution.py:28
  41.9 4.9 %collective-permute-done.9.refs_3_ = bf16[64,3712]{1,0:T(8,128)(2,1)S(1)} collective-permute-done((bf16[64,3712]{1,0:T(8,128)(2,1)}, bf16[64,3712]{1,0:T(8,128)(2,1)S(1)}, u32[]{:S(2)}, u32[]{:S(2)}) %collective-permute-start.9) | collective-permute-done | bytes 475168 | tf_op jit(solution)/shard_map/ppermute | solution.py:28
  48.3 2.9 %collective-permute-start.13 = (bf16[64,3712]{1,0:T(8,128)(2,1)S(1)}, bf16[64,3712]{1,0:T(8,128)(2,1)S(1)}, u32[]{:S(2)}, u32[]{:S(2)}) collective-permute-start(bf16[64,3712]{1,0:T(8,128)(2,1)S(1)} %collective-permute-done.1.refs_0_), channel_id=1, source_target_pairs={{0,8},{1,9},{2,10},{3,11},{4,12},{5,13},{6,14},{7,15},{8,0},{9,1},... | collective-permute-start | bytes 1425416 | tf_op jit(solution)/shard_map/ppermute | solution.py:28
  51.2 2.6 %collective-permute-start.14 = (bf16[64,3712]{1,0:T(8,128)(2,1)S(1)}, bf16[64,3712]{1,0:T(8,128)(2,1)S(1)}, u32[]{:S(2)}, u32[]{:S(2)}) collective-permute-start(bf16[64,3712]{1,0:T(8,128)(2,1)S(1)} %collective-permute-done.9.refs_3_), channel_id=1, source_target_pairs={{0,2},{1,7},{2,4},{3,1},{4,6},{5,3},{6,0},{7,5},{8,10},{9,15},{10,... | collective-permute-start | bytes 1425416 | tf_op jit(solution)/shard_map/ppermute | solution.py:28
  53.8 2.0 %copy-done = bf16[1,3584,512]{2,1,0:T(8,128)(2,1)S(1)} copy-done((bf16[1,3584,512]{2,1,0:T(8,128)(2,1)S(1)}, bf16[1,3584,512]{2,1,0:T(8,128)(2,1)}, u32[]{:S(2)}) %copy-start) | copy-done | bytes 3670040
  55.8 2.0 %copy-done.2 = bf16[1,3584,512]{2,1,0:T(8,128)(2,1)S(1)} copy-done((bf16[1,3584,512]{2,1,0:T(8,128)(2,1)S(1)}, bf16[1,3584,512]{2,1,0:T(8,128)(2,1)}, u32[]{:S(2)}) %copy-start.2) | copy-done | bytes 3670040
  59.9 4.9 %shard_map.115 = (bf16[64,3584]{1,0:T(8,128)(2,1)S(1)}, bf16[64,3584]{1,0:T(8,128)(2,1)S(1)}, bf16[64,3584]{1,0:T(8,128)(2,1)S(1)}) custom-call(bf16[64,3712]{1,0:T(8,128)(2,1)S(1)} %collective-permute-done.3.refs_0_, bf16[64,3712]{1,0:T(8,128)(2,1)S(1)} %collective-permute-done.11.refs_1_, bf16[64,3712]{1,0:T(8,128)(2,1)S(1)} %collective-permute-done.12.refs_2_, ...), custom_call_target="tpu_custom_call" | custom-call | flops 4227858432 | bytes 22020096 | tf_op jit(solution)/shard_map/pallas_call | solution.py:102
  66.7 4.2 %shard_map.116 = bf16[64,3584]{1,0:T(8,128)(2,1)S(1)} custom-call(bf16[64,3712]{1,0:T(8,128)(2,1)S(1)} %collective-permute-done.8.refs_0_, bf16[3584,512]{1,0:T(8,128)(2,1)S(1)} %bitcast.22, bf16[3584,512]{1,0:T(8,128)(2,1)S(1)} %bitcast.29, bf16[512,3584]{1,0:T(8,128)(2,1)S(1)} %bitcast.36, ...), custom_call_target="tpu_custom_call" | custom-call | flops 1409286144 | bytes 22020096 | tf_op jit(solution)/shard_map/pallas_call | solution.py:102
  72.8 4.9 %shard_map.117 = (bf16[64,3584]{1,0:T(8,128)(2,1)S(1)}, bf16[64,3584]{1,0:T(8,128)(2,1)S(1)}, bf16[64,3584]{1,0:T(8,128)(2,1)S(1)}) custom-call(bf16[64,3712]{1,0:T(8,128)(2,1)S(1)} %collective-permute-done.1.refs_0_, bf16[64,3712]{1,0:T(8,128)(2,1)S(1)} %collective-permute-done.14.refs_1_, bf16[64,3712]{1,0:T(8,128)(2,1)S(1)} %collective-permute-done.10.refs_2_, ...), custom_call_target="tpu_custom_call" | custom-call | flops 4227858432 | bytes 22020096 | tf_op jit(solution)/shard_map/pallas_call | solution.py:102
  78.8 4.2 %shard_map.118 = bf16[64,3584]{1,0:T(8,128)(2,1)S(1)} custom-call(bf16[64,3712]{1,0:T(8,128)(2,1)S(1)} %collective-permute-done.13.refs_0_, bf16[3584,512]{1,0:T(8,128)(2,1)S(1)} %bitcast.24, bf16[3584,512]{1,0:T(8,128)(2,1)S(1)} %bitcast.31, bf16[512,3584]{1,0:T(8,128)(2,1)S(1)} %bitcast.38, ...), custom_call_target="tpu_custom_call" | custom-call | flops 1409286144 | bytes 22020096 | tf_op jit(solution)/shard_map/pallas_call | solution.py:102
  83.3 2.5 %collective-permute-start.20 = (bf16[64,3584]{1,0:T(8,128)(2,1)S(1)}, bf16[64,3584]{1,0:T(8,128)(2,1)S(1)}, u32[]{:S(2)}, u32[]{:S(2)}) collective-permute-start(bf16[64,3584]{1,0:T(8,128)(2,1)S(1)} %shard_map.118), channel_id=1, source_target_pairs={{0,8},{1,9},{2,10},{3,11},{4,12},{5,13},{6,14},{7,15},{8,0},{9,1},... | collective-permute-start | bytes 1376264 | tf_op jit(solution)/shard_map/ppermute | solution.py:28
  85.9 2.8 %collective-permute-start.24 = (bf16[64,3584]{1,0:T(8,128)(2,1)S(1)}, bf16[64,3584]{1,0:T(8,128)(2,1)S(1)}, u32[]{:S(2)}, u32[]{:S(2)}) collective-permute-start(bf16[64,3584]{1,0:T(8,128)(2,1)S(1)} %add_convert_fusion.8), channel_id=1, source_target_pairs={{0,4},{1,5},{2,6},{3,7},{4,0},{5,1},{6,2},{7,3},{8,12},{9,13},{10,... | collective-permute-start | bytes 1376264 | tf_op jit(solution)/shard_map/ppermute | solution.py:28
  88.7 6.3 %shard_map.119 = (bf16[64,3584]{1,0:T(8,128)(2,1)S(1)}, bf16[64,3584]{1,0:T(8,128)(2,1)S(1)}, bf16[64,3584]{1,0:T(8,128)(2,1)S(1)}, bf16[64,3584]{1,0:T(8,128)(2,1)S(1)}) custom-call(bf16[64,3712]{1,0:T(8,128)(2,1)S(1)} %copy-done.5, bf16[64,3712]{1,0:T(8,128)(2,1)S(1)} %collective-permute-done.2.refs_1_, ...), custom_call_target="tpu_custom_call" | custom-call | flops 5637144576 | bytes 22020096 | tf_op jit(solution)/shard_map/pallas_call | solution.py:102
  96.3 6.3 %shard_map.120 = (bf16[64,3584]{1,0:T(8,128)(2,1)S(1)}, bf16[64,3584]{1,0:T(8,128)(2,1)S(1)}, bf16[64,3584]{1,0:T(8,128)(2,1)S(1)}, bf16[64,3584]{1,0:T(8,128)(2,1)S(1)}) custom-call(bf16[64,3712]{1,0:T(8,128)(2,1)S(1)} %copy-done.4, bf16[64,3712]{1,0:T(8,128)(2,1)S(1)} %collective-permute-done.refs_1_, ...), custom_call_target="tpu_custom_call" | custom-call | flops 5637144576 | bytes 22020096 | tf_op jit(solution)/shard_map/pallas_call | solution.py:102
  104.8 2.4 %collective-permute-start.28 = (bf16[64,3584]{1,0:T(8,128)(2,1)S(1)}, bf16[64,3584]{1,0:T(8,128)(2,1)S(1)}, u32[]{:S(2)}, u32[]{:S(2)}) collective-permute-start(bf16[64,3584]{1,0:T(8,128)(2,1)S(1)} %add_convert_fusion.5), channel_id=1, source_target_pairs={{2,0},{7,1},{4,2},{1,3},{6,4},{3,5},{0,6},{5,7},{10,8},{15,9},{12,... | collective-permute-start | bytes 1376264 | tf_op jit(solution)/shard_map/ppermute | solution.py:28
  110.2 2.9 %collective-permute-done.22 = bf16[64,3584]{1,0:T(8,128)(2,1)S(1)} collective-permute-done((bf16[64,3584]{1,0:T(8,128)(2,1)S(1)}, bf16[64,3584]{1,0:T(8,128)(2,1)S(1)}, u32[]{:S(2)}, u32[]{:S(2)}) %collective-permute-start.22) | collective-permute-done | bytes 458784 | tf_op jit(solution)/shard_map/ppermute | solution.py:28
  113.4 2.4 %collective-permute-start.25 = (bf16[64,3584]{1,0:T(8,128)(2,1)S(1)}, bf16[64,3584]{1,0:T(8,128)(2,1)S(1)}, u32[]{:S(2)}, u32[]{:S(2)}) collective-permute-start(bf16[64,3584]{1,0:T(8,128)(2,1)S(1)} %add_convert_fusion.7), channel_id=1, source_target_pairs={{0,112},{16,0},{32,16},{48,32},{64,48},{80,64},{96,80},{112,96},{1... | collective-permute-start | bytes 1376264 | tf_op jit(solution)/shard_map/ppermute | solution.py:43
  115.8 2.3 %collective-permute-done.28 = bf16[64,3584]{1,0:T(8,128)(2,1)S(1)} collective-permute-done((bf16[64,3584]{1,0:T(8,128)(2,1)S(1)}, bf16[64,3584]{1,0:T(8,128)(2,1)S(1)}, u32[]{:S(2)}, u32[]{:S(2)}) %collective-permute-start.28) | collective-permute-done | bytes 458784 | tf_op jit(solution)/shard_map/ppermute | solution.py:28
  118.9 8.7 %collective-permute-done.30 = bf16[64,3584]{1,0:T(8,128)(2,1)S(1)} collective-permute-done((bf16[64,3584]{1,0:T(8,128)(2,1)S(1)}, bf16[64,3584]{1,0:T(8,128)(2,1)S(1)}, u32[]{:S(2)}, u32[]{:S(2)}) %collective-permute-start.30) | collective-permute-done | bytes 458784 | tf_op jit(solution)/shard_map/ppermute | solution.py:28
  127.7 3.0 %collective-permute-start.32 = (bf16[64,3584]{1,0:T(8,128)(2,1)S(1)}, bf16[64,3584]{1,0:T(8,128)(2,1)S(1)}, u32[]{:S(2)}, u32[]{:S(2)}) collective-permute-start(bf16[64,3584]{1,0:T(8,128)(2,1)S(1)} %add_convert_fusion.2), channel_id=1, source_target_pairs={{0,120},{1,121},{2,122},{3,123},{4,124},{5,125},{6,126},{7,127},{8... | collective-permute-start | bytes 1376264 | tf_op jit(solution)/shard_map/ppermute | solution.py:53
  133.3 7.1 %collective-permute-done.32 = bf16[64,3584]{1,0:T(8,128)(2,1)S(1)} collective-permute-done((bf16[64,3584]{1,0:T(8,128)(2,1)S(1)}, bf16[64,3584]{1,0:T(8,128)(2,1)S(1)}, u32[]{:S(2)}, u32[]{:S(2)}) %collective-permute-start.32) | collective-permute-done | bytes 458784 | tf_op jit(solution)/shard_map/ppermute | solution.py:53
  141.3 5.3 %collective-permute-done.31 = bf16[64,3584]{1,0:T(8,128)(2,1)S(1)} collective-permute-done((bf16[64,3584]{1,0:T(8,128)(2,1)S(1)}, bf16[64,3584]{1,0:T(8,128)(2,1)S(1)}, u32[]{:S(2)}, u32[]{:S(2)}) %collective-permute-start.31) | collective-permute-done | bytes 458784 | tf_op jit(solution)/shard_map/ppermute | solution.py:43
  (67 shorter events, 24.7 us)
Async XLA Ops:
  4.8 11.4 %collective-permute-start.5 = (bf16[3584,512]{1,0:T(8,128)(2,1)}, bf16[3584,512]{1,0:T(8,128)(2,1)S(1)}, u32[]{:S(2)}, u32[]{:S(2)}) collective-permute-start(bf16[3584,512]{1,0:T(8,128)(2,1)} %bitcast.20), channel_id=1, source_target_pairs={{0,1},{1,0},{2,3},{3,2},{4,5},{5,4},{6,7},{7,6},{8,9},{9,8},{10,11... | collective-permute-start | bytes 11010056 | tf_op jit(solution)/shard_map/ppermute | solution.py:28
  6.3 11.5 %collective-permute-start.6 = (bf16[512,3584]{1,0:T(8,128)(2,1)}, bf16[512,3584]{1,0:T(8,128)(2,1)S(1)}, u32[]{:S(2)}, u32[]{:S(2)}) collective-permute-start(bf16[512,3584]{1,0:T(8,128)(2,1)} %bitcast.34), channel_id=1, source_target_pairs={{0,1},{1,0},{2,3},{3,2},{4,5},{5,4},{6,7},{7,6},{8,9},{9,8},{10,11... | collective-permute-start | bytes 11010056 | tf_op jit(solution)/shard_map/ppermute | solution.py:28
  17.7 18.9 %collective-permute-start.7 = (bf16[3584,512]{1,0:T(8,128)(2,1)}, bf16[3584,512]{1,0:T(8,128)(2,1)S(1)}, u32[]{:S(2)}, u32[]{:S(2)}) collective-permute-start(bf16[3584,512]{1,0:T(8,128)(2,1)} %bitcast.27), channel_id=1, source_target_pairs={{0,1},{1,0},{2,3},{3,2},{4,5},{5,4},{6,7},{7,6},{8,9},{9,8},{10,11... | collective-permute-start | bytes 11010056 | tf_op jit(solution)/shard_map/ppermute | solution.py:28
  18.1 9.8 %collective-permute-start = (bf16[64,3712]{1,0:T(8,128)(2,1)}, bf16[64,3712]{1,0:T(8,128)(2,1)S(1)}, u32[]{:S(2)}, u32[]{:S(2)}) collective-permute-start(bf16[64,3712]{1,0:T(8,128)(2,1)} %shard_map.114.refs_0_), channel_id=1, source_target_pairs={{0,2},{1,7},{2,4},{3,1},{4,6},{5,3},{6,0},{7,5},{8,10},{9,15},{10,... | collective-permute-start | bytes 1425416 | tf_op jit(solution)/shard_map/ppermute | solution.py:28
  22.0 14.6 %collective-permute-start.4 = (bf16[64,3712]{1,0:T(8,128)(2,1)}, bf16[64,3712]{1,0:T(8,128)(2,1)S(1)}, u32[]{:S(2)}, u32[]{:S(2)}) collective-permute-start(bf16[64,3712]{1,0:T(8,128)(2,1)} %shard_map.113.refs_0_), channel_id=1, source_target_pairs={{0,8},{1,9},{2,10},{3,11},{4,12},{5,13},{6,14},{7,15},{8,0},{9,1},... | collective-permute-start | bytes 1425416 | tf_op jit(solution)/shard_map/ppermute | solution.py:28
  24.9 14.1 %collective-permute-start.3 = (bf16[64,3712]{1,0:T(8,128)(2,1)S(1)}, bf16[64,3712]{1,0:T(8,128)(2,1)S(1)}, u32[]{:S(2)}, u32[]{:S(2)}) collective-permute-start(bf16[64,3712]{1,0:T(8,128)(2,1)S(1)} %collective-permute-done.2.refs_1_), channel_id=1, source_target_pairs={{0,2},{1,7},{2,4},{3,1},{4,6},{5,3},{6,0},{7,5},{8,10},{9,15},{10,... | collective-permute-start | bytes 1425416 | tf_op jit(solution)/shard_map/ppermute | solution.py:28
  25.0 21.8 %collective-permute-start.9 = (bf16[64,3712]{1,0:T(8,128)(2,1)}, bf16[64,3712]{1,0:T(8,128)(2,1)S(1)}, u32[]{:S(2)}, u32[]{:S(2)}) collective-permute-start(bf16[64,3712]{1,0:T(8,128)(2,1)} %shard_map.114.refs_0_), channel_id=1, source_target_pairs={{0,8},{1,9},{2,10},{3,11},{4,12},{5,13},{6,14},{7,15},{8,0},{9,1},... | collective-permute-start | bytes 1425416 | tf_op jit(solution)/shard_map/ppermute | solution.py:28
  27.9 18.9 %collective-permute-start.1 = (bf16[64,3712]{1,0:T(8,128)(2,1)S(1)}, bf16[64,3712]{1,0:T(8,128)(2,1)S(1)}, u32[]{:S(2)}, u32[]{:S(2)}) collective-permute-start(bf16[64,3712]{1,0:T(8,128)(2,1)S(1)} %collective-permute-done.refs_1_), channel_id=1, source_target_pairs={{0,2},{1,7},{2,4},{3,1},{4,6},{5,3},{6,0},{7,5},{8,10},{9,15},{10,... | collective-permute-start | bytes 1425416 | tf_op jit(solution)/shard_map/ppermute | solution.py:28
  36.6 11.7 %collective-permute-start.11 = (bf16[64,3712]{1,0:T(8,128)(2,1)S(1)}, bf16[64,3712]{1,0:T(8,128)(2,1)S(1)}, u32[]{:S(2)}, u32[]{:S(2)}) collective-permute-start(bf16[64,3712]{1,0:T(8,128)(2,1)S(1)} %collective-permute-done.4.refs_3_), channel_id=1, source_target_pairs={{0,2},{1,7},{2,4},{3,1},{4,6},{5,3},{6,0},{7,5},{8,10},{9,15},{10,... | collective-permute-start | bytes 1425416 | tf_op jit(solution)/shard_map/ppermute | solution.py:28
  36.6 17.2 %collective-permute-start.12 = (bf16[64,3712]{1,0:T(8,128)(2,1)S(1)}, bf16[64,3712]{1,0:T(8,128)(2,1)S(1)}, u32[]{:S(2)}, u32[]{:S(2)}) collective-permute-start(bf16[64,3712]{1,0:T(8,128)(2,1)S(1)} %collective-permute-done.4.refs_3_), channel_id=1, source_target_pairs={{0,7},{1,2},{2,1},{3,4},{4,3},{5,6},{6,5},{7,0},{8,15},{9,10},{10,... | collective-permute-start | bytes 1425416 | tf_op jit(solution)/shard_map/ppermute | solution.py:28
  38.9 25.8 %collective-permute-start.8 = (bf16[64,3712]{1,0:T(8,128)(2,1)S(1)}, bf16[64,3712]{1,0:T(8,128)(2,1)S(1)}, u32[]{:S(2)}, u32[]{:S(2)}) collective-permute-start(bf16[64,3712]{1,0:T(8,128)(2,1)S(1)} %collective-permute-done.3.refs_0_), channel_id=1, source_target_pairs={{0,8},{1,9},{2,10},{3,11},{4,12},{5,13},{6,14},{7,15},{8,0},{9,1},... | collective-permute-start | bytes 1425416 | tf_op jit(solution)/shard_map/ppermute | solution.py:28
  46.8 18.0 %collective-permute-start.10 = (bf16[64,3712]{1,0:T(8,128)(2,1)S(1)}, bf16[64,3712]{1,0:T(8,128)(2,1)S(1)}, u32[]{:S(2)}, u32[]{:S(2)}) collective-permute-start(bf16[64,3712]{1,0:T(8,128)(2,1)S(1)} %collective-permute-done.9.refs_3_), channel_id=1, source_target_pairs={{0,7},{1,2},{2,1},{3,4},{4,3},{5,6},{6,5},{7,0},{8,15},{9,10},{10,... | collective-permute-start | bytes 1425416 | tf_op jit(solution)/shard_map/ppermute | solution.py:28
  48.3 22.5 %collective-permute-start.13 = (bf16[64,3712]{1,0:T(8,128)(2,1)S(1)}, bf16[64,3712]{1,0:T(8,128)(2,1)S(1)}, u32[]{:S(2)}, u32[]{:S(2)}) collective-permute-start(bf16[64,3712]{1,0:T(8,128)(2,1)S(1)} %collective-permute-done.1.refs_0_), channel_id=1, source_target_pairs={{0,8},{1,9},{2,10},{3,11},{4,12},{5,13},{6,14},{7,15},{8,0},{9,1},... | collective-permute-start | bytes 1425416 | tf_op jit(solution)/shard_map/ppermute | solution.py:28
  51.2 19.6 %collective-permute-start.14 = (bf16[64,3712]{1,0:T(8,128)(2,1)S(1)}, bf16[64,3712]{1,0:T(8,128)(2,1)S(1)}, u32[]{:S(2)}, u32[]{:S(2)}) collective-permute-start(bf16[64,3712]{1,0:T(8,128)(2,1)S(1)} %collective-permute-done.9.refs_3_), channel_id=1, source_target_pairs={{0,2},{1,7},{2,4},{3,1},{4,6},{5,3},{6,0},{7,5},{8,10},{9,15},{10,... | collective-permute-start | bytes 1425416 | tf_op jit(solution)/shard_map/ppermute | solution.py:28
  64.8 12.8 %collective-permute-start.15 = (bf16[64,3584]{1,0:T(8,128)(2,1)S(1)}, bf16[64,3584]{1,0:T(8,128)(2,1)S(1)}, u32[]{:S(2)}, u32[]{:S(2)}) collective-permute-start(bf16[64,3584]{1,0:T(8,128)(2,1)S(1)} %get-tuple-element.71), channel_id=1, source_target_pairs={{7,0},{2,1},{1,2},{4,3},{3,4},{6,5},{5,6},{0,7},{15,8},{10,9},{9,1... | collective-permute-start | bytes 1376264 | tf_op jit(solution)/shard_map/ppermute | solution.py:28
  66.4 11.8 %collective-permute-start.18 = (bf16[64,3712]{1,0:T(8,128)(2,1)S(1)}, bf16[64,3712]{1,0:T(8,128)(2,1)S(1)}, u32[]{:S(2)}, u32[]{:S(2)}) collective-permute-start(bf16[64,3712]{1,0:T(8,128)(2,1)S(1)} %copy-done.4), channel_id=1, source_target_pairs={{0,7},{1,2},{2,1},{3,4},{4,3},{5,6},{6,5},{7,0},{8,15},{9,10},{10,... | collective-permute-start | bytes 1425416 | tf_op jit(solution)/shard_map/ppermute | solution.py:28
  70.9 15.0 %collective-permute-start.17 = (bf16[64,3584]{1,0:T(8,128)(2,1)S(1)}, bf16[64,3584]{1,0:T(8,128)(2,1)S(1)}, u32[]{:S(2)}, u32[]{:S(2)}) collective-permute-start(bf16[64,3584]{1,0:T(8,128)(2,1)S(1)} %shard_map.116), channel_id=1, source_target_pairs={{0,8},{1,9},{2,10},{3,11},{4,12},{5,13},{6,14},{7,15},{8,0},{9,1},... | collective-permute-start | bytes 1376264 | tf_op jit(solution)/shard_map/ppermute | solution.py:28
  71.2 12.1 %collective-permute-start.19 = (bf16[64,3712]{1,0:T(8,128)(2,1)S(1)}, bf16[64,3712]{1,0:T(8,128)(2,1)S(1)}, u32[]{:S(2)}, u32[]{:S(2)}) collective-permute-start(bf16[64,3712]{1,0:T(8,128)(2,1)S(1)} %copy-done.5), channel_id=1, source_target_pairs={{0,7},{1,2},{2,1},{3,4},{4,3},{5,6},{6,5},{7,0},{8,15},{9,10},{10,... | collective-permute-start | bytes 1425416 | tf_op jit(solution)/shard_map/ppermute | solution.py:28
  77.7 11.0 %collective-permute-start.16 = (bf16[64,3584]{1,0:T(8,128)(2,1)S(1)}, bf16[64,3584]{1,0:T(8,128)(2,1)S(1)}, u32[]{:S(2)}, u32[]{:S(2)}) collective-permute-start(bf16[64,3584]{1,0:T(8,128)(2,1)S(1)} %get-tuple-element.72), channel_id=1, source_target_pairs={{7,0},{2,1},{1,2},{4,3},{3,4},{6,5},{5,6},{0,7},{15,8},{10,9},{9,1... | collective-permute-start | bytes 1376264 | tf_op jit(solution)/shard_map/ppermute | solution.py:28
  78.2 24.4 %collective-permute-start.21 = (bf16[64,3584]{1,0:T(8,128)(2,1)S(1)}, bf16[64,3584]{1,0:T(8,128)(2,1)S(1)}, u32[]{:S(2)}, u32[]{:S(2)}) collective-permute-start(bf16[64,3584]{1,0:T(8,128)(2,1)S(1)} %get-tuple-element.86), channel_id=1, source_target_pairs={{2,0},{7,1},{4,2},{1,3},{6,4},{3,5},{0,6},{5,7},{10,8},{15,9},{12,... | collective-permute-start | bytes 1376264 | tf_op jit(solution)/shard_map/ppermute | solution.py:28
  83.3 20.4 %collective-permute-start.20 = (bf16[64,3584]{1,0:T(8,128)(2,1)S(1)}, bf16[64,3584]{1,0:T(8,128)(2,1)S(1)}, u32[]{:S(2)}, u32[]{:S(2)}) collective-permute-start(bf16[64,3584]{1,0:T(8,128)(2,1)S(1)} %shard_map.118), channel_id=1, source_target_pairs={{0,8},{1,9},{2,10},{3,11},{4,12},{5,13},{6,14},{7,15},{8,0},{9,1},... | collective-permute-start | bytes 1376264 | tf_op jit(solution)/shard_map/ppermute | solution.py:28
  85.9 17.7 %collective-permute-start.24 = (bf16[64,3584]{1,0:T(8,128)(2,1)S(1)}, bf16[64,3584]{1,0:T(8,128)(2,1)S(1)}, u32[]{:S(2)}, u32[]{:S(2)}) collective-permute-start(bf16[64,3584]{1,0:T(8,128)(2,1)S(1)} %add_convert_fusion.8), channel_id=1, source_target_pairs={{0,4},{1,5},{2,6},{3,7},{4,0},{5,1},{6,2},{7,3},{8,12},{9,13},{10,... | collective-permute-start | bytes 1376264 | tf_op jit(solution)/shard_map/ppermute | solution.py:28
  95.0 12.9 %collective-permute-start.23 = (bf16[64,3584]{1,0:T(8,128)(2,1)S(1)}, bf16[64,3584]{1,0:T(8,128)(2,1)S(1)}, u32[]{:S(2)}, u32[]{:S(2)}) collective-permute-start(bf16[64,3584]{1,0:T(8,128)(2,1)S(1)} %get-tuple-element.84), channel_id=1, source_target_pairs={{7,0},{2,1},{1,2},{4,3},{3,4},{6,5},{5,6},{0,7},{15,8},{10,9},{9,1... | collective-permute-start | bytes 1376264 | tf_op jit(solution)/shard_map/ppermute | solution.py:28
  102.6 10.5 %collective-permute-start.22 = (bf16[64,3584]{1,0:T(8,128)(2,1)S(1)}, bf16[64,3584]{1,0:T(8,128)(2,1)S(1)}, u32[]{:S(2)}, u32[]{:S(2)}) collective-permute-start(bf16[64,3584]{1,0:T(8,128)(2,1)S(1)} %get-tuple-element.87), channel_id=1, source_target_pairs={{2,0},{7,1},{4,2},{1,3},{6,4},{3,5},{0,6},{5,7},{10,8},{15,9},{12,... | collective-permute-start | bytes 1376264 | tf_op jit(solution)/shard_map/ppermute | solution.py:28
  103.8 15.1 %collective-permute-start.27 = (bf16[64,3584]{1,0:T(8,128)(2,1)S(1)}, bf16[64,3584]{1,0:T(8,128)(2,1)S(1)}, u32[]{:S(2)}, u32[]{:S(2)}) collective-permute-start(bf16[64,3584]{1,0:T(8,128)(2,1)S(1)} %add_convert_fusion.6), channel_id=1, source_target_pairs={{0,24},{1,25},{2,26},{3,27},{4,28},{5,29},{6,30},{7,31},{8,16},{9,... | collective-permute-start | bytes 1376264 | tf_op jit(solution)/shard_map/ppermute | solution.py:53
  104.8 13.3 %collective-permute-start.28 = (bf16[64,3584]{1,0:T(8,128)(2,1)S(1)}, bf16[64,3584]{1,0:T(8,128)(2,1)S(1)}, u32[]{:S(2)}, u32[]{:S(2)}) collective-permute-start(bf16[64,3584]{1,0:T(8,128)(2,1)S(1)} %add_convert_fusion.5), channel_id=1, source_target_pairs={{2,0},{7,1},{4,2},{1,3},{6,4},{3,5},{0,6},{5,7},{10,8},{15,9},{12,... | collective-permute-start | bytes 1376264 | tf_op jit(solution)/shard_map/ppermute | solution.py:28
  107.9 19.7 %collective-permute-start.26 = (bf16[64,3584]{1,0:T(8,128)(2,1)S(1)}, bf16[64,3584]{1,0:T(8,128)(2,1)S(1)}, u32[]{:S(2)}, u32[]{:S(2)}) collective-permute-start(bf16[64,3584]{1,0:T(8,128)(2,1)S(1)} %get-tuple-element.89), channel_id=1, source_target_pairs={{2,0},{7,1},{4,2},{1,3},{6,4},{3,5},{0,6},{5,7},{10,8},{15,9},{12,... | collective-permute-start | bytes 1376264 | tf_op jit(solution)/shard_map/ppermute | solution.py:28
  108.5 19.1 %collective-permute-start.30 = (bf16[64,3584]{1,0:T(8,128)(2,1)S(1)}, bf16[64,3584]{1,0:T(8,128)(2,1)S(1)}, u32[]{:S(2)}, u32[]{:S(2)}) collective-permute-start(bf16[64,3584]{1,0:T(8,128)(2,1)S(1)} %get-tuple-element.97), channel_id=1, source_target_pairs={{7,0},{2,1},{1,2},{4,3},{3,4},{6,5},{5,6},{0,7},{15,8},{10,9},{9,1... | collective-permute-start | bytes 1376264 | tf_op jit(solution)/shard_map/ppermute | solution.py:28
  113.4 17.4 %collective-permute-start.25 = (bf16[64,3584]{1,0:T(8,128)(2,1)S(1)}, bf16[64,3584]{1,0:T(8,128)(2,1)S(1)}, u32[]{:S(2)}, u32[]{:S(2)}) collective-permute-start(bf16[64,3584]{1,0:T(8,128)(2,1)S(1)} %add_convert_fusion.7), channel_id=1, source_target_pairs={{0,112},{16,0},{32,16},{48,32},{64,48},{80,64},{96,80},{112,96},{1... | collective-permute-start | bytes 1376264 | tf_op jit(solution)/shard_map/ppermute | solution.py:43
  118.1 14.3 %collective-permute-start.29 = (bf16[64,3584]{1,0:T(8,128)(2,1)S(1)}, bf16[64,3584]{1,0:T(8,128)(2,1)S(1)}, u32[]{:S(2)}, u32[]{:S(2)}) collective-permute-start(bf16[64,3584]{1,0:T(8,128)(2,1)S(1)} %add_convert_fusion.4), channel_id=1, source_target_pairs={{2,0},{7,1},{4,2},{1,3},{6,4},{3,5},{0,6},{5,7},{10,8},{15,9},{12,... | collective-permute-start | bytes 1376264 | tf_op jit(solution)/shard_map/ppermute | solution.py:28
  127.7 12.7 %collective-permute-start.32 = (bf16[64,3584]{1,0:T(8,128)(2,1)S(1)}, bf16[64,3584]{1,0:T(8,128)(2,1)S(1)}, u32[]{:S(2)}, u32[]{:S(2)}) collective-permute-start(bf16[64,3584]{1,0:T(8,128)(2,1)S(1)} %add_convert_fusion.2), channel_id=1, source_target_pairs={{0,120},{1,121},{2,122},{3,123},{4,124},{5,125},{6,126},{7,127},{8... | collective-permute-start | bytes 1376264 | tf_op jit(solution)/shard_map/ppermute | solution.py:53
  132.7 13.9 %collective-permute-start.31 = (bf16[64,3584]{1,0:T(8,128)(2,1)S(1)}, bf16[64,3584]{1,0:T(8,128)(2,1)S(1)}, u32[]{:S(2)}, u32[]{:S(2)}) collective-permute-start(bf16[64,3584]{1,0:T(8,128)(2,1)S(1)} %add_convert_fusion.3), channel_id=1, source_target_pairs={{0,16},{16,32},{32,48},{48,64},{64,80},{80,96},{96,112},{112,0},{1... | collective-permute-start | bytes 1376264 | tf_op jit(solution)/shard_map/ppermute | solution.py:43
  (9 other events, 83.5 us)

commit v4 on v3

--- a/solution.py
+++ b/solution.py
@@ -81,9 +81,8 @@
             hidden = gate_value * (1.0 / (1.0 + jnp.exp(-gate_value))) * up_value * share
             hidden_all[:, pl.ds(side * units + start, TILE)] = hidden.astype(jnp.bfloat16)
 
-    @pl.loop(0, width // WIDE)
-    def _(n):
-        columns = pl.ds(pl.multiple_of(n * WIDE, WIDE), WIDE)
+    for start in range(0, width, WIDE):
+        columns = pl.ds(start, WIDE)
         partial = jnp.dot(hidden_all[:, :units], mine[2][:, columns], preferred_element_type=jnp.float32)
         partial += jnp.dot(hidden_all[:, units:], other[2][:, columns], preferred_element_type=jnp.float32)
         row = 0

time: 148 us -> 147 us (level)
  waiting for transfers between devices: 51.5 us -> 54.7 us
  Pallas kernels: 34.7 us -> 33 us
  starting transfers between devices: 51.3 us -> 49.7 us
    ppermute x29, waiting for transfers between devices: 39.1 us -> 42.3 us  [sent(): return lambda block: lax.ppermute(block, 'expert', route)]
    pallas_call x6, Pallas kernels: 30.6 us -> 28.9 us  [ffn(): pl.pallas_call(functools.partial(ffn_kernel, len(blocks), width), in_spec...]
    ppermute x29, starting transfers between devices: 44.5 us -> 42.8 us  [sent(): return lambda block: lax.ppermute(block, 'expert', route)]
  transfers between devices with their start and end apart: 33 -> 33, of which waited for: 15 -> 16; matrix products, arithmetic and copies ran while one was open for 1% -> 1% of each run, Pallas kernels for 21% -> 20%
where the time goes in v4:
time: 147 us
  waiting for transfers between devices  54.7 us (37%)
  starting transfers between devices  49.7 us (34%)
  Pallas kernels  33 us (22%)
  local copies, waits for them, and re-layouts  6.14 us (4%)
  other arithmetic  2.91 us (2%)
    ppermute x29, starting transfers between devices, sent(): return lambda block: lax.ppermute(block, 'expert', route)  42.8 us
    ppermute x29, waiting for transfers between devices, sent(): return lambda block: lax.ppermute(block, 'expert', route)  42.3 us
    pallas_call x6, Pallas kernels, ffn(): pl.pallas_call(functools.partial(ffn_kernel, len(blocks), width), in_spec...  28.9 us
    ppermute x2, waiting for transfers between devices, shifted_across(): return lax.ppermute(block, ('section', 'expert'), route)  7.08 us
    unnamed x16, local copies, waits for them, and re-layouts  6.14 us
    ppermute x2, waiting for transfers between devices, shifted(): return lax.ppermute(block, 'section', route)  5.31 us
    pallas_call x2, Pallas kernels, prepare(): pl.pallas_call(prepare_kernel, in_specs=[pl.BlockSpec(memory_space=pltpu....  4.11 us
    ppermute x2, starting transfers between devices, shifted_across(): return lax.ppermute(block, ('section', 'expert'), route)  3.89 us
  transfers between devices with their start and end apart: 33, of which 16 were waited for; matrix products, arithmetic and copies ran while one was open for 1% of the time, Pallas kernels for 20%

profile of v4, /device:TPU:1, one launch (start us, length us, event | category | flops | bytes accessed | tf_op | source)
XLA Modules:
  0.0 147.2 jit_solution(17248336372779293756)
XLA Ops:
  0.6 2.0 %shard_map.113.refs_0_ = bf16[64,3712]{1,0:T(8,128)(2,1)} custom-call(bf16[64,3584]{1,0:T(8,128)(2,1)} %bitcast.41, f32[1,3584]{1,0:T(1,128)} %refs_1_.3, s32[2,64]{1,0:T(2,128)} %bitcast.46, f32[2,64]{1,0:T(2,128)} %bitcast.47), custom_call_target="tpu_custom_call" | custom-call | flops 1376256 | bytes 917504 | tf_op jit(solution)/shard_map/pallas_call | solution.py:146
  2.7 2.1 %shard_map.114.refs_0_ = bf16[64,3712]{1,0:T(8,128)(2,1)} custom-call(bf16[64,3584]{1,0:T(8,128)(2,1)} %bitcast.43, f32[1,3584]{1,0:T(1,128)} %refs_1_.3, s32[2,64]{1,0:T(2,128)} %bitcast.48, f32[2,64]{1,0:T(2,128)} %bitcast.49), custom_call_target="tpu_custom_call" | custom-call | flops 1376256 | bytes 917504 | tf_op jit(solution)/shard_map/pallas_call | solution.py:146
  6.3 3.8 %collective-permute-start.2 = (bf16[64,3712]{1,0:T(8,128)(2,1)}, bf16[64,3712]{1,0:T(8,128)(2,1)S(1)}, u32[]{:S(2)}, u32[]{:S(2)}) collective-permute-start(bf16[64,3712]{1,0:T(8,128)(2,1)} %shard_map.113.refs_0_), channel_id=1, source_target_pairs={{0,2},{1,7},{2,4},{3,1},{4,6},{5,3},{6,0},{7,5},{8,10},{9,15},{10,... | collective-permute-start | bytes 1425416 | tf_op jit(solution)/shard_map/ppermute | solution.py:28
  10.2 5.9 %collective-permute-done.2.refs_1_ = bf16[64,3712]{1,0:T(8,128)(2,1)S(1)} collective-permute-done((bf16[64,3712]{1,0:T(8,128)(2,1)}, bf16[64,3712]{1,0:T(8,128)(2,1)S(1)}, u32[]{:S(2)}, u32[]{:S(2)}) %collective-permute-start.2) | collective-permute-done | bytes 475168 | tf_op jit(solution)/shard_map/ppermute | solution.py:28
  18.1 3.8 %collective-permute-start = (bf16[64,3712]{1,0:T(8,128)(2,1)}, bf16[64,3712]{1,0:T(8,128)(2,1)S(1)}, u32[]{:S(2)}, u32[]{:S(2)}) collective-permute-start(bf16[64,3712]{1,0:T(8,128)(2,1)} %shard_map.114.refs_0_), channel_id=1, source_target_pairs={{0,2},{1,7},{2,4},{3,1},{4,6},{5,3},{6,0},{7,5},{8,10},{9,15},{10,... | collective-permute-start | bytes 1425416 | tf_op jit(solution)/shard_map/ppermute | solution.py:28
  22.0 2.9 %collective-permute-start.4 = (bf16[64,3712]{1,0:T(8,128)(2,1)}, bf16[64,3712]{1,0:T(8,128)(2,1)S(1)}, u32[]{:S(2)}, u32[]{:S(2)}) collective-permute-start(bf16[64,3712]{1,0:T(8,128)(2,1)} %shard_map.113.refs_0_), channel_id=1, source_target_pairs={{0,8},{1,9},{2,10},{3,11},{4,12},{5,13},{6,14},{7,15},{8,0},{9,1},... | collective-permute-start | bytes 1425416 | tf_op jit(solution)/shard_map/ppermute | solution.py:28
  25.1 2.8 %collective-permute-done.refs_1_ = bf16[64,3712]{1,0:T(8,128)(2,1)S(1)} collective-permute-done((bf16[64,3712]{1,0:T(8,128)(2,1)}, bf16[64,3712]{1,0:T(8,128)(2,1)S(1)}, u32[]{:S(2)}, u32[]{:S(2)}) %collective-permute-start) | collective-permute-done | bytes 475168 | tf_op jit(solution)/shard_map/ppermute | solution.py:28
  27.9 3.3 %collective-permute-start.1 = (bf16[64,3712]{1,0:T(8,128)(2,1)S(1)}, bf16[64,3712]{1,0:T(8,128)(2,1)S(1)}, u32[]{:S(2)}, u32[]{:S(2)}) collective-permute-start(bf16[64,3712]{1,0:T(8,128)(2,1)S(1)} %collective-permute-done.refs_1_), channel_id=1, source_target_pairs={{0,2},{1,7},{2,4},{3,1},{4,6},{5,3},{6,0},{7,5},{8,10},{9,15},{10,... | collective-permute-start | bytes 1425416 | tf_op jit(solution)/shard_map/ppermute | solution.py:28
  31.2 5.4 %collective-permute-done.4.refs_3_ = bf16[64,3712]{1,0:T(8,128)(2,1)S(1)} collective-permute-done((bf16[64,3712]{1,0:T(8,128)(2,1)}, bf16[64,3712]{1,0:T(8,128)(2,1)S(1)}, u32[]{:S(2)}, u32[]{:S(2)}) %collective-permute-start.4) | collective-permute-done | bytes 475168 | tf_op jit(solution)/shard_map/ppermute | solution.py:28
  36.6 2.3 %collective-permute-start.12 = (bf16[64,3712]{1,0:T(8,128)(2,1)S(1)}, bf16[64,3712]{1,0:T(8,128)(2,1)S(1)}, u32[]{:S(2)}, u32[]{:S(2)}) collective-permute-start(bf16[64,3712]{1,0:T(8,128)(2,1)S(1)} %collective-permute-done.4.refs_3_), channel_id=1, source_target_pairs={{0,7},{1,2},{2,1},{3,4},{4,3},{5,6},{6,5},{7,0},{8,15},{9,10},{10,... | collective-permute-start | bytes 1425416 | tf_op jit(solution)/shard_map/ppermute | solution.py:28
  38.9 2.9 %collective-permute-start.8 = (bf16[64,3712]{1,0:T(8,128)(2,1)S(1)}, bf16[64,3712]{1,0:T(8,128)(2,1)S(1)}, u32[]{:S(2)}, u32[]{:S(2)}) collective-permute-start(bf16[64,3712]{1,0:T(8,128)(2,1)S(1)} %collective-permute-done.3.refs_0_), channel_id=1, source_target_pairs={{0,8},{1,9},{2,10},{3,11},{4,12},{5,13},{6,14},{7,15},{8,0},{9,1},... | collective-permute-start | bytes 1425416 | tf_op jit(solution)/shard_map/ppermute | solution.py:28
  41.9 4.9 %collective-permute-done.9.refs_3_ = bf16[64,3712]{1,0:T(8,128)(2,1)S(1)} collective-permute-done((bf16[64,3712]{1,0:T(8,128)(2,1)}, bf16[64,3712]{1,0:T(8,128)(2,1)S(1)}, u32[]{:S(2)}, u32[]{:S(2)}) %collective-permute-start.9) | collective-permute-done | bytes 475168 | tf_op jit(solution)/shard_map/ppermute | solution.py:28
  48.3 2.9 %collective-permute-start.13 = (bf16[64,3712]{1,0:T(8,128)(2,1)S(1)}, bf16[64,3712]{1,0:T(8,128)(2,1)S(1)}, u32[]{:S(2)}, u32[]{:S(2)}) collective-permute-start(bf16[64,3712]{1,0:T(8,128)(2,1)S(1)} %collective-permute-done.1.refs_0_), channel_id=1, source_target_pairs={{0,8},{1,9},{2,10},{3,11},{4,12},{5,13},{6,14},{7,15},{8,0},{9,1},... | collective-permute-start | bytes 1425416 | tf_op jit(solution)/shard_map/ppermute | solution.py:28
  51.2 2.6 %collective-permute-start.14 = (bf16[64,3712]{1,0:T(8,128)(2,1)S(1)}, bf16[64,3712]{1,0:T(8,128)(2,1)S(1)}, u32[]{:S(2)}, u32[]{:S(2)}) collective-permute-start(bf16[64,3712]{1,0:T(8,128)(2,1)S(1)} %collective-permute-done.9.refs_3_), channel_id=1, source_target_pairs={{0,2},{1,7},{2,4},{3,1},{4,6},{5,3},{6,0},{7,5},{8,10},{9,15},{10,... | collective-permute-start | bytes 1425416 | tf_op jit(solution)/shard_map/ppermute | solution.py:28
  53.8 2.0 %copy-done = bf16[1,3584,512]{2,1,0:T(8,128)(2,1)S(1)} copy-done((bf16[1,3584,512]{2,1,0:T(8,128)(2,1)S(1)}, bf16[1,3584,512]{2,1,0:T(8,128)(2,1)}, u32[]{:S(2)}) %copy-start) | copy-done | bytes 3670040
  55.8 2.0 %copy-done.2 = bf16[1,3584,512]{2,1,0:T(8,128)(2,1)S(1)} copy-done((bf16[1,3584,512]{2,1,0:T(8,128)(2,1)S(1)}, bf16[1,3584,512]{2,1,0:T(8,128)(2,1)}, u32[]{:S(2)}) %copy-start.2) | copy-done | bytes 3670040
  57.9 2.0 %copy-done.3 = bf16[1,512,3584]{2,1,0:T(8,128)(2,1)S(1)} copy-done((bf16[1,512,3584]{2,1,0:T(8,128)(2,1)S(1)}, bf16[1,512,3584]{2,1,0:T(8,128)(2,1)}, u32[]{:S(2)}) %copy-start.3) | copy-done | bytes 3670040
  59.9 4.6 %shard_map.115 = (bf16[64,3584]{1,0:T(8,128)(2,1)S(1)}, bf16[64,3584]{1,0:T(8,128)(2,1)S(1)}, bf16[64,3584]{1,0:T(8,128)(2,1)S(1)}) custom-call(bf16[64,3712]{1,0:T(8,128)(2,1)S(1)} %collective-permute-done.3.refs_0_, bf16[64,3712]{1,0:T(8,128)(2,1)S(1)} %collective-permute-done.11.refs_1_, bf16[64,3712]{1,0:T(8,128)(2,1)S(1)} %collective-permute-done.12.refs_2_, ...), custom_call_target="tpu_custom_call" | custom-call | flops 4227858432 | bytes 22020096 | tf_op jit(solution)/shard_map/pallas_call | solution.py:101
  66.4 4.0 %shard_map.116 = bf16[64,3584]{1,0:T(8,128)(2,1)S(1)} custom-call(bf16[64,3712]{1,0:T(8,128)(2,1)S(1)} %collective-permute-done.8.refs_0_, bf16[3584,512]{1,0:T(8,128)(2,1)S(1)} %bitcast.22, bf16[3584,512]{1,0:T(8,128)(2,1)S(1)} %bitcast.29, bf16[512,3584]{1,0:T(8,128)(2,1)S(1)} %bitcast.36, ...), custom_call_target="tpu_custom_call" | custom-call | flops 1409286144 | bytes 22020096 | tf_op jit(solution)/shard_map/pallas_call | solution.py:101
  72.3 4.6 %shard_map.117 = (bf16[64,3584]{1,0:T(8,128)(2,1)S(1)}, bf16[64,3584]{1,0:T(8,128)(2,1)S(1)}, bf16[64,3584]{1,0:T(8,128)(2,1)S(1)}) custom-call(bf16[64,3712]{1,0:T(8,128)(2,1)S(1)} %collective-permute-done.1.refs_0_, bf16[64,3712]{1,0:T(8,128)(2,1)S(1)} %collective-permute-done.14.refs_1_, bf16[64,3712]{1,0:T(8,128)(2,1)S(1)} %collective-permute-done.10.refs_2_, ...), custom_call_target="tpu_custom_call" | custom-call | flops 4227858432 | bytes 22020096 | tf_op jit(solution)/shard_map/pallas_call | solution.py:101
  78.5 4.0 %shard_map.118 = bf16[64,3584]{1,0:T(8,128)(2,1)S(1)} custom-call(bf16[64,3712]{1,0:T(8,128)(2,1)S(1)} %collective-permute-done.13.refs_0_, bf16[3584,512]{1,0:T(8,128)(2,1)S(1)} %bitcast.24, bf16[3584,512]{1,0:T(8,128)(2,1)S(1)} %bitcast.31, bf16[512,3584]{1,0:T(8,128)(2,1)S(1)} %bitcast.38, ...), custom_call_target="tpu_custom_call" | custom-call | flops 1409286144 | bytes 22020096 | tf_op jit(solution)/shard_map/pallas_call | solution.py:101
  85.0 3.0 %collective-permute-start.24 = (bf16[64,3584]{1,0:T(8,128)(2,1)S(1)}, bf16[64,3584]{1,0:T(8,128)(2,1)S(1)}, u32[]{:S(2)}, u32[]{:S(2)}) collective-permute-start(bf16[64,3584]{1,0:T(8,128)(2,1)S(1)} %add_convert_fusion.8), channel_id=1, source_target_pairs={{0,4},{1,5},{2,6},{3,7},{4,0},{5,1},{6,2},{7,3},{8,12},{9,13},{10,... | collective-permute-start | bytes 1376264 | tf_op jit(solution)/shard_map/ppermute | solution.py:28
  87.9 5.9 %shard_map.119 = (bf16[64,3584]{1,0:T(8,128)(2,1)S(1)}, bf16[64,3584]{1,0:T(8,128)(2,1)S(1)}, bf16[64,3584]{1,0:T(8,128)(2,1)S(1)}, bf16[64,3584]{1,0:T(8,128)(2,1)S(1)}) custom-call(bf16[64,3712]{1,0:T(8,128)(2,1)S(1)} %copy-done.5, bf16[64,3712]{1,0:T(8,128)(2,1)S(1)} %collective-permute-done.2.refs_1_, ...), custom_call_target="tpu_custom_call" | custom-call | flops 5637144576 | bytes 22020096 | tf_op jit(solution)/shard_map/pallas_call | solution.py:101
  95.1 5.9 %shard_map.120 = (bf16[64,3584]{1,0:T(8,128)(2,1)S(1)}, bf16[64,3584]{1,0:T(8,128)(2,1)S(1)}, bf16[64,3584]{1,0:T(8,128)(2,1)S(1)}, bf16[64,3584]{1,0:T(8,128)(2,1)S(1)}) custom-call(bf16[64,3712]{1,0:T(8,128)(2,1)S(1)} %copy-done.4, bf16[64,3712]{1,0:T(8,128)(2,1)S(1)} %collective-permute-done.refs_1_, ...), custom_call_target="tpu_custom_call" | custom-call | flops 5637144576 | bytes 22020096 | tf_op jit(solution)/shard_map/pallas_call | solution.py:101
  105.4 2.2 %collective-permute-done.23 = bf16[64,3584]{1,0:T(8,128)(2,1)S(1)} collective-permute-done((bf16[64,3584]{1,0:T(8,128)(2,1)S(1)}, bf16[64,3584]{1,0:T(8,128)(2,1)S(1)}, u32[]{:S(2)}, u32[]{:S(2)}) %collective-permute-start.23) | collective-permute-done | bytes 458784 | tf_op jit(solution)/shard_map/ppermute | solution.py:28
  109.9 2.9 %collective-permute-done.22 = bf16[64,3584]{1,0:T(8,128)(2,1)S(1)} collective-permute-done((bf16[64,3584]{1,0:T(8,128)(2,1)S(1)}, bf16[64,3584]{1,0:T(8,128)(2,1)S(1)}, u32[]{:S(2)}, u32[]{:S(2)}) %collective-permute-start.22) | collective-permute-done | bytes 458784 | tf_op jit(solution)/shard_map/ppermute | solution.py:28
  113.1 2.4 %collective-permute-start.25 = (bf16[64,3584]{1,0:T(8,128)(2,1)S(1)}, bf16[64,3584]{1,0:T(8,128)(2,1)S(1)}, u32[]{:S(2)}, u32[]{:S(2)}) collective-permute-start(bf16[64,3584]{1,0:T(8,128)(2,1)S(1)} %add_convert_fusion.7), channel_id=1, source_target_pairs={{0,112},{16,0},{32,16},{48,32},{64,48},{80,64},{96,80},{112,96},{1... | collective-permute-start | bytes 1376264 | tf_op jit(solution)/shard_map/ppermute | solution.py:43
  115.5 2.3 %collective-permute-done.28 = bf16[64,3584]{1,0:T(8,128)(2,1)S(1)} collective-permute-done((bf16[64,3584]{1,0:T(8,128)(2,1)S(1)}, bf16[64,3584]{1,0:T(8,128)(2,1)S(1)}, u32[]{:S(2)}, u32[]{:S(2)}) %collective-permute-start.28) | collective-permute-done | bytes 458784 | tf_op jit(solution)/shard_map/ppermute | solution.py:28
  118.6 8.7 %collective-permute-done.30 = bf16[64,3584]{1,0:T(8,128)(2,1)S(1)} collective-permute-done((bf16[64,3584]{1,0:T(8,128)(2,1)S(1)}, bf16[64,3584]{1,0:T(8,128)(2,1)S(1)}, u32[]{:S(2)}, u32[]{:S(2)}) %collective-permute-start.30) | collective-permute-done | bytes 458784 | tf_op jit(solution)/shard_map/ppermute | solution.py:28
  127.5 3.0 %collective-permute-start.32 = (bf16[64,3584]{1,0:T(8,128)(2,1)S(1)}, bf16[64,3584]{1,0:T(8,128)(2,1)S(1)}, u32[]{:S(2)}, u32[]{:S(2)}) collective-permute-start(bf16[64,3584]{1,0:T(8,128)(2,1)S(1)} %add_convert_fusion.2), channel_id=1, source_target_pairs={{0,120},{1,121},{2,122},{3,123},{4,124},{5,125},{6,126},{7,127},{8... | collective-permute-start | bytes 1376264 | tf_op jit(solution)/shard_map/ppermute | solution.py:53
  133.0 7.1 %collective-permute-done.32 = bf16[64,3584]{1,0:T(8,128)(2,1)S(1)} collective-permute-done((bf16[64,3584]{1,0:T(8,128)(2,1)S(1)}, bf16[64,3584]{1,0:T(8,128)(2,1)S(1)}, u32[]{:S(2)}, u32[]{:S(2)}) %collective-permute-start.32) | collective-permute-done | bytes 458784 | tf_op jit(solution)/shard_map/ppermute | solution.py:53
  141.0 5.3 %collective-permute-done.31 = bf16[64,3584]{1,0:T(8,128)(2,1)S(1)} collective-permute-done((bf16[64,3584]{1,0:T(8,128)(2,1)S(1)}, bf16[64,3584]{1,0:T(8,128)(2,1)S(1)}, u32[]{:S(2)}, u32[]{:S(2)}) %collective-permute-start.31) | collective-permute-done | bytes 458784 | tf_op jit(solution)/shard_map/ppermute | solution.py:43
  (67 shorter events, 26.7 us)
Async XLA Ops:
  4.8 11.4 %collective-permute-start.5 = (bf16[3584,512]{1,0:T(8,128)(2,1)}, bf16[3584,512]{1,0:T(8,128)(2,1)S(1)}, u32[]{:S(2)}, u32[]{:S(2)}) collective-permute-start(bf16[3584,512]{1,0:T(8,128)(2,1)} %bitcast.20), channel_id=1, source_target_pairs={{0,1},{1,0},{2,3},{3,2},{4,5},{5,4},{6,7},{7,6},{8,9},{9,8},{10,11... | collective-permute-start | bytes 11010056 | tf_op jit(solution)/shard_map/ppermute | solution.py:28
  6.3 11.5 %collective-permute-start.6 = (bf16[512,3584]{1,0:T(8,128)(2,1)}, bf16[512,3584]{1,0:T(8,128)(2,1)S(1)}, u32[]{:S(2)}, u32[]{:S(2)}) collective-permute-start(bf16[512,3584]{1,0:T(8,128)(2,1)} %bitcast.34), channel_id=1, source_target_pairs={{0,1},{1,0},{2,3},{3,2},{4,5},{5,4},{6,7},{7,6},{8,9},{9,8},{10,11... | collective-permute-start | bytes 11010056 | tf_op jit(solution)/shard_map/ppermute | solution.py:28
  17.7 18.9 %collective-permute-start.7 = (bf16[3584,512]{1,0:T(8,128)(2,1)}, bf16[3584,512]{1,0:T(8,128)(2,1)S(1)}, u32[]{:S(2)}, u32[]{:S(2)}) collective-permute-start(bf16[3584,512]{1,0:T(8,128)(2,1)} %bitcast.27), channel_id=1, source_target_pairs={{0,1},{1,0},{2,3},{3,2},{4,5},{5,4},{6,7},{7,6},{8,9},{9,8},{10,11... | collective-permute-start | bytes 11010056 | tf_op jit(solution)/shard_map/ppermute | solution.py:28
  18.1 9.8 %collective-permute-start = (bf16[64,3712]{1,0:T(8,128)(2,1)}, bf16[64,3712]{1,0:T(8,128)(2,1)S(1)}, u32[]{:S(2)}, u32[]{:S(2)}) collective-permute-start(bf16[64,3712]{1,0:T(8,128)(2,1)} %shard_map.114.refs_0_), channel_id=1, source_target_pairs={{0,2},{1,7},{2,4},{3,1},{4,6},{5,3},{6,0},{7,5},{8,10},{9,15},{10,... | collective-permute-start | bytes 1425416 | tf_op jit(solution)/shard_map/ppermute | solution.py:28
  22.0 14.6 %collective-permute-start.4 = (bf16[64,3712]{1,0:T(8,128)(2,1)}, bf16[64,3712]{1,0:T(8,128)(2,1)S(1)}, u32[]{:S(2)}, u32[]{:S(2)}) collective-permute-start(bf16[64,3712]{1,0:T(8,128)(2,1)} %shard_map.113.refs_0_), channel_id=1, source_target_pairs={{0,8},{1,9},{2,10},{3,11},{4,12},{5,13},{6,14},{7,15},{8,0},{9,1},... | collective-permute-start | bytes 1425416 | tf_op jit(solution)/shard_map/ppermute | solution.py:28
  24.9 14.1 %collective-permute-start.3 = (bf16[64,3712]{1,0:T(8,128)(2,1)S(1)}, bf16[64,3712]{1,0:T(8,128)(2,1)S(1)}, u32[]{:S(2)}, u32[]{:S(2)}) collective-permute-start(bf16[64,3712]{1,0:T(8,128)(2,1)S(1)} %collective-permute-done.2.refs_1_), channel_id=1, source_target_pairs={{0,2},{1,7},{2,4},{3,1},{4,6},{5,3},{6,0},{7,5},{8,10},{9,15},{10,... | collective-permute-start | bytes 1425416 | tf_op jit(solution)/shard_map/ppermute | solution.py:28
  25.0 21.8 %collective-permute-start.9 = (bf16[64,3712]{1,0:T(8,128)(2,1)}, bf16[64,3712]{1,0:T(8,128)(2,1)S(1)}, u32[]{:S(2)}, u32[]{:S(2)}) collective-permute-start(bf16[64,3712]{1,0:T(8,128)(2,1)} %shard_map.114.refs_0_), channel_id=1, source_target_pairs={{0,8},{1,9},{2,10},{3,11},{4,12},{5,13},{6,14},{7,15},{8,0},{9,1},... | collective-permute-start | bytes 1425416 | tf_op jit(solution)/shard_map/ppermute | solution.py:28
  27.9 18.9 %collective-permute-start.1 = (bf16[64,3712]{1,0:T(8,128)(2,1)S(1)}, bf16[64,3712]{1,0:T(8,128)(2,1)S(1)}, u32[]{:S(2)}, u32[]{:S(2)}) collective-permute-start(bf16[64,3712]{1,0:T(8,128)(2,1)S(1)} %collective-permute-done.refs_1_), channel_id=1, source_target_pairs={{0,2},{1,7},{2,4},{3,1},{4,6},{5,3},{6,0},{7,5},{8,10},{9,15},{10,... | collective-permute-start | bytes 1425416 | tf_op jit(solution)/shard_map/ppermute | solution.py:28
  36.6 11.7 %collective-permute-start.11 = (bf16[64,3712]{1,0:T(8,128)(2,1)S(1)}, bf16[64,3712]{1,0:T(8,128)(2,1)S(1)}, u32[]{:S(2)}, u32[]{:S(2)}) collective-permute-start(bf16[64,3712]{1,0:T(8,128)(2,1)S(1)} %collective-permute-done.4.refs_3_), channel_id=1, source_target_pairs={{0,2},{1,7},{2,4},{3,1},{4,6},{5,3},{6,0},{7,5},{8,10},{9,15},{10,... | collective-permute-start | bytes 1425416 | tf_op jit(solution)/shard_map/ppermute | solution.py:28
  36.6 17.2 %collective-permute-start.12 = (bf16[64,3712]{1,0:T(8,128)(2,1)S(1)}, bf16[64,3712]{1,0:T(8,128)(2,1)S(1)}, u32[]{:S(2)}, u32[]{:S(2)}) collective-permute-start(bf16[64,3712]{1,0:T(8,128)(2,1)S(1)} %collective-permute-done.4.refs_3_), channel_id=1, source_target_pairs={{0,7},{1,2},{2,1},{3,4},{4,3},{5,6},{6,5},{7,0},{8,15},{9,10},{10,... | collective-permute-start | bytes 1425416 | tf_op jit(solution)/shard_map/ppermute | solution.py:28
  38.9 25.6 %collective-permute-start.8 = (bf16[64,3712]{1,0:T(8,128)(2,1)S(1)}, bf16[64,3712]{1,0:T(8,128)(2,1)S(1)}, u32[]{:S(2)}, u32[]{:S(2)}) collective-permute-start(bf16[64,3712]{1,0:T(8,128)(2,1)S(1)} %collective-permute-done.3.refs_0_), channel_id=1, source_target_pairs={{0,8},{1,9},{2,10},{3,11},{4,12},{5,13},{6,14},{7,15},{8,0},{9,1},... | collective-permute-start | bytes 1425416 | tf_op jit(solution)/shard_map/ppermute | solution.py:28
  46.8 17.7 %collective-permute-start.10 = (bf16[64,3712]{1,0:T(8,128)(2,1)S(1)}, bf16[64,3712]{1,0:T(8,128)(2,1)S(1)}, u32[]{:S(2)}, u32[]{:S(2)}) collective-permute-start(bf16[64,3712]{1,0:T(8,128)(2,1)S(1)} %collective-permute-done.9.refs_3_), channel_id=1, source_target_pairs={{0,7},{1,2},{2,1},{3,4},{4,3},{5,6},{6,5},{7,0},{8,15},{9,10},{10,... | collective-permute-start | bytes 1425416 | tf_op jit(solution)/shard_map/ppermute | solution.py:28
  48.3 22.1 %collective-permute-start.13 = (bf16[64,3712]{1,0:T(8,128)(2,1)S(1)}, bf16[64,3712]{1,0:T(8,128)(2,1)S(1)}, u32[]{:S(2)}, u32[]{:S(2)}) collective-permute-start(bf16[64,3712]{1,0:T(8,128)(2,1)S(1)} %collective-permute-done.1.refs_0_), channel_id=1, source_target_pairs={{0,8},{1,9},{2,10},{3,11},{4,12},{5,13},{6,14},{7,15},{8,0},{9,1},... | collective-permute-start | bytes 1425416 | tf_op jit(solution)/shard_map/ppermute | solution.py:28
  51.2 19.2 %collective-permute-start.14 = (bf16[64,3712]{1,0:T(8,128)(2,1)S(1)}, bf16[64,3712]{1,0:T(8,128)(2,1)S(1)}, u32[]{:S(2)}, u32[]{:S(2)}) collective-permute-start(bf16[64,3712]{1,0:T(8,128)(2,1)S(1)} %collective-permute-done.9.refs_3_), channel_id=1, source_target_pairs={{0,2},{1,7},{2,4},{3,1},{4,6},{5,3},{6,0},{7,5},{8,10},{9,15},{10,... | collective-permute-start | bytes 1425416 | tf_op jit(solution)/shard_map/ppermute | solution.py:28
  64.5 12.4 %collective-permute-start.15 = (bf16[64,3584]{1,0:T(8,128)(2,1)S(1)}, bf16[64,3584]{1,0:T(8,128)(2,1)S(1)}, u32[]{:S(2)}, u32[]{:S(2)}) collective-permute-start(bf16[64,3584]{1,0:T(8,128)(2,1)S(1)} %get-tuple-element.71), channel_id=1, source_target_pairs={{7,0},{2,1},{1,2},{4,3},{3,4},{6,5},{5,6},{0,7},{15,8},{10,9},{9,1... | collective-permute-start | bytes 1376264 | tf_op jit(solution)/shard_map/ppermute | solution.py:28
  66.2 11.8 %collective-permute-start.18 = (bf16[64,3712]{1,0:T(8,128)(2,1)S(1)}, bf16[64,3712]{1,0:T(8,128)(2,1)S(1)}, u32[]{:S(2)}, u32[]{:S(2)}) collective-permute-start(bf16[64,3712]{1,0:T(8,128)(2,1)S(1)} %copy-done.4), channel_id=1, source_target_pairs={{0,7},{1,2},{2,1},{3,4},{4,3},{5,6},{6,5},{7,0},{8,15},{9,10},{10,... | collective-permute-start | bytes 1425416 | tf_op jit(solution)/shard_map/ppermute | solution.py:28
  70.4 14.4 %collective-permute-start.17 = (bf16[64,3584]{1,0:T(8,128)(2,1)S(1)}, bf16[64,3584]{1,0:T(8,128)(2,1)S(1)}, u32[]{:S(2)}, u32[]{:S(2)}) collective-permute-start(bf16[64,3584]{1,0:T(8,128)(2,1)S(1)} %shard_map.116), channel_id=1, source_target_pairs={{0,8},{1,9},{2,10},{3,11},{4,12},{5,13},{6,14},{7,15},{8,0},{9,1},... | collective-permute-start | bytes 1376264 | tf_op jit(solution)/shard_map/ppermute | solution.py:28
  70.7 12.3 %collective-permute-start.19 = (bf16[64,3712]{1,0:T(8,128)(2,1)S(1)}, bf16[64,3712]{1,0:T(8,128)(2,1)S(1)}, u32[]{:S(2)}, u32[]{:S(2)}) collective-permute-start(bf16[64,3712]{1,0:T(8,128)(2,1)S(1)} %copy-done.5), channel_id=1, source_target_pairs={{0,7},{1,2},{2,1},{3,4},{4,3},{5,6},{6,5},{7,0},{8,15},{9,10},{10,... | collective-permute-start | bytes 1425416 | tf_op jit(solution)/shard_map/ppermute | solution.py:28
  76.9 11.0 %collective-permute-start.16 = (bf16[64,3584]{1,0:T(8,128)(2,1)S(1)}, bf16[64,3584]{1,0:T(8,128)(2,1)S(1)}, u32[]{:S(2)}, u32[]{:S(2)}) collective-permute-start(bf16[64,3584]{1,0:T(8,128)(2,1)S(1)} %get-tuple-element.72), channel_id=1, source_target_pairs={{7,0},{2,1},{1,2},{4,3},{3,4},{6,5},{5,6},{0,7},{15,8},{10,9},{9,1... | collective-permute-start | bytes 1376264 | tf_op jit(solution)/shard_map/ppermute | solution.py:28
  77.9 23.1 %collective-permute-start.21 = (bf16[64,3584]{1,0:T(8,128)(2,1)S(1)}, bf16[64,3584]{1,0:T(8,128)(2,1)S(1)}, u32[]{:S(2)}, u32[]{:S(2)}) collective-permute-start(bf16[64,3584]{1,0:T(8,128)(2,1)S(1)} %get-tuple-element.86), channel_id=1, source_target_pairs={{2,0},{7,1},{4,2},{1,3},{6,4},{3,5},{0,6},{5,7},{10,8},{15,9},{12,... | collective-permute-start | bytes 1376264 | tf_op jit(solution)/shard_map/ppermute | solution.py:28
  83.0 18.9 %collective-permute-start.20 = (bf16[64,3584]{1,0:T(8,128)(2,1)S(1)}, bf16[64,3584]{1,0:T(8,128)(2,1)S(1)}, u32[]{:S(2)}, u32[]{:S(2)}) collective-permute-start(bf16[64,3584]{1,0:T(8,128)(2,1)S(1)} %shard_map.118), channel_id=1, source_target_pairs={{0,8},{1,9},{2,10},{3,11},{4,12},{5,13},{6,14},{7,15},{8,0},{9,1},... | collective-permute-start | bytes 1376264 | tf_op jit(solution)/shard_map/ppermute | solution.py:28
  85.0 17.8 %collective-permute-start.24 = (bf16[64,3584]{1,0:T(8,128)(2,1)S(1)}, bf16[64,3584]{1,0:T(8,128)(2,1)S(1)}, u32[]{:S(2)}, u32[]{:S(2)}) collective-permute-start(bf16[64,3584]{1,0:T(8,128)(2,1)S(1)} %add_convert_fusion.8), channel_id=1, source_target_pairs={{0,4},{1,5},{2,6},{3,7},{4,0},{5,1},{6,2},{7,3},{8,12},{9,13},{10,... | collective-permute-start | bytes 1376264 | tf_op jit(solution)/shard_map/ppermute | solution.py:28
  93.8 13.8 %collective-permute-start.23 = (bf16[64,3584]{1,0:T(8,128)(2,1)S(1)}, bf16[64,3584]{1,0:T(8,128)(2,1)S(1)}, u32[]{:S(2)}, u32[]{:S(2)}) collective-permute-start(bf16[64,3584]{1,0:T(8,128)(2,1)S(1)} %get-tuple-element.84), channel_id=1, source_target_pairs={{7,0},{2,1},{1,2},{4,3},{3,4},{6,5},{5,6},{0,7},{15,8},{10,9},{9,1... | collective-permute-start | bytes 1376264 | tf_op jit(solution)/shard_map/ppermute | solution.py:28
  101.0 11.8 %collective-permute-start.22 = (bf16[64,3584]{1,0:T(8,128)(2,1)S(1)}, bf16[64,3584]{1,0:T(8,128)(2,1)S(1)}, u32[]{:S(2)}, u32[]{:S(2)}) collective-permute-start(bf16[64,3584]{1,0:T(8,128)(2,1)S(1)} %get-tuple-element.87), channel_id=1, source_target_pairs={{2,0},{7,1},{4,2},{1,3},{6,4},{3,5},{0,6},{5,7},{10,8},{15,9},{12,... | collective-permute-start | bytes 1376264 | tf_op jit(solution)/shard_map/ppermute | solution.py:28
  103.0 15.6 %collective-permute-start.27 = (bf16[64,3584]{1,0:T(8,128)(2,1)S(1)}, bf16[64,3584]{1,0:T(8,128)(2,1)S(1)}, u32[]{:S(2)}, u32[]{:S(2)}) collective-permute-start(bf16[64,3584]{1,0:T(8,128)(2,1)S(1)} %add_convert_fusion.6), channel_id=1, source_target_pairs={{0,24},{1,25},{2,26},{3,27},{4,28},{5,29},{6,30},{7,31},{8,16},{9,... | collective-permute-start | bytes 1376264 | tf_op jit(solution)/shard_map/ppermute | solution.py:53
  103.9 13.8 %collective-permute-start.28 = (bf16[64,3584]{1,0:T(8,128)(2,1)S(1)}, bf16[64,3584]{1,0:T(8,128)(2,1)S(1)}, u32[]{:S(2)}, u32[]{:S(2)}) collective-permute-start(bf16[64,3584]{1,0:T(8,128)(2,1)S(1)} %add_convert_fusion.5), channel_id=1, source_target_pairs={{2,0},{7,1},{4,2},{1,3},{6,4},{3,5},{0,6},{5,7},{10,8},{15,9},{12,... | collective-permute-start | bytes 1376264 | tf_op jit(solution)/shard_map/ppermute | solution.py:28
  107.6 19.7 %collective-permute-start.26 = (bf16[64,3584]{1,0:T(8,128)(2,1)S(1)}, bf16[64,3584]{1,0:T(8,128)(2,1)S(1)}, u32[]{:S(2)}, u32[]{:S(2)}) collective-permute-start(bf16[64,3584]{1,0:T(8,128)(2,1)S(1)} %get-tuple-element.89), channel_id=1, source_target_pairs={{2,0},{7,1},{4,2},{1,3},{6,4},{3,5},{0,6},{5,7},{10,8},{15,9},{12,... | collective-permute-start | bytes 1376264 | tf_op jit(solution)/shard_map/ppermute | solution.py:28
  108.2 19.1 %collective-permute-start.30 = (bf16[64,3584]{1,0:T(8,128)(2,1)S(1)}, bf16[64,3584]{1,0:T(8,128)(2,1)S(1)}, u32[]{:S(2)}, u32[]{:S(2)}) collective-permute-start(bf16[64,3584]{1,0:T(8,128)(2,1)S(1)} %get-tuple-element.97), channel_id=1, source_target_pairs={{7,0},{2,1},{1,2},{4,3},{3,4},{6,5},{5,6},{0,7},{15,8},{10,9},{9,1... | collective-permute-start | bytes 1376264 | tf_op jit(solution)/shard_map/ppermute | solution.py:28
  113.1 17.4 %collective-permute-start.25 = (bf16[64,3584]{1,0:T(8,128)(2,1)S(1)}, bf16[64,3584]{1,0:T(8,128)(2,1)S(1)}, u32[]{:S(2)}, u32[]{:S(2)}) collective-permute-start(bf16[64,3584]{1,0:T(8,128)(2,1)S(1)} %add_convert_fusion.7), channel_id=1, source_target_pairs={{0,112},{16,0},{32,16},{48,32},{64,48},{80,64},{96,80},{112,96},{1... | collective-permute-start | bytes 1376264 | tf_op jit(solution)/shard_map/ppermute | solution.py:43
  117.8 14.3 %collective-permute-start.29 = (bf16[64,3584]{1,0:T(8,128)(2,1)S(1)}, bf16[64,3584]{1,0:T(8,128)(2,1)S(1)}, u32[]{:S(2)}, u32[]{:S(2)}) collective-permute-start(bf16[64,3584]{1,0:T(8,128)(2,1)S(1)} %add_convert_fusion.4), channel_id=1, source_target_pairs={{2,0},{7,1},{4,2},{1,3},{6,4},{3,5},{0,6},{5,7},{10,8},{15,9},{12,... | collective-permute-start | bytes 1376264 | tf_op jit(solution)/shard_map/ppermute | solution.py:28
  127.5 12.7 %collective-permute-start.32 = (bf16[64,3584]{1,0:T(8,128)(2,1)S(1)}, bf16[64,3584]{1,0:T(8,128)(2,1)S(1)}, u32[]{:S(2)}, u32[]{:S(2)}) collective-permute-start(bf16[64,3584]{1,0:T(8,128)(2,1)S(1)} %add_convert_fusion.2), channel_id=1, source_target_pairs={{0,120},{1,121},{2,122},{3,123},{4,124},{5,125},{6,126},{7,127},{8... | collective-permute-start | bytes 1376264 | tf_op jit(solution)/shard_map/ppermute | solution.py:53
  132.4 13.9 %collective-permute-start.31 = (bf16[64,3584]{1,0:T(8,128)(2,1)S(1)}, bf16[64,3584]{1,0:T(8,128)(2,1)S(1)}, u32[]{:S(2)}, u32[]{:S(2)}) collective-permute-start(bf16[64,3584]{1,0:T(8,128)(2,1)S(1)} %add_convert_fusion.3), channel_id=1, source_target_pairs={{0,16},{16,32},{32,48},{48,64},{64,80},{80,96},{96,112},{112,0},{1... | collective-permute-start | bytes 1376264 | tf_op jit(solution)/shard_map/ppermute | solution.py:43
  (9 other events, 84.3 us)
